TPU v7x, 32 devices: a whole 2x2x4 slice. The times are simulated.
32 devices in a mesh: ctx: 8 (over y, x, core), rep: 4 (over z).
Axes of the slice: x: 2, y: 2, z: 4, core: 2. Of those that a mesh axis runs over, the one named last changes fastest.
Arguments:
- inputs: bfloat16 [4, 2048, 256], P('rep', 'ctx'), may hold values from -6 to 6
- w_expand: bfloat16 [512, 1024], replicated, may hold values from -0.25 to 0.25
- b_expand: float32 [1024], replicated, may hold values from -1 to 1
- w_reduce: bfloat16 [1024, 512], replicated, may hold values from -0.1875 to 0.1875
- b_reduce: float32 [512], replicated, may hold values from -0.5 to 0.5
- gate_logit: float32 [512], replicated, may hold values from -2 to 2
- cotangent: bfloat16 [4, 2048, 256], P('rep', 'ctx'), may hold values from -6 to 6
Outputs:
- outputs: bfloat16 [4, 2048, 256], P('rep', 'ctx')
- grad_inputs: bfloat16 [4, 2048, 256], P('rep', 'ctx')
- grad_w_expand: float32 [512, 1024], P('ctx')
- grad_b_expand: float32 [1024], replicated
- grad_w_reduce: float32 [1024, 512], P('ctx')
- grad_b_reduce: float32 [512], replicated
- grad_gate: float32 [512], replicated
All inputs are finite; a program needn't handle non-finite values.
Results may differ from a plain program's by a relative error of at most 0.018.
Values may be sent and summed in bfloat16 or wider, within the bound.
No kernel may reach another device: no remote copies, remote signals or barrier semaphores. Data moves between devices by JAX's collectives and lax.ppermute only.
A program may use at most 64 MiB of HBM per device.

v0:
```python
import math

import jax
import jax.numpy as jnp
from jax import lax
from jax.sharding import PartitionSpec as P

SECTIONS = 4


EPSILON = 1e-05


def gelu_back(preact, upstream):
    return jax.vjp(lambda value: jax.nn.gelu(value, approximate=False), preact)[1](upstream)[0]


def switch_forward(lower, upper, w_expand, b_expand):
    joined = jnp.concatenate([lower, upper], axis=-1).astype(jnp.float32)
    centred = joined - jnp.mean(joined, axis=-1, keepdims=True)
    inv_std = lax.rsqrt(jnp.mean(centred * centred, axis=-1, keepdims=True) + EPSILON)
    normed = centred * inv_std
    normed_low = normed.astype(jnp.bfloat16)
    preact = jnp.dot(normed_low, w_expand, preferred_element_type=jnp.float32) + b_expand
    hidden = jax.nn.gelu(preact, approximate=False).astype(jnp.bfloat16)
    return (joined, normed, inv_std, normed_low, preact, hidden)


def switch_apply(lower, upper, w_expand, b_expand, w_reduce, b_reduce, gate_logit):
    joined, normed, inv_std, normed_low, preact, hidden = switch_forward(
        lower, upper, w_expand, b_expand
    )
    mixed = jnp.dot(hidden, w_reduce, preferred_element_type=jnp.float32)
    result = (jax.nn.sigmoid(gate_logit) * joined + mixed + b_reduce).astype(jnp.bfloat16)
    width = lower.shape[-1]
    return (result[:, :width], result[:, width:])


def switch_backward(
    lower, upper, grad_lower, grad_upper, w_expand, b_expand, w_reduce, b_reduce, gate_logit
):
    joined, normed, inv_std, normed_low, preact, hidden = switch_forward(
        lower, upper, w_expand, b_expand
    )
    grad_out = jnp.concatenate([grad_lower, grad_upper], axis=-1)
    grad_float = grad_out.astype(jnp.float32)
    sigma = jax.nn.sigmoid(gate_logit)
    grad_bias_red = jnp.sum(grad_float, axis=0)
    grad_gate = jnp.sum(grad_float * joined, axis=0) * sigma * (1.0 - sigma)
    grad_weight_red = jnp.dot(hidden.T, grad_out, preferred_element_type=jnp.float32)
    grad_hidden = jnp.dot(grad_out, w_reduce.T, preferred_element_type=jnp.float32)
    grad_pre = gelu_back(preact, grad_hidden)
    grad_pre_low = grad_pre.astype(jnp.bfloat16)
    grad_bias_exp = jnp.sum(grad_pre, axis=0)
    grad_weight_exp = jnp.dot(normed_low.T, grad_pre_low, preferred_element_type=jnp.float32)
    grad_normed = jnp.dot(grad_pre_low, w_expand.T, preferred_element_type=jnp.float32)
    grad_joined = sigma * grad_float + inv_std * (
        grad_normed
        - jnp.mean(grad_normed, axis=-1, keepdims=True)
        - normed * jnp.mean(grad_normed * normed, axis=-1, keepdims=True)
    )
    grad_joined = grad_joined.astype(jnp.bfloat16)
    width = lower.shape[-1]
    return (
        grad_joined[:, :width],
        grad_joined[:, width:],
        (grad_weight_exp, grad_bias_exp, grad_weight_red, grad_bias_red, grad_gate),
    )


def local_split(grouped, block):
    devs, slice_rows, width = grouped.shape
    view = grouped.reshape(devs // (2 * block), 2, block, slice_rows, width)
    return (view[:, 0].reshape(-1, width), view[:, 1].reshape(-1, width))


def local_join(first, second, shape, block):
    devs, slice_rows, width = shape
    first = first.reshape(devs // (2 * block), block, slice_rows, width)
    second = second.reshape(devs // (2 * block), block, slice_rows, width)
    return jnp.stack([first, second], axis=1).reshape(shape)


def body(inputs, w_expand, b_expand, w_reduce, b_reduce, gate_logit, cotangent):
    weights = (w_expand, b_expand, w_reduce, b_reduce, gate_logit)
    rows = inputs.shape[1]
    width = inputs.shape[2]
    devs = lax.axis_size("ctx")
    slice_rows = rows // devs
    grouped_shape = (devs, slice_rows, width)
    count = devs.bit_length() - 1
    totals = (
        jnp.zeros(w_expand.shape, jnp.float32),
        jnp.zeros(b_expand.shape, jnp.float32),
        jnp.zeros(w_reduce.shape, jnp.float32),
        jnp.zeros(b_reduce.shape, jnp.float32),
        jnp.zeros(gate_logit.shape, jnp.float32),
    )
    moved = lax.all_to_all(
        inputs.reshape(1, devs, slice_rows, width), "ctx", split_axis=1, concat_axis=0, tiled=True
    )
    grouped = moved.reshape(grouped_shape)
    saved = []
    for section in range(SECTIONS):
        block = 2 ** ((count - 1 - section) % count)
        lower, upper = local_split(grouped, block)
        saved.append((lower, upper, block))
        out_lower, out_upper = switch_apply(lower, upper, *weights)
        grouped = local_join(out_lower, out_upper, grouped_shape, block)
    back = lax.all_to_all(
        grouped.reshape(devs, 1, slice_rows, width), "ctx", split_axis=0, concat_axis=1, tiled=True
    )
    outputs = back.reshape(inputs.shape)
    moved_grad = lax.all_to_all(
        cotangent.reshape(1, devs, slice_rows, width),
        "ctx",
        split_axis=1,
        concat_axis=0,
        tiled=True,
    )
    grad_grouped = moved_grad.reshape(grouped_shape)
    for section in reversed(range(SECTIONS)):
        lower, upper, block = saved[section]
        grad_lower, grad_upper = local_split(grad_grouped, block)
        back_lower, back_upper, grads = switch_backward(
            lower, upper, grad_lower, grad_upper, *weights
        )
        totals = tuple((total + piece for total, piece in zip(totals, grads)))
        grad_grouped = local_join(back_lower, back_upper, grouped_shape, block)
    grad_back = lax.all_to_all(
        grad_grouped.reshape(devs, 1, slice_rows, width),
        "ctx",
        split_axis=0,
        concat_axis=1,
        tiled=True,
    )
    grad_inputs = grad_back.reshape(inputs.shape)
    share = 1.0
    factor = share / math.sqrt(lax.axis_size("rep") * devs * rows)
    part_expand, part_reduce = (
        lax.psum_scatter(totals[0], "ctx", scatter_dimension=0, tiled=True),
        lax.psum_scatter(totals[2], "ctx", scatter_dimension=0, tiled=True),
    )
    part_expand, part_reduce = (
        lax.psum(part_expand.astype(jnp.bfloat16), "rep").astype(jnp.float32),
        lax.psum(part_reduce.astype(jnp.bfloat16), "rep").astype(jnp.float32),
    )
    bias_expand, bias_reduce, gate_sum = lax.psum((totals[1], totals[3], totals[4]), ("ctx", "rep"))
    return (
        outputs,
        grad_inputs,
        part_expand * factor,
        bias_expand * factor,
        part_reduce * factor,
        bias_reduce * factor,
        gate_sum * factor,
    )


def solution(mesh):
    return jax.shard_map(
        body,
        mesh=mesh,
        in_specs=(P("rep", "ctx", None), P(), P(), P(), P(), P(), P("rep", "ctx", None)),
        out_specs=(
            P("rep", "ctx", None),
            P("rep", "ctx", None),
            P("ctx", None),
            P(),
            P("ctx", None),
            P(),
            P(),
        ),
        check_vma=False,
    )
```

profile of v0, /device:TPU:0, one launch (start us, length us, event | category | flops | bytes accessed | tf_op | source)
XLA Modules:
  0.0 183.2 jit_solution(173477698205586263)
XLA Ops:
  7.2 5.3 %all-to-all-start = ((bf16[1,8,32,256]{3,2,0,1:T(8,128)(2,1)}), bf16[1,8,32,256]{3,2,0,1:T(8,128)(2,1)S(1)}, u32[]{:S(2)}, u32[]{:S(2)}) async-start(bf16[1,8,32,256]{3,2,0,1:T(8,128)(2,1)} %bitcast.200), calls=%async_computation | async-start | bytes 262144 | tf_op jit(solution)/shard_map/all_to_all | solution.py:99
  12.5 0.7 add_divide_fusion
  13.2 4.8 %all-to-all-done = bf16[1,8,32,256]{3,2,0,1:T(8,128)(2,1)S(1)} async-done(((bf16[1,8,32,256]{3,2,0,1:T(8,128)(2,1)}), bf16[1,8,32,256]{3,2,0,1:T(8,128)(2,1)S(1)}, u32[]{:S(2)}, u32[]{:S(2)}) %all-to-all-start) | async-done | bytes 131104 | tf_op jit(solution)/shard_map/all_to_all | solution.py:99
  18.0 3.4 %all-to-all-start.2 = ((bf16[1,8,32,256]{3,2,0,1:T(8,128)(2,1)}), bf16[1,8,32,256]{3,2,0,1:T(8,128)(2,1)S(1)}, u32[]{:S(2)}, u32[]{:S(2)}) async-start(bf16[1,8,32,256]{3,2,0,1:T(8,128)(2,1)} %bitcast.201), calls=%async_computation.2 | async-start | bytes 262144 | tf_op jit(solution)/shard_map/all_to_all | solution.py:114
  21.8 5.1 %all-to-all-done.2 = bf16[1,8,32,256]{3,2,0,1:T(8,128)(2,1)S(1)} async-done(((bf16[1,8,32,256]{3,2,0,1:T(8,128)(2,1)}), bf16[1,8,32,256]{3,2,0,1:T(8,128)(2,1)S(1)}, u32[]{:S(2)}, u32[]{:S(2)}) %all-to-all-start.2) | async-done | bytes 131104 | tf_op jit(solution)/shard_map/all_to_all | solution.py:114
  26.9 2.2 %multiply_convert_fusion.3 = (bf16[128,1024]{1,0:T(8,128)(2,1)S(1)}, f32[128,1024]{1,0:T(8,128)S(1)}, f32[128,1024]{1,0:T(8,128)S(1)}) fusion(f32[1024]{0:T(1024)} %param.9, bf16[512,1024]{1,0:T(8,128)(2,1)S(1)} %copy-done, f32[128]{0:T(128)S(1)} %add_rsqrt_fusion.3, f32[128]{0:T(128)S(1)} %broadcast_multiply_fusion.14, bf16[128,256]{1,0:T(8,128)(2,1)S(1)} %bitcast.97, ...), kind=kOutput, calls=%fused_computation.69 | convolution fusion | flops 143327232 | bytes 2495488 | tf_op jit(solution)/shard_map/dot_general | solution.py:24
  29.8 1.4 multiply_convert_fusion.2
  31.9 1.4 multiply_convert_fusion.1
  34.0 1.4 multiply_convert_fusion
  36.0 1.1 fusion.115
  37.3 1.1 fusion.137
  38.5 1.1 fusion.114
  39.8 1.1 fusion.135
  41.0 1.1 fusion.113
  44.0 1.1 fusion.134
  45.1 0.7 copy-done.12
  45.8 1.9 %add_add_fusion.1 = f32[512,1024]{1,0:T(8,128)} fusion(f32[512,1024]{1,0:T(8,128)S(1)} %fusion.83, f32[512,1024]{1,0:T(8,128)S(1)} %fusion.91, f32[512,1024]{1,0:T(8,128)S(1)} %fusion.87, bf16[128,1024]{1,0:T(8,128)(2,1)S(1)} %get-tuple-element.77, f32[128]{0:T(128)S(1)} %copy-done.20, f32[128]{0:T(128)S(1)} %broadcast_multiply_fusion.14, ...), kind=kOutput, calls=%fused_computation.1 | convolution fusion | flops 136249344 | bytes 8782848 | tf_op jit(solution)/shard_map/dot_general | solution.py:55
  48.0 1.4 fusion.106
  50.4 1.8 add_add_fusion
  52.6 0.7 pad_maximum_fusion.6
  53.3 3.4 %all-to-all-start.1 = ((bf16[8,1,32,256]{3,2,1,0:T(8,128)(2,1)}), bf16[8,1,32,256]{3,2,1,0:T(8,128)(2,1)S(1)}, u32[]{:S(2)}, u32[]{:S(2)}) async-start(bf16[8,1,32,256]{3,2,1,0:T(8,128)(2,1)} %bitcast.24), calls=%async_computation.1 | async-start | bytes 262144 | tf_op jit(solution)/shard_map/all_to_all | solution.py:110
  57.4 41.1 %all-reduce = (f32[1024]{0:T(1024)S(1)}, f32[512]{0:T(512)S(1)}, f32[512]{0:T(512)S(1)}) all-reduce(f32[1024]{0:T(1024)S(1)} %add_add_fusion.2, f32[512]{0:T(512)S(1)} %get-tuple-element.85, f32[512]{0:T(512)S(1)} %get-tuple-element.84), channel_id=1, replica_groups=mesh['ctx'=8,'rep'=4] {'ctx','rep'}, use_global_device_ids=true, to_apply=%region_22.0 | all-reduce | flops 2048 | bytes 16384 | tf_op jit(solution)/shard_map/psum | solution.py:148
  100.0 1.6 convert_element_type.136
  101.6 32.0 %reduce-scatter.5.cloned.1.call-done = f32[128,512]{1,0:T(8,128)} async-done(((f32[1024,512]{1,0:T(8,128)}), f32[128,512]{1,0:T(8,128)}) %reduce-scatter.5.cloned.1.call-update) | async-done | bytes 262160 | tf_op jit(solution)/shard_map/reduce_scatter | solution.py:142
  133.6 1.6 convert_element_type.138
  135.2 0.7 pad_maximum_fusion.13
  135.9 3.4 %all-to-all-start.3 = ((bf16[8,1,32,256]{3,2,1,0:T(8,128)(2,1)}), bf16[8,1,32,256]{3,2,1,0:T(8,128)(2,1)S(1)}, u32[]{:S(2)}, u32[]{:S(2)}) async-start(bf16[8,1,32,256]{3,2,1,0:T(8,128)(2,1)} %bitcast.46), calls=%async_computation.3 | async-start | bytes 262144 | tf_op jit(solution)/shard_map/all_to_all | solution.py:130
  139.8 4.9 %all-to-all-done.3 = bf16[8,1,32,256]{3,2,1,0:T(8,128)(2,1)S(1)} async-done(((bf16[8,1,32,256]{3,2,1,0:T(8,128)(2,1)}), bf16[8,1,32,256]{3,2,1,0:T(8,128)(2,1)S(1)}, u32[]{:S(2)}, u32[]{:S(2)}) %all-to-all-start.3) | async-done | bytes 131104 | tf_op jit(solution)/shard_map/all_to_all | solution.py:130
  144.7 27.3 %all-reduce.4.cloned.1.call-done = (bf16[64,1024]{1,0:T(8,128)(2,1)}, bf16[128,512]{1,0:T(8,128)(2,1)}) async-done(((bf16[64,1024]{1,0:T(8,128)(2,1)}, bf16[128,512]{1,0:T(8,128)(2,1)}), (bf16[64,1024]{1,0:T(8,128)(2,1)}, bf16[128,512]{1,0:T(8,128)(2,1)})) %all-reduce.4.cloned.1.call-update) | async-done | bytes 262160 | tf_op jit(solution)/shard_map/psum | solution.py:145
  172.1 1.6 convert_multiply_fusion.13
  173.7 1.6 convert_multiply_fusion.12
  176.0 0.7 copy.47
  (132 shorter events, 10.0 us)
Async XLA Ops:
  7.2 19.7 %copy-start = (bf16[512,1024]{1,0:T(8,128)(2,1)S(1)}, bf16[512,1024]{1,0:T(8,128)(2,1)}, u32[]{:S(2)}) copy-start(bf16[512,1024]{1,0:T(8,128)(2,1)} %param.8) | copy-start | bytes 3145732
  7.2 10.8 %all-to-all-start = ((bf16[1,8,32,256]{3,2,0,1:T(8,128)(2,1)}), bf16[1,8,32,256]{3,2,0,1:T(8,128)(2,1)S(1)}, u32[]{:S(2)}, u32[]{:S(2)}) async-start(bf16[1,8,32,256]{3,2,0,1:T(8,128)(2,1)} %bitcast.200), calls=%async_computation | async-start | bytes 262144 | tf_op jit(solution)/shard_map/all_to_all | solution.py:99
  18.0 8.8 %all-to-all-start.2 = ((bf16[1,8,32,256]{3,2,0,1:T(8,128)(2,1)}), bf16[1,8,32,256]{3,2,0,1:T(8,128)(2,1)S(1)}, u32[]{:S(2)}, u32[]{:S(2)}) async-start(bf16[1,8,32,256]{3,2,0,1:T(8,128)(2,1)} %bitcast.201), calls=%async_computation.2 | async-start | bytes 262144 | tf_op jit(solution)/shard_map/all_to_all | solution.py:114
  21.4 78.5 %reduce-scatter.3.cloned.1.call-start = ((), (), s32[]{:S(2)}) async-start(), calls=%async_computation.6 | async-start | bytes 2359296 | tf_op jit(solution)/shard_map/reduce_scatter | solution.py:141
  21.8 7.3 %copy-start.19 = (f32[128]{0:T(128)}, f32[128]{0:T(128)S(1)}, u32[]{:S(2)}) copy-start(f32[128]{0:T(128)S(1)} %add_rsqrt_fusion.3) | copy-start | bytes 1540
  26.9 10.2 %copy-start.4 = (bf16[1,1,4,32,256]{4,3,2,1,0:T(8,128)(2,1)}, bf16[1,1,4,32,256]{4,3,2,1,0:T(8,128)(2,1)S(1)}, u32[]{:S(2)}) copy-start(bf16[1,1,4,32,256]{4,3,2,1,0:T(8,128)(2,1)S(1)} %get-tuple-element.50) | copy-start | bytes 196612
  26.9 10.2 %copy-start.6 = (bf16[1,1,4,32,256]{4,3,2,1,0:T(8,128)(2,1)}, bf16[1,1,4,32,256]{4,3,2,1,0:T(8,128)(2,1)S(1)}, u32[]{:S(2)}) copy-start(bf16[1,1,4,32,256]{4,3,2,1,0:T(8,128)(2,1)S(1)} %get-tuple-element.51) | copy-start | bytes 196612
  26.9 2.2 %copy-start.1 = (bf16[1024,512]{1,0:T(8,128)(2,1)S(1)}, bf16[1024,512]{1,0:T(8,128)(2,1)}, u32[]{:S(2)}) copy-start(bf16[1024,512]{1,0:T(8,128)(2,1)} %param.10) | copy-start | bytes 3145732
  26.9 2.2 %copy-start.14 = (f32[512]{0:T(512)S(1)}, f32[512]{0:T(512)}, u32[]{:S(2)}) copy-start(f32[512]{0:T(512)} %param.11) | copy-start | bytes 6148
  37.3 2.3 %copy-start.8 = (bf16[4,1,1,32,256]{4,3,1,0,2:T(8,128)(2,1)}, bf16[4,1,1,32,256]{4,3,1,0,2:T(8,128)(2,1)S(1)}, u32[]{:S(2)}) copy-start(bf16[4,1,1,32,256]{4,3,1,0,2:T(8,128)(2,1)S(1)} %get-tuple-element.46) | copy-start | bytes 196612
  37.3 2.3 %copy-start.10 = (bf16[4,1,1,32,256]{4,3,1,0,2:T(8,128)(2,1)}, bf16[4,1,1,32,256]{4,3,1,0,2:T(8,128)(2,1)S(1)}, u32[]{:S(2)}) copy-start(bf16[4,1,1,32,256]{4,3,1,0,2:T(8,128)(2,1)S(1)} %get-tuple-element.47) | copy-start | bytes 196612
  39.8 3.9 %copy-start.2 = (bf16[2,1,2,32,256]{4,3,2,0,1:T(8,128)(2,1)}, bf16[2,1,2,32,256]{4,3,2,0,1:T(8,128)(2,1)S(1)}, u32[]{:S(2)}) copy-start(bf16[2,1,2,32,256]{4,3,2,0,1:T(8,128)(2,1)S(1)} %copy.40) | copy-start | bytes 196612
  39.8 3.9 %copy-start.3 = (bf16[2,1,2,32,256]{4,3,2,0,1:T(8,128)(2,1)}, bf16[2,1,2,32,256]{4,3,2,0,1:T(8,128)(2,1)S(1)}, u32[]{:S(2)}) copy-start(bf16[2,1,2,32,256]{4,3,2,0,1:T(8,128)(2,1)S(1)} %copy.41) | copy-start | bytes 196612
  43.9 1.9 %copy-start.20 = (f32[128]{0:T(128)S(1)}, f32[128]{0:T(128)}, u32[]{:S(2)}) copy-start(f32[128]{0:T(128)} %copy-done.19) | copy-start | bytes 1540
  47.8 85.8 %reduce-scatter.5.cloned.1.call-start = ((), (), s32[]{:S(2)}) async-start(), calls=%async_computation.7 | async-start | bytes 2359296 | tf_op jit(solution)/shard_map/reduce_scatter | solution.py:142
  48.0 1.9 %copy-start.5 = (bf16[1,1,4,32,256]{4,3,2,1,0:T(8,128)(2,1)S(1)}, bf16[1,1,4,32,256]{4,3,2,1,0:T(8,128)(2,1)}, u32[]{:S(2)}) copy-start(bf16[1,1,4,32,256]{4,3,2,1,0:T(8,128)(2,1)} %copy-done.4) | copy-start | bytes 196612
  48.0 1.9 %copy-start.7 = (bf16[1,1,4,32,256]{4,3,2,1,0:T(8,128)(2,1)S(1)}, bf16[1,1,4,32,256]{4,3,2,1,0:T(8,128)(2,1)}, u32[]{:S(2)}) copy-start(bf16[1,1,4,32,256]{4,3,2,1,0:T(8,128)(2,1)} %copy-done.6) | copy-start | bytes 196612
  52.1 4.6 %copy-start.16 = (f32[1024]{0:T(1024)S(1)}, f32[1024]{0:T(1024)}, u32[]{:S(2)}) copy-start(f32[1024]{0:T(1024)} %get-tuple-element.82) | copy-start | bytes 12292
  52.1 4.6 %copy-start.17 = (f32[1024]{0:T(1024)S(1)}, f32[1024]{0:T(1024)}, u32[]{:S(2)}) copy-start(f32[1024]{0:T(1024)} %get-tuple-element.78) | copy-start | bytes 12292
  52.1 4.6 %copy-start.18 = (f32[1024]{0:T(1024)S(1)}, f32[1024]{0:T(1024)}, u32[]{:S(2)}) copy-start(f32[1024]{0:T(1024)} %get-tuple-element.76) | copy-start | bytes 12292
  52.1 4.6 %copy-start.13 = (bf16[128,1024]{1,0:T(8,128)(2,1)S(1)}, bf16[128,1024]{1,0:T(8,128)(2,1)}, u32[]{:S(2)}) copy-start(bf16[128,1024]{1,0:T(8,128)(2,1)} %copy-done.12) | copy-start | bytes 786436
  52.1 4.6 %copy-start.21 = (f32[128]{0:T(128)S(1)}, f32[128]{0:T(128)}, u32[]{:S(2)}) copy-start(f32[128]{0:T(128)} %copy-done.19) | copy-start | bytes 1540
  52.2 5.2 %copy-start.15 = (f32[512]{0:T(512)S(1)}, f32[512]{0:T(512)}, u32[]{:S(2)}) copy-start(f32[512]{0:T(512)} %param.12) | copy-start | bytes 6148
  52.2 5.2 %copy-start.22 = (f32[512]{0:T(512)S(1)}, f32[512]{0:T(512)}, u32[]{:S(2)}) copy-start(f32[512]{0:T(512)} %get-tuple-element.15) | copy-start | bytes 6148
  52.2 5.2 %copy-start.23 = (f32[512]{0:T(512)S(1)}, f32[512]{0:T(512)}, u32[]{:S(2)}) copy-start(f32[512]{0:T(512)} %get-tuple-element.16) | copy-start | bytes 6148
  52.2 5.2 %copy-start.24 = (f32[512]{0:T(512)S(1)}, f32[512]{0:T(512)}, u32[]{:S(2)}) copy-start(f32[512]{0:T(512)} %get-tuple-element.17) | copy-start | bytes 6148
  52.2 5.2 %copy-start.25 = (f32[512]{0:T(512)S(1)}, f32[512]{0:T(512)}, u32[]{:S(2)}) copy-start(f32[512]{0:T(512)} %get-tuple-element.18) | copy-start | bytes 6148
  52.2 5.2 %copy-start.26 = (f32[512]{0:T(512)S(1)}, f32[512]{0:T(512)}, u32[]{:S(2)}) copy-start(f32[512]{0:T(512)} %get-tuple-element.19) | copy-start | bytes 6148
  52.2 5.2 %copy-start.27 = (f32[512]{0:T(512)S(1)}, f32[512]{0:T(512)}, u32[]{:S(2)}) copy-start(f32[512]{0:T(512)} %get-tuple-element.20) | copy-start | bytes 6148
  53.3 82.6 %all-to-all-start.1 = ((bf16[8,1,32,256]{3,2,1,0:T(8,128)(2,1)}), bf16[8,1,32,256]{3,2,1,0:T(8,128)(2,1)S(1)}, u32[]{:S(2)}, u32[]{:S(2)}) async-start(bf16[8,1,32,256]{3,2,1,0:T(8,128)(2,1)} %bitcast.24), calls=%async_computation.1 | async-start | bytes 262144 | tf_op jit(solution)/shard_map/all_to_all | solution.py:110
  56.6 115.4 %all-reduce.4.cloned.1.call-start = ((), (), s32[]{:S(2)}) async-start(), calls=%async_computation.8 | async-start | bytes 524288 | tf_op jit(solution)/shard_map/psum | solution.py:145
  135.9 8.8 %all-to-all-start.3 = ((bf16[8,1,32,256]{3,2,1,0:T(8,128)(2,1)}), bf16[8,1,32,256]{3,2,1,0:T(8,128)(2,1)S(1)}, u32[]{:S(2)}, u32[]{:S(2)}) async-start(bf16[8,1,32,256]{3,2,1,0:T(8,128)(2,1)} %bitcast.46), calls=%async_computation.3 | async-start | bytes 262144 | tf_op jit(solution)/shard_map/all_to_all | solution.py:130
  (4 other events, 4.3 us)
Sparse Core Ops, SparseCore 0:
  47.9 40.7 reduce-scatter.2
  92.3 41.1 reduce-scatter.4
  136.5 35.5 all-reduce.3
where the time goes:
time: 184 us; the launch traced here: 183 us
  waiting for transfers between devices  74.2 us (40%)
  blocking collectives  41.1 us (22%)
  matrix products  23 us (12%)
  starting transfers between devices  15.7 us (9%)
  between operations  14.6 us (8%)
  other arithmetic  12.3 us (7%)
  local copies, waits for them, and re-layouts  2.33 us (1%)
    psum x1, blocking collectives, body(): lax.psum((totals[1], totals[3], totals[4]), ('ctx', 'rep'))  41.1 us
    reduce_scatter x1, waiting for transfers between devices, body(): lax.psum_scatter(totals[2], 'ctx', scatter_dimension=0, tiled=True)  32 us
    psum x1, waiting for transfers between devices, body(): lax.psum(part_expand.astype(jnp.bfloat16), 'rep').astype(jnp.float32)  27.3 us
    dot_general x4, matrix products, switch_forward(): jnp.dot(normed_low, w_expand, preferred_element_type=jnp.float32) + b_expand  6.3 us
    all_to_all x1, starting transfers between devices, body(): lax.all_to_all(inputs.reshape(1, devs, slice_rows, width), 'ctx', split_a...  5.31 us
    all_to_all x1, waiting for transfers between devices, body(): lax.all_to_all(cotangent.reshape(1, devs, slice_rows, width), 'ctx', spli...  5.06 us
    all_to_all x1, waiting for transfers between devices, body(): lax.all_to_all(grad_grouped.reshape(devs, 1, slice_rows, width), 'ctx', s...  4.88 us
    all_to_all x1, waiting for transfers between devices, body(): lax.all_to_all(inputs.reshape(1, devs, slice_rows, width), 'ctx', split_a...  4.84 us
  transfers between devices with their start and end apart: 7, of which 5 were waited for; matrix products, arithmetic and copies ran while one was open for 7% of the time, Pallas kernels for 0%

commit v1 on v0

v1 whole, which is shorter than its diff:
```python
import functools
import math

import jax
import jax.numpy as jnp
from jax import lax
from jax.experimental import pallas as pl
from jax.experimental.pallas import tpu as pltpu
from jax.sharding import PartitionSpec as P

SECTIONS = 4
EPSILON = 1e-05
EXTRA = 16
F32 = jnp.float32
BF16 = jnp.bfloat16

ROOT = 0.3275911
COEFFS = (0.254829592, -0.284496736, 1.421413741, -1.453152027, 1.061405429)


def gelu_pair(x):
    bell = jnp.exp(-0.5 * x * x)
    t = 1.0 / (1.0 + (ROOT * math.sqrt(0.5)) * jnp.abs(x))
    poly = COEFFS[4]
    for a in (COEFFS[3], COEFFS[2], COEFFS[1], COEFFS[0]):
        poly = poly * t + a
    tail = (0.5 * poly * t) * bell
    cdf = jnp.where(x < 0.0, tail, 1.0 - tail)
    return x * cdf, cdf + x * bell * (1.0 / math.sqrt(2.0 * math.pi))


def split_parts(x):
    high = x.astype(BF16).astype(F32)
    return high, x - high


def write_extra(refs, small):
    high, low = split_parts(small)
    pad = jnp.zeros((EXTRA // 2 - small.shape[0], small.shape[1]), F32)
    rows = jnp.concatenate([high, pad, low, pad], axis=0).astype(BF16)
    for ref in refs:
        ref[ref.shape[0] - EXTRA :, :] = rows


def read_extra(ref, count):
    rows = ref[ref.shape[0] - EXTRA :, :].astype(F32)
    return rows[:count] + rows[EXTRA // 2 : EXTRA // 2 + count]


def slabs_of(order, ctx_bits, me_ctx, me_rep):
    count = 2 ** len(order)
    slabs = []
    for q in range(count):
        flip_ctx, flip_rep = 0, 0
        for place, (axis, bit) in enumerate(order):
            if q >> (len(order) - 1 - place) & 1:
                if axis == "ctx":
                    flip_ctx |= bit
                else:
                    flip_rep |= bit
        slabs.append((me_ctx ^ flip_ctx, (me_rep & 1) ^ flip_rep))
    return slabs


def main_kernel(
    blocks, order_a, order_b, where_ref, moved_ref, we_ref, be_ref, wr_ref, br_ref, gate_ref,
    back_ref, send_a, keep_a, send_b, keep_b,
    normed_s, low_s, hid_s, slope_s, gpre_s, gout_s, rstd_s, joined_s, acc_e, acc_r,
):
    groups, _, rows, width = moved_ref.shape
    pairs = groups * rows // 2
    both = 2 * width
    sigma = jax.nn.sigmoid(gate_ref[...])

    def gather(get, block):
        low = [g for g in range(groups) if not g & block]
        first = jnp.concatenate([get(g) for g in low], axis=0)
        second = jnp.concatenate([get(g | block) for g in low], axis=0)
        return jnp.concatenate([first, second], axis=1)

    def scatter(put, value, block):
        low = [g for g in range(groups) if not g & block]
        for i, g in enumerate(low):
            piece = value[i * rows : (i + 1) * rows]
            put(g, piece[:, :width])
            put(g | block, piece[:, width:])

    for s, block in enumerate(blocks):
        source = moved_ref if s == 0 else back_ref
        joined = gather(lambda g: source[g, 0], block).astype(F32)
        centred = joined - jnp.mean(joined, axis=-1, keepdims=True)
        rstd = lax.rsqrt(jnp.mean(centred * centred, axis=-1, keepdims=True) + EPSILON)
        normed = centred * rstd
        low = normed.astype(BF16)
        here = pl.ds(s * pairs, pairs)
        normed_s[here, :] = normed
        joined_s[here, :] = joined
        low_s[here, :] = low
        rstd_s[here, :] = rstd
        preact = jnp.dot(low, we_ref[...], preferred_element_type=F32) + be_ref[...]
        hidden, slope = gelu_pair(preact)
        hidden = hidden.astype(BF16)
        hid_s[here, :] = hidden
        slope_s[here, :] = slope
        mixed = jnp.dot(hidden, wr_ref[...], preferred_element_type=F32)
        result = (sigma * joined + mixed + br_ref[...]).astype(BF16)

        def put(g, piece):
            back_ref[g, 0] = piece

        scatter(put, result, block)

    sum_be = jnp.zeros((1, we_ref.shape[1]), F32)
    sum_br = jnp.zeros((1, both), F32)
    sum_gate = jnp.zeros((1, both), F32)
    for s in reversed(range(len(blocks))):
        block = blocks[s]
        here = pl.ds(s * pairs, pairs)
        source = moved_ref if s == len(blocks) - 1 else back_ref
        gout = gather(lambda g: source[g, 1], block)
        gout_s[here, :] = gout
        gfloat = gout.astype(F32)
        sum_br += jnp.sum(gfloat, axis=0, keepdims=True)
        sum_gate += jnp.sum(gfloat * joined_s[here, :], axis=0, keepdims=True)
        ghidden = lax.dot_general(gout, wr_ref[...], (((1,), (1,)), ((), ())), preferred_element_type=F32)
        gpre = ghidden * slope_s[here, :]
        sum_be += jnp.sum(gpre, axis=0, keepdims=True)
        gpre = gpre.astype(BF16)
        gpre_s[here, :] = gpre
        gnormed = lax.dot_general(gpre, we_ref[...], (((1,), (1,)), ((), ())), preferred_element_type=F32)
        normed = normed_s[here, :]
        inner = gnormed - jnp.mean(gnormed, axis=-1, keepdims=True)
        inner = inner - normed * jnp.mean(gnormed * normed, axis=-1, keepdims=True)
        gjoined = (sigma * gfloat + rstd_s[here, :] * inner).astype(BF16)

        def put(g, piece):
            back_ref[g, 1] = piece

        scatter(put, gjoined, block)

    rows_t = (((0,), (0,)), ((), ()))
    acc_e[...] = lax.dot_general(low_s[...], gpre_s[...], rows_t, preferred_element_type=F32)
    acc_r[...] = lax.dot_general(hid_s[...], gout_s[...], rows_t, preferred_element_type=F32)

    me_ctx, me_rep = where_ref[0], where_ref[1]
    slabs = slabs_of(order_a, None, me_ctx, me_rep)
    half = len(slabs) // 2
    size = acc_e.shape[0] * acc_e.shape[1] // (both * len(slabs))
    for q, (shard, side) in enumerate(slabs):
        target, at = (keep_a, q) if q < half else (send_a, q - half)
        row = pl.multiple_of(shard * size, size)
        lane = pl.multiple_of(side * both, both)
        target[at * size : (at + 1) * size, :] = acc_e[pl.ds(row, size), pl.ds(lane, both)].astype(BF16)
    slabs = slabs_of(order_b, None, me_ctx, me_rep)
    for q, (shard, side) in enumerate(slabs):
        target, at = (keep_b, q) if q < half else (send_b, q - half)
        row = pl.multiple_of((shard * 2 + side) * size, size)
        target[at * size : (at + 1) * size, :] = acc_r[pl.ds(row, size), :].astype(BF16)
    small = jnp.concatenate(
        [sum_be[:, :both], sum_be[:, both:], sum_br, sum_gate * sigma * (1.0 - sigma)], axis=0
    )
    write_extra((send_a, keep_a), small)


def halve_kernel(extra, keep_ref, recv_ref, send_out, keep_out):
    half = (keep_ref.shape[0] - extra) // 2
    for out, start in ((keep_out, 0), (send_out, half)):
        span = slice(start, start + half)
        out[:half, :] = (keep_ref[span, :].astype(F32) + recv_ref[span, :].astype(F32)).astype(BF16)
    if extra:
        write_extra((send_out, keep_out), read_extra(keep_ref, 4) + read_extra(recv_ref, 4))


def add_kernel(extra, keep_ref, recv_ref, out_ref):
    size = keep_ref.shape[0] - extra
    out_ref[:size, :] = (keep_ref[:size, :].astype(F32) + recv_ref[:size, :].astype(F32)).astype(BF16)
    if extra:
        write_extra((out_ref,), read_extra(keep_ref, 4) + read_extra(recv_ref, 4))


def final_kernel(factor, where_ref, own_a, other_a, own_b, other_b, out_e, out_be, out_r, out_br, out_gate):
    side = where_ref[1] & 1
    size, lanes = own_b.shape
    rows = pl.multiple_of(side * size, size)
    rest = pl.multiple_of((1 - side) * size, size)
    out_r[pl.ds(rows, size), :] = own_b[...].astype(F32) * factor
    out_r[pl.ds(rest, size), :] = other_b[...].astype(F32) * factor
    here = pl.multiple_of(side * lanes, lanes)
    there = pl.multiple_of((1 - side) * lanes, lanes)
    out_e[:, pl.ds(here, lanes)] = own_a[:size, :].astype(F32) * factor
    out_e[:, pl.ds(there, lanes)] = other_a[...].astype(F32) * factor
    small = read_extra(own_a, 4) * factor
    out_be[:, :lanes] = small[0:1]
    out_be[:, lanes:] = small[1:2]
    out_br[...] = small[2:3]
    out_gate[...] = small[3:4]


VMEM = pl.BlockSpec(memory_space=pltpu.VMEM)
SMEM = pl.BlockSpec(memory_space=pltpu.SMEM)


def call(kernel, name, shapes, args, scratch=(), scalars=0):
    return pl.pallas_call(
        kernel,
        name=name,
        out_shape=shapes,
        in_specs=[SMEM] * scalars + [VMEM] * (len(args) - scalars),
        out_specs=[VMEM] * len(shapes),
        scratch_shapes=scratch,
        compiler_params=pltpu.CompilerParams(vmem_limit_bytes=48 * 2**20),
    )(*args)


def rows_of(count, lanes):
    return jax.ShapeDtypeStruct((count, lanes), BF16)


def swap(value, axis, bit):
    return lax.ppermute(value, axis, [(i, i ^ bit) for i in range(lax.axis_size(axis))])


def body(inputs, w_expand, b_expand, w_reduce, b_reduce, gate_logit, cotangent):
    rows, width = inputs.shape[1:]
    devs, reps = lax.axis_size("ctx"), lax.axis_size("rep")
    slice_rows = rows // devs
    count = devs.bit_length() - 1
    groups = min(devs, 2**SECTIONS)
    inner = devs // groups
    blocks = [2 ** ((count - 1 - s) % count) // inner for s in range(SECTIONS)]
    both, hid = w_expand.shape

    ctx_bits = [("ctx", 2**i) for i in range(count)]
    rep_bits = [("rep", 2**i) for i in range(reps.bit_length() - 1)]
    order_a = ctx_bits + rep_bits[:1]
    order_b = ctx_bits[:1] + ctx_bits[2:] + rep_bits[:1] + ctx_bits[1:2]
    where = jnp.stack([lax.axis_index("ctx"), lax.axis_index("rep")]).astype(jnp.int32)

    packed = jnp.stack([inputs.reshape(devs, slice_rows, width), cotangent.reshape(devs, slice_rows, width)], axis=1)
    moved = lax.all_to_all(packed, "ctx", split_axis=0, concat_axis=0, tiled=True)
    moved = moved.reshape(groups, inner, 2, slice_rows, width).swapaxes(1, 2)
    moved = moved.reshape(groups, 2, inner * slice_rows, width)

    pairs = rows // 2
    total = SECTIONS * pairs
    half = both * hid // both // 2
    back, send_a, keep_a, send_b, keep_b = call(
        functools.partial(main_kernel, blocks, order_a, order_b),
        "sections",
        [
            jax.ShapeDtypeStruct(moved.shape, BF16),
            rows_of(half + EXTRA, both),
            rows_of(half + EXTRA, both),
            rows_of(half, both),
            rows_of(half, both),
        ],
        (where, moved, w_expand, b_expand[None], w_reduce, b_reduce[None], gate_logit[None]),
        [
            pltpu.VMEM((total, both), F32),
            pltpu.VMEM((total, both), BF16),
            pltpu.VMEM((total, hid), BF16),
            pltpu.VMEM((total, hid), F32),
            pltpu.VMEM((total, hid), BF16),
            pltpu.VMEM((total, both), BF16),
            pltpu.VMEM((total, 1), F32),
            pltpu.VMEM((total, both), F32),
            pltpu.VMEM((both, hid), F32),
            pltpu.VMEM((hid, both), F32),
        ],
        scalars=1,
    )

    back = back.reshape(groups, 2, inner, slice_rows, width).swapaxes(1, 2).reshape(devs, 2, slice_rows, width)
    home = lax.all_to_all(back, "ctx", split_axis=0, concat_axis=0, tiled=True)
    outputs = home[:, 0].reshape(inputs.shape)
    grad_inputs = home[:, 1].reshape(inputs.shape)

    def halve(send, keep, order, extra):
        for step, (axis, bit) in enumerate(order):
            received = swap(send, axis, bit)
            if step + 1 == len(order):
                return call(functools.partial(add_kernel, extra), "add", [rows_of(*keep.shape)], (keep, received))[0]
            size = (keep.shape[0] - extra) // 2 + extra
            send, keep = call(
                functools.partial(halve_kernel, extra), "halve", [rows_of(size, both)] * 2, (keep, received)
            )

    own_a = halve(send_a, keep_a, order_a, EXTRA)
    own_b = halve(send_b, keep_b, order_b, 0)
    for axis, bit in rep_bits[1:]:
        got_a, got_b = swap(own_a, axis, bit), swap(own_b, axis, bit)
        own_a = call(functools.partial(add_kernel, EXTRA), "add", [rows_of(*own_a.shape)], (own_a, got_a))[0]
        own_b = call(functools.partial(add_kernel, 0), "add", [rows_of(*own_b.shape)], (own_b, got_b))[0]
    size = own_b.shape[0]
    other_a, other_b = swap(own_a[:size], "rep", 1), swap(own_b, "rep", 1)
    factor = 1.0 / math.sqrt(reps * devs * rows)
    grad_e, grad_be, grad_r, grad_br, grad_gate = call(
        functools.partial(final_kernel, factor),
        "final",
        [
            jax.ShapeDtypeStruct((both // devs, hid), F32),
            jax.ShapeDtypeStruct((1, hid), F32),
            jax.ShapeDtypeStruct((hid // devs, both), F32),
            jax.ShapeDtypeStruct((1, both), F32),
            jax.ShapeDtypeStruct((1, both), F32),
        ],
        (where, own_a, other_a, own_b, other_b),
        scalars=1,
    )
    return outputs, grad_inputs, grad_e, grad_be[0], grad_r, grad_br[0], grad_gate[0]


def solution(mesh):
    return jax.shard_map(
        body,
        mesh=mesh,
        in_specs=(P("rep", "ctx", None), P(), P(), P(), P(), P(), P("rep", "ctx", None)),
        out_specs=(
            P("rep", "ctx", None),
            P("rep", "ctx", None),
            P("ctx", None),
            P(),
            P("ctx", None),
            P(),
            P(),
        ),
        check_vma=False,
    )
```

time: 184 us -> 63.3 us (0.34)
  waiting for transfers between devices: 74.2 us -> 24 us
  blocking collectives: 41.1 us -> 0 us
  matrix products: 23 us -> 0 us
  between operations: 14.6 us -> 0.74 us
  Pallas kernels: 0 us -> 11.3 us
  other arithmetic: 12.3 us -> 1.86 us
  starting transfers between devices: 15.7 us -> 22.4 us
    psum x1 -> x0, blocking collectives: 41.1 us -> none  [body(): lax.psum((totals[1], totals[3], totals[4]), ('ctx', 'rep'))]
    reduce_scatter x2 -> x0, waiting for transfers between devices: 32 us -> none  [the longest x1 32 us: body(): lax.psum_scatter(totals[2], 'ctx', scatter_dimension=0, tiled=True)]
    psum x1 -> x0, waiting for transfers between devices: 27.3 us -> none  [body(): lax.psum(part_expand.astype(jnp.bfloat16), 'rep').astype(jnp.float32)]
    dot_general x24 -> x0, matrix products: 23 us -> none  [the longest x4 6.3 us: switch_forward(): jnp.dot(normed_low, w_expand, preferred_element_type=jnp.float32) + b_expand]
    ppermute x0 -> x12, waiting for transfers between devices: none -> 17.2 us  [swap(): lax.ppermute(value, axis, [(i, i ^ bit) for i in range(lax.axis_size(axis...]
    ppermute x0 -> x12, starting transfers between devices: none -> 13.8 us  [swap(): lax.ppermute(value, axis, [(i, i ^ bit) for i in range(lax.axis_size(axis...]
    pallas_call x0 -> x12, Pallas kernels: none -> 11.3 us  [call(): pl.pallas_call(kernel, name=name, out_shape=shapes, in_specs=[SMEM] * sca...]
    all_to_all x4 -> x2, waiting for transfers between devices: 14.8 us -> 6.84 us  [the longest x1 6.84 us: body(): lax.all_to_all(packed, 'ctx', split_axis=0, concat_axis=0, tiled=True)]
  transfers between devices with their start and end apart: 7 -> 14, of which waited for: 5 -> 7; matrix products, arithmetic and copies ran while one was open for 7% -> 1% of each run, Pallas kernels for 0% -> 1%
where the time goes in v1:
time: 63.3 us; the launch traced here: 62.9 us
  waiting for transfers between devices  24 us (38%)
  starting transfers between devices  22.4 us (35%)
  Pallas kernels  11.3 us (18%)
  local copies, waits for them, and re-layouts  2.63 us (4%)
  other arithmetic  1.86 us (3%)
  between operations  0.74 us (1%)
    ppermute x12, waiting for transfers between devices, swap(): lax.ppermute(value, axis, [(i, i ^ bit) for i in range(lax.axis_size(axis...  17.2 us
    ppermute x12, starting transfers between devices, swap(): lax.ppermute(value, axis, [(i, i ^ bit) for i in range(lax.axis_size(axis...  13.8 us
    pallas_call x12, Pallas kernels, call(): pl.pallas_call(kernel, name=name, out_shape=shapes, in_specs=[SMEM] * sca...  11.3 us
    all_to_all x1, waiting for transfers between devices, body(): lax.all_to_all(packed, 'ctx', split_axis=0, concat_axis=0, tiled=True)  6.84 us
    all_to_all x1, starting transfers between devices, body(): lax.all_to_all(packed, 'ctx', split_axis=0, concat_axis=0, tiled=True)  5.17 us
    all_to_all x1, starting transfers between devices, body(): home = lax.all_to_all(back, 'ctx', split_axis=0, concat_axis=0, tiled=True)  3.41 us
    unnamed x10, local copies, waits for them, and re-layouts  1.91 us
    another operation x1, other arithmetic, body(): jnp.stack([inputs.reshape(devs, slice_rows, width), cotangent.reshape(dev...  1.79 us
  transfers between devices with their start and end apart: 14, of which 7 were waited for; matrix products, arithmetic and copies ran while one was open for 1% of the time, Pallas kernels for 1%

profile of v1, /device:TPU:0, one launch (start us, length us, event | category | flops | bytes accessed | tf_op | source)
XLA Modules:
  0.0 62.9 jit_solution(14159256099262956990)
XLA Ops:
  0.6 1.8 %pad_maximum_fusion = bf16[8,2,32,256]{3,2,1,0:T(8,128)(2,1)} fusion(bf16[8,1,32,256]{3,2,1,0:T(8,128)(2,1)} %bitcast.15, bf16[8,1,32,256]{3,2,1,0:T(8,128)(2,1)} %bitcast.16), kind=kLoop, calls=%fused_computation | loop fusion | flops 131072 | bytes 524288 | tf_op jit(solution)/shard_map/stack | solution.py:239
  2.4 5.2 %all-to-all-start = ((bf16[8,2,32,256]{3,2,1,0:T(8,128)(2,1)}), bf16[8,2,32,256]{3,2,1,0:T(8,128)(2,1)S(1)}, u32[]{:S(2)}, u32[]{:S(2)}) async-start(bf16[8,2,32,256]{3,2,1,0:T(8,128)(2,1)} %pad_maximum_fusion), calls=%async_computation | async-start | bytes 524288 | tf_op jit(solution)/shard_map/all_to_all | solution.py:240
  7.6 0.0 copy-start.2
  7.6 0.1 pad_add_fusion.where_ref
  7.7 6.8 %all-to-all-done.moved_ref = bf16[8,2,32,256]{3,2,1,0:T(8,128)(2,1)S(1)} async-done(((bf16[8,2,32,256]{3,2,1,0:T(8,128)(2,1)}), bf16[8,2,32,256]{3,2,1,0:T(8,128)(2,1)S(1)}, u32[]{:S(2)}, u32[]{:S(2)}) %all-to-all-start) | async-done | bytes 262176 | tf_op jit(solution)/shard_map/all_to_all | solution.py:240
  14.5 0.7 %copy-done.3 = f32[512]{0:T(512)S(1)} copy-done((f32[512]{0:T(512)S(1)}, f32[512]{0:T(512)}, u32[]{:S(2)}) %copy-start.3) | copy-done | bytes 2072
  15.2 1.2 %copy-done.1 = bf16[1024,512]{1,0:T(8,128)(2,1)S(1)} copy-done((bf16[1024,512]{1,0:T(8,128)(2,1)S(1)}, bf16[1024,512]{1,0:T(8,128)(2,1)}, u32[]{:S(2)}) %copy-start.1) | copy-done | bytes 1048600
  16.4 9.4 %sections.1 = (bf16[8,2,32,256]{3,2,1,0:T(8,128)(2,1)}, bf16[528,512]{1,0:T(8,128)(2,1)S(1)}, bf16[528,512]{1,0:T(8,128)(2,1)S(1)}, bf16[512,512]{1,0:T(8,128)(2,1)S(1)}, bf16[512,512]{1,0:T(8,128)(2,1)S(1)}) custom-call(s32[2]{0:T(128)S(1)} %pad_add_fusion.where_ref, bf16[8,2,32,256]{3,2,1,0:T(8,128)(2,1)S(1)} %all-to-all-done.moved_ref, ...), custom_call_target="tpu_custom_call" | custom-call | tf_op jit(solution)/shard_map/sections/pallas_call | solution.py:204
  25.8 0.5 collective-permute-start.6
  26.3 1.4 %collective-permute-done.recv_ref = bf16[528,512]{1,0:T(8,128)(2,1)S(1)} collective-permute-done((bf16[528,512]{1,0:T(8,128)(2,1)S(1)}, bf16[528,512]{1,0:T(8,128)(2,1)S(1)}, u32[]{:S(2)}, u32[]{:S(2)}) %collective-permute-start) | collective-permute-done | bytes 540704 | tf_op jit(solution)/shard_map/ppermute | solution.py:220
  27.7 0.1 halve.6
  27.9 0.6 collective-permute-start.1
  28.5 0.1 halve.9
  28.6 0.6 collective-permute-start.7
  29.2 7.4 %collective-permute-done.1.recv_ref = bf16[272,512]{1,0:T(8,128)(2,1)S(1)} collective-permute-done((bf16[272,512]{1,0:T(8,128)(2,1)S(1)}, bf16[272,512]{1,0:T(8,128)(2,1)S(1)}, u32[]{:S(2)}, u32[]{:S(2)}) %collective-permute-start.1) | collective-permute-done | bytes 278560 | tf_op jit(solution)/shard_map/ppermute | solution.py:220
  36.6 0.1 halve.7
  36.7 0.6 collective-permute-start.2
  37.3 0.1 halve.10
  37.4 1.6 %collective-permute-start.8 = (bf16[128,512]{1,0:T(8,128)(2,1)S(1)}, bf16[128,512]{1,0:T(8,128)(2,1)S(1)}, u32[]{:S(2)}, u32[]{:S(2)}) collective-permute-start(bf16[128,512]{1,0:T(8,128)(2,1)S(1)} %get-tuple-element.43), channel_id=1, source_target_pairs={{0,1},{1,0},{2,3},{3,2},{4,5},{5,4},{6,7},{7,6},{8,9},{9,8},{10,11... | collective-permute-start | bytes 393224 | tf_op jit(solution)/shard_map/ppermute | solution.py:220
  39.0 3.4 %all-to-all-start.1 = ((bf16[8,2,32,256]{3,2,1,0:T(8,128)(2,1)}), bf16[8,2,32,256]{3,2,1,0:T(8,128)(2,1)S(1)}, u32[]{:S(2)}, u32[]{:S(2)}) async-start(bf16[8,2,32,256]{3,2,1,0:T(8,128)(2,1)} %get-tuple-element.29), calls=%async_computation.1 | async-start | bytes 524288 | tf_op jit(solution)/shard_map/all_to_all | solution.py:274
  42.5 1.1 %collective-permute-start.3 = (bf16[80,512]{1,0:T(8,128)(2,1)S(1)}, bf16[80,512]{1,0:T(8,128)(2,1)S(1)}, u32[]{:S(2)}, u32[]{:S(2)}) collective-permute-start(bf16[80,512]{1,0:T(8,128)(2,1)S(1)} %get-tuple-element.37), channel_id=1, source_target_pairs={{0,1},{1,0},{2,3},{3,2},{4,5},{5,4},{6,7},{7,6},{8,9},{9,8},{10,11... | collective-permute-start | bytes 245768 | tf_op jit(solution)/shard_map/ppermute | solution.py:220
  43.6 1.4 %collective-permute-start.9 = (bf16[64,512]{1,0:T(8,128)(2,1)S(1)}, bf16[64,512]{1,0:T(8,128)(2,1)S(1)}, u32[]{:S(2)}, u32[]{:S(2)}) collective-permute-start(bf16[64,512]{1,0:T(8,128)(2,1)S(1)} %get-tuple-element.45), channel_id=1, source_target_pairs={{0,8},{4,12},{8,0},{12,4},{16,24},{20,28},{24,16},{28,20},{1,9},{5... | collective-permute-start | bytes 196616 | tf_op jit(solution)/shard_map/ppermute | solution.py:220
  45.1 2.3 %collective-permute-done.3.recv_ref = bf16[80,512]{1,0:T(8,128)(2,1)S(1)} collective-permute-done((bf16[80,512]{1,0:T(8,128)(2,1)S(1)}, bf16[80,512]{1,0:T(8,128)(2,1)S(1)}, u32[]{:S(2)}, u32[]{:S(2)}) %collective-permute-start.3) | collective-permute-done | bytes 81952 | tf_op jit(solution)/shard_map/ppermute | solution.py:220
  47.4 2.7 %collective-permute-start.4 = (bf16[80,512]{1,0:T(8,128)(2,1)S(1)}, bf16[80,512]{1,0:T(8,128)(2,1)S(1)}, u32[]{:S(2)}, u32[]{:S(2)}) collective-permute-start(bf16[80,512]{1,0:T(8,128)(2,1)S(1)} %add.6.keep_ref), channel_id=1, source_target_pairs={{0,2},{1,3},{2,0},{3,1},{4,6},{5,7},{6,4},{7,5},{8,10},{9,11},{10,... | collective-permute-start | bytes 245768 | tf_op jit(solution)/shard_map/ppermute | solution.py:220
  50.0 2.4 %collective-permute-start.10 = (bf16[64,512]{1,0:T(8,128)(2,1)S(1)}, bf16[64,512]{1,0:T(8,128)(2,1)S(1)}, u32[]{:S(2)}, u32[]{:S(2)}) collective-permute-start(bf16[64,512]{1,0:T(8,128)(2,1)S(1)} %add.8.keep_ref), channel_id=1, source_target_pairs={{0,2},{1,3},{2,0},{3,1},{4,6},{5,7},{6,4},{7,5},{8,10},{9,11},{10,... | collective-permute-start | bytes 196616 | tf_op jit(solution)/shard_map/ppermute | solution.py:220
  52.5 4.0 %collective-permute-done.10.recv_ref = bf16[64,512]{1,0:T(8,128)(2,1)S(1)} collective-permute-done((bf16[64,512]{1,0:T(8,128)(2,1)S(1)}, bf16[64,512]{1,0:T(8,128)(2,1)S(1)}, u32[]{:S(2)}, u32[]{:S(2)}) %collective-permute-start.10) | collective-permute-done | bytes 65568 | tf_op jit(solution)/shard_map/ppermute | solution.py:220
  56.5 0.2 collective-permute-start.11
  56.7 1.9 %collective-permute-start.5 = (bf16[64,512]{1,0:T(8,128)(2,1)S(1)}, bf16[64,512]{1,0:T(8,128)(2,1)S(1)}, u32[]{:S(2)}, u32[]{:S(2)}) collective-permute-start(bf16[64,512]{1,0:T(8,128)(2,1)S(1)} %slice.14), channel_id=1, source_target_pairs={{0,1},{1,0},{2,3},{3,2},{4,5},{5,4},{6,7},{7,6},{8,9},{9,8},{10,11... | collective-permute-start | bytes 196616 | tf_op jit(solution)/shard_map/ppermute | solution.py:220
  58.7 0.7 %fusion = (bf16[8,1,32,256]{3,2,1,0:T(8,128)(2,1)}, bf16[8,1,32,256]{3,2,1,0:T(8,128)(2,1)}) fusion(bf16[8,2,32,256]{3,2,1,0:T(8,128)(2,1)S(1)} %all-to-all-done.1), kind=kLoop, calls=%fused_computation.2 | loop fusion | bytes 524288 | tf_op jit(solution)/shard_map/slice | solution.py:276
  59.4 1.4 %collective-permute-done.11.other_b = bf16[64,512]{1,0:T(8,128)(2,1)S(1)} collective-permute-done((bf16[64,512]{1,0:T(8,128)(2,1)S(1)}, bf16[64,512]{1,0:T(8,128)(2,1)S(1)}, u32[]{:S(2)}, u32[]{:S(2)}) %collective-permute-start.11) | collective-permute-done | bytes 65568 | tf_op jit(solution)/shard_map/ppermute | solution.py:220
  60.8 0.7 %collective-permute-done.5.other_a = bf16[64,512]{1,0:T(8,128)(2,1)S(1)} collective-permute-done((bf16[64,512]{1,0:T(8,128)(2,1)S(1)}, bf16[64,512]{1,0:T(8,128)(2,1)S(1)}, u32[]{:S(2)}, u32[]{:S(2)}) %collective-permute-start.5) | collective-permute-done | bytes 65568 | tf_op jit(solution)/shard_map/ppermute | solution.py:220
  61.5 1.4 %final.1 = (f32[64,1024]{1,0:T(8,128)}, f32[1,1024]{1,0:T(1,128)}, f32[128,512]{1,0:T(8,128)}, f32[1,512]{1,0:T(1,128)}, f32[1,512]{1,0:T(1,128)}) custom-call(s32[2]{0:T(128)S(1)} %pad_add_fusion.where_ref, bf16[80,512]{1,0:T(8,128)(2,1)S(1)} %add.7.own_a, bf16[64,512]{1,0:T(8,128)(2,1)S(1)} %collective-permute-done.5.other_a, ...), custom_call_target="tpu_custom_call" | custom-call | tf_op jit(solution)/shard_map/final/pallas_call | solution.py:204
  (22 shorter events, 0.2 us)
Async XLA Ops:
  0.6 13.9 %copy-start = (bf16[512,1024]{1,0:T(8,128)(2,1)S(1)}, bf16[512,1024]{1,0:T(8,128)(2,1)}, u32[]{:S(2)}) copy-start(bf16[512,1024]{1,0:T(8,128)(2,1)} %we_ref.1) | copy-start | bytes 3145732
  2.4 12.1 %all-to-all-start = ((bf16[8,2,32,256]{3,2,1,0:T(8,128)(2,1)}), bf16[8,2,32,256]{3,2,1,0:T(8,128)(2,1)S(1)}, u32[]{:S(2)}, u32[]{:S(2)}) async-start(bf16[8,2,32,256]{3,2,1,0:T(8,128)(2,1)} %pad_maximum_fusion), calls=%async_computation | async-start | bytes 524288 | tf_op jit(solution)/shard_map/all_to_all | solution.py:240
  7.6 6.9 %copy-start.4 = (f32[512]{0:T(512)S(1)}, f32[512]{0:T(512)}, u32[]{:S(2)}) copy-start(f32[512]{0:T(512)} %param.12) | copy-start | bytes 6148
  7.6 6.9 %copy-start.2 = (f32[1024]{0:T(1024)S(1)}, f32[1024]{0:T(1024)}, u32[]{:S(2)}) copy-start(f32[1024]{0:T(1024)} %param.9) | copy-start | bytes 12292
  14.5 0.7 %copy-start.3 = (f32[512]{0:T(512)S(1)}, f32[512]{0:T(512)}, u32[]{:S(2)}) copy-start(f32[512]{0:T(512)} %param.11) | copy-start | bytes 6148
  15.2 1.2 %copy-start.1 = (bf16[1024,512]{1,0:T(8,128)(2,1)S(1)}, bf16[1024,512]{1,0:T(8,128)(2,1)}, u32[]{:S(2)}) copy-start(bf16[1024,512]{1,0:T(8,128)(2,1)} %wr_ref.1) | copy-start | bytes 3145732
  25.8 1.9 %collective-permute-start = (bf16[528,512]{1,0:T(8,128)(2,1)S(1)}, bf16[528,512]{1,0:T(8,128)(2,1)S(1)}, u32[]{:S(2)}, u32[]{:S(2)}) collective-permute-start(bf16[528,512]{1,0:T(8,128)(2,1)S(1)} %get-tuple-element.31), channel_id=1, source_target_pairs={{0,4},{4,0},{8,12},{12,8},{16,20},{20,16},{24,28},{28,24},{1,5},{5... | collective-permute-start | bytes 1622024 | tf_op jit(solution)/shard_map/ppermute | solution.py:220
  25.8 2.7 %collective-permute-start.6 = (bf16[512,512]{1,0:T(8,128)(2,1)S(1)}, bf16[512,512]{1,0:T(8,128)(2,1)S(1)}, u32[]{:S(2)}, u32[]{:S(2)}) collective-permute-start(bf16[512,512]{1,0:T(8,128)(2,1)S(1)} %get-tuple-element.39), channel_id=1, source_target_pairs={{0,4},{4,0},{8,12},{12,8},{16,20},{20,16},{24,28},{28,24},{1,5},{5... | collective-permute-start | bytes 1572872 | tf_op jit(solution)/shard_map/ppermute | solution.py:220
  27.9 8.8 %collective-permute-start.1 = (bf16[272,512]{1,0:T(8,128)(2,1)S(1)}, bf16[272,512]{1,0:T(8,128)(2,1)S(1)}, u32[]{:S(2)}, u32[]{:S(2)}) collective-permute-start(bf16[272,512]{1,0:T(8,128)(2,1)S(1)} %get-tuple-element.33), channel_id=1, source_target_pairs={{0,8},{4,12},{8,0},{12,4},{16,24},{20,28},{24,16},{28,20},{1,9},{5... | collective-permute-start | bytes 835592 | tf_op jit(solution)/shard_map/ppermute | solution.py:220
  28.6 8.7 %collective-permute-start.7 = (bf16[256,512]{1,0:T(8,128)(2,1)S(1)}, bf16[256,512]{1,0:T(8,128)(2,1)S(1)}, u32[]{:S(2)}, u32[]{:S(2)}) collective-permute-start(bf16[256,512]{1,0:T(8,128)(2,1)S(1)} %get-tuple-element.41), channel_id=1, source_target_pairs={{0,16},{4,20},{8,24},{12,28},{16,0},{20,4},{24,8},{28,12},{1,17},{... | collective-permute-start | bytes 786440 | tf_op jit(solution)/shard_map/ppermute | solution.py:220
  36.7 5.8 %collective-permute-start.2 = (bf16[144,512]{1,0:T(8,128)(2,1)S(1)}, bf16[144,512]{1,0:T(8,128)(2,1)S(1)}, u32[]{:S(2)}, u32[]{:S(2)}) collective-permute-start(bf16[144,512]{1,0:T(8,128)(2,1)S(1)} %get-tuple-element.35), channel_id=1, source_target_pairs={{0,16},{4,20},{8,24},{12,28},{16,0},{20,4},{24,8},{28,12},{1,17},{... | collective-permute-start | bytes 442376 | tf_op jit(solution)/shard_map/ppermute | solution.py:220
  37.4 6.2 %collective-permute-start.8 = (bf16[128,512]{1,0:T(8,128)(2,1)S(1)}, bf16[128,512]{1,0:T(8,128)(2,1)S(1)}, u32[]{:S(2)}, u32[]{:S(2)}) collective-permute-start(bf16[128,512]{1,0:T(8,128)(2,1)S(1)} %get-tuple-element.43), channel_id=1, source_target_pairs={{0,1},{1,0},{2,3},{3,2},{4,5},{5,4},{6,7},{7,6},{8,9},{9,8},{10,11... | collective-permute-start | bytes 393224 | tf_op jit(solution)/shard_map/ppermute | solution.py:220
  39.0 19.6 %all-to-all-start.1 = ((bf16[8,2,32,256]{3,2,1,0:T(8,128)(2,1)}), bf16[8,2,32,256]{3,2,1,0:T(8,128)(2,1)S(1)}, u32[]{:S(2)}, u32[]{:S(2)}) async-start(bf16[8,2,32,256]{3,2,1,0:T(8,128)(2,1)} %get-tuple-element.29), calls=%async_computation.1 | async-start | bytes 524288 | tf_op jit(solution)/shard_map/all_to_all | solution.py:274
  42.5 4.8 %collective-permute-start.3 = (bf16[80,512]{1,0:T(8,128)(2,1)S(1)}, bf16[80,512]{1,0:T(8,128)(2,1)S(1)}, u32[]{:S(2)}, u32[]{:S(2)}) collective-permute-start(bf16[80,512]{1,0:T(8,128)(2,1)S(1)} %get-tuple-element.37), channel_id=1, source_target_pairs={{0,1},{1,0},{2,3},{3,2},{4,5},{5,4},{6,7},{7,6},{8,9},{9,8},{10,11... | collective-permute-start | bytes 245768 | tf_op jit(solution)/shard_map/ppermute | solution.py:220
  43.6 6.4 %collective-permute-start.9 = (bf16[64,512]{1,0:T(8,128)(2,1)S(1)}, bf16[64,512]{1,0:T(8,128)(2,1)S(1)}, u32[]{:S(2)}, u32[]{:S(2)}) collective-permute-start(bf16[64,512]{1,0:T(8,128)(2,1)S(1)} %get-tuple-element.45), channel_id=1, source_target_pairs={{0,8},{4,12},{8,0},{12,4},{16,24},{20,28},{24,16},{28,20},{1,9},{5... | collective-permute-start | bytes 196616 | tf_op jit(solution)/shard_map/ppermute | solution.py:220
  47.4 9.3 %collective-permute-start.4 = (bf16[80,512]{1,0:T(8,128)(2,1)S(1)}, bf16[80,512]{1,0:T(8,128)(2,1)S(1)}, u32[]{:S(2)}, u32[]{:S(2)}) collective-permute-start(bf16[80,512]{1,0:T(8,128)(2,1)S(1)} %add.6.keep_ref), channel_id=1, source_target_pairs={{0,2},{1,3},{2,0},{3,1},{4,6},{5,7},{6,4},{7,5},{8,10},{9,11},{10,... | collective-permute-start | bytes 245768 | tf_op jit(solution)/shard_map/ppermute | solution.py:220
  50.0 6.4 %collective-permute-start.10 = (bf16[64,512]{1,0:T(8,128)(2,1)S(1)}, bf16[64,512]{1,0:T(8,128)(2,1)S(1)}, u32[]{:S(2)}, u32[]{:S(2)}) collective-permute-start(bf16[64,512]{1,0:T(8,128)(2,1)S(1)} %add.8.keep_ref), channel_id=1, source_target_pairs={{0,2},{1,3},{2,0},{3,1},{4,6},{5,7},{6,4},{7,5},{8,10},{9,11},{10,... | collective-permute-start | bytes 196616 | tf_op jit(solution)/shard_map/ppermute | solution.py:220
  56.5 4.3 %collective-permute-start.11 = (bf16[64,512]{1,0:T(8,128)(2,1)S(1)}, bf16[64,512]{1,0:T(8,128)(2,1)S(1)}, u32[]{:S(2)}, u32[]{:S(2)}) collective-permute-start(bf16[64,512]{1,0:T(8,128)(2,1)S(1)} %add.9.own_b), channel_id=1, source_target_pairs={{0,1},{1,0},{2,3},{3,2},{4,5},{5,4},{6,7},{7,6},{8,9},{9,8},{10,11... | collective-permute-start | bytes 196616 | tf_op jit(solution)/shard_map/ppermute | solution.py:220
  56.7 4.8 %collective-permute-start.5 = (bf16[64,512]{1,0:T(8,128)(2,1)S(1)}, bf16[64,512]{1,0:T(8,128)(2,1)S(1)}, u32[]{:S(2)}, u32[]{:S(2)}) collective-permute-start(bf16[64,512]{1,0:T(8,128)(2,1)S(1)} %slice.14), channel_id=1, source_target_pairs={{0,1},{1,0},{2,3},{3,2},{4,5},{5,4},{6,7},{7,6},{8,9},{9,8},{10,11... | collective-permute-start | bytes 196616 | tf_op jit(solution)/shard_map/ppermute | solution.py:220

commit v2 on v1

--- a/solution.py
+++ b/solution.py
@@ -47,7 +47,7 @@
     return rows[:count] + rows[EXTRA // 2 : EXTRA // 2 + count]
 
 
-def slabs_of(order, ctx_bits, me_ctx, me_rep):
+def slabs_of(order, me_ctx, me_rep):
     count = 2 ** len(order)
     slabs = []
     for q in range(count):
@@ -62,11 +62,60 @@
     return slabs
 
 
-def main_kernel(
-    blocks, order_a, order_b, where_ref, moved_ref, we_ref, be_ref, wr_ref, br_ref, gate_ref,
-    back_ref, send_a, keep_a, send_b, keep_b,
-    normed_s, low_s, hid_s, slope_s, gpre_s, gout_s, rstd_s, joined_s, acc_e, acc_r,
-):
+def prep_kernel(we_ref, be_ref, wr_ref, br_ref, gate_ref, we_out, wet_out, wr_out, wrt_out, be_out, br_out, gate_out, sems):
+    pairs = (
+        (we_ref, we_out), (wr_ref, wr_out), (be_ref, be_out), (br_ref, br_out), (gate_ref, gate_out),
+    )
+    copies = [pltpu.make_async_copy(a, b, sems.at[i]) for i, (a, b) in enumerate(pairs)]
+    for copy in copies:
+        copy.start()
+    copies[0].wait()
+    wet_out[...] = we_out[...].T
+    copies[1].wait()
+    wrt_out[...] = wr_out[...].T
+    for copy in copies[2:]:
+        copy.wait()
+
+
+def pack_kernel(where_ref, inputs_ref, cot_ref, send_ref, keep_ref, inputs_s, cot_s, sems):
+    me = where_ref[0]
+    chips, _, rows, _ = send_ref.shape
+    sources = (inputs_s, cot_s)
+    copies = [pltpu.make_async_copy(a, b, sems.at[i]) for i, (a, b) in enumerate(zip((inputs_ref, cot_ref), sources))]
+    for copy in copies:
+        copy.start()
+    for which, source in enumerate(sources):
+        copies[which].wait()
+        for k in range(chips):
+            for out, to in ((send_ref, me ^ (2 * k) ^ 1), (keep_ref, me ^ (2 * k))):
+                out[k, which] = source[pl.ds(pl.multiple_of(to * rows, rows), rows), :]
+
+
+def relay_kernel(keep_ref, got_ref, *outs):
+    for k, out in enumerate(outs, 1):
+        out[0] = keep_ref[k]
+        out[1] = got_ref[k]
+
+
+def main_kernel(blocks, chains, pieces, where_ref, *refs):
+    arrived, refs = refs[:pieces], refs[pieces:]
+    (
+        we_ref, wet_ref, wr_ref, wrt_ref, be_ref, br_ref, gate_ref,
+    ) = refs[:7]
+    back_ref, messages, refs = refs[7], refs[8 : 8 + 2 * len(chains)], refs[8 + 2 * len(chains) :]
+    (
+        normed_s, low_s, hid_s, slope_s, gpre_s, gout_s, rstd_s, joined_s, acc_e, acc_r, *moved_s,
+    ) = refs
+    if pieces == 1:
+        moved_ref = arrived[0]
+    else:
+        moved_ref = moved_s[0]
+        keep_ref, got_ref, *relayed = arrived
+        for core, ref in enumerate((keep_ref, got_ref)):
+            moved_ref[where_ref[0] ^ core] = ref[0]
+        for k, ref in enumerate(relayed, 1):
+            for core in range(2):
+                moved_ref[where_ref[0] ^ (2 * k) ^ core] = ref[core]
     groups, _, rows, width = moved_ref.shape
     pairs = groups * rows // 2
     both = 2 * width
@@ -122,12 +171,12 @@
         gfloat = gout.astype(F32)
         sum_br += jnp.sum(gfloat, axis=0, keepdims=True)
         sum_gate += jnp.sum(gfloat * joined_s[here, :], axis=0, keepdims=True)
-        ghidden = lax.dot_general(gout, wr_ref[...], (((1,), (1,)), ((), ())), preferred_element_type=F32)
+        ghidden = jnp.dot(gout, wrt_ref[...], preferred_element_type=F32)
         gpre = ghidden * slope_s[here, :]
         sum_be += jnp.sum(gpre, axis=0, keepdims=True)
         gpre = gpre.astype(BF16)
         gpre_s[here, :] = gpre
-        gnormed = lax.dot_general(gpre, we_ref[...], (((1,), (1,)), ((), ())), preferred_element_type=F32)
+        gnormed = jnp.dot(gpre, wet_ref[...], preferred_element_type=F32)
         normed = normed_s[here, :]
         inner = gnormed - jnp.mean(gnormed, axis=-1, keepdims=True)
         inner = inner - normed * jnp.mean(gnormed * normed, axis=-1, keepdims=True)
@@ -143,23 +192,29 @@
     acc_r[...] = lax.dot_general(hid_s[...], gout_s[...], rows_t, preferred_element_type=F32)
 
     me_ctx, me_rep = where_ref[0], where_ref[1]
-    slabs = slabs_of(order_a, None, me_ctx, me_rep)
-    half = len(slabs) // 2
-    size = acc_e.shape[0] * acc_e.shape[1] // (both * len(slabs))
-    for q, (shard, side) in enumerate(slabs):
-        target, at = (keep_a, q) if q < half else (send_a, q - half)
-        row = pl.multiple_of(shard * size, size)
-        lane = pl.multiple_of(side * both, both)
-        target[at * size : (at + 1) * size, :] = acc_e[pl.ds(row, size), pl.ds(lane, both)].astype(BF16)
-    slabs = slabs_of(order_b, None, me_ctx, me_rep)
-    for q, (shard, side) in enumerate(slabs):
-        target, at = (keep_b, q) if q < half else (send_b, q - half)
-        row = pl.multiple_of((shard * 2 + side) * size, size)
-        target[at * size : (at + 1) * size, :] = acc_r[pl.ds(row, size), :].astype(BF16)
     small = jnp.concatenate(
         [sum_be[:, :both], sum_be[:, both:], sum_br, sum_gate * sigma * (1.0 - sigma)], axis=0
     )
-    write_extra((send_a, keep_a), small)
+    for i, (order, parts, extra) in enumerate(chains):
+        send, keep = messages[2 * i], messages[2 * i + 1]
+        slabs = slabs_of(order, me_ctx, me_rep)
+        half = len(slabs) // 2
+        size = acc_r.shape[0] // len(slabs)
+        for q, (shard, side) in enumerate(slabs):
+            target = keep if q < half else send
+            at = q % half * sum(count for _, _, count in parts)
+            for name, start, count in parts:
+                if name == "e":
+                    row = pl.multiple_of(shard * size + start, math.gcd(size, start))
+                    lane = pl.multiple_of(side * both, both)
+                    value = acc_e[pl.ds(row, count), pl.ds(lane, both)]
+                else:
+                    row = pl.multiple_of((shard * 2 + side) * size + start, math.gcd(size, start))
+                    value = acc_r[pl.ds(row, count), :]
+                target[at : at + count, :] = value.astype(BF16)
+                at += count
+        if extra:
+            write_extra((send, keep), small)
 
 
 def halve_kernel(extra, keep_ref, recv_ref, send_out, keep_out):
@@ -171,49 +226,69 @@
         write_extra((send_out, keep_out), read_extra(keep_ref, 4) + read_extra(recv_ref, 4))
 
 
-def add_kernel(extra, keep_ref, recv_ref, out_ref):
+def add_kernel(extra, keep_ref, recv_ref, out_ref, *bare_ref):
     size = keep_ref.shape[0] - extra
-    out_ref[:size, :] = (keep_ref[:size, :].astype(F32) + recv_ref[:size, :].astype(F32)).astype(BF16)
+    total = (keep_ref[:size, :].astype(F32) + recv_ref[:size, :].astype(F32)).astype(BF16)
+    for ref in (out_ref, *bare_ref):
+        ref[:size, :] = total
     if extra:
         write_extra((out_ref,), read_extra(keep_ref, 4) + read_extra(recv_ref, 4))
 
 
-def final_kernel(factor, where_ref, own_a, other_a, own_b, other_b, out_e, out_be, out_r, out_br, out_gate):
+def final_kernel(factor, chains, where_ref, *refs):
+    owns, others, outs = refs[: len(chains)], refs[len(chains) : 2 * len(chains)], refs[2 * len(chains) :]
+    out_e, out_be, out_r, out_br, out_gate = outs
     side = where_ref[1] & 1
-    size, lanes = own_b.shape
-    rows = pl.multiple_of(side * size, size)
-    rest = pl.multiple_of((1 - side) * size, size)
-    out_r[pl.ds(rows, size), :] = own_b[...].astype(F32) * factor
-    out_r[pl.ds(rest, size), :] = other_b[...].astype(F32) * factor
-    here = pl.multiple_of(side * lanes, lanes)
-    there = pl.multiple_of((1 - side) * lanes, lanes)
-    out_e[:, pl.ds(here, lanes)] = own_a[:size, :].astype(F32) * factor
-    out_e[:, pl.ds(there, lanes)] = other_a[...].astype(F32) * factor
-    small = read_extra(own_a, 4) * factor
-    out_be[:, :lanes] = small[0:1]
-    out_be[:, lanes:] = small[1:2]
-    out_br[...] = small[2:3]
-    out_gate[...] = small[3:4]
+    lanes = out_r.shape[1]
+    size = out_r.shape[0] // 2
+    for own, other, (_, parts, extra) in zip(owns, others, chains):
+        for source, half in ((own, side), (other, 1 - side)):
+            at = 0
+            for name, start, count in parts:
+                value = source[at : at + count, :].astype(F32) * factor
+                at += count
+                if name == "e":
+                    out_e[start : start + count, pl.ds(pl.multiple_of(half * lanes, lanes), lanes)] = value
+                else:
+                    row = pl.multiple_of(half * size + start, math.gcd(size, start))
+                    out_r[pl.ds(row, count), :] = value
+        if extra:
+            small = read_extra(own, 4) * factor
+            out_be[:, :lanes] = small[0:1]
+            out_be[:, lanes:] = small[1:2]
+            out_br[...] = small[2:3]
+            out_gate[...] = small[3:4]
 
 
 VMEM = pl.BlockSpec(memory_space=pltpu.VMEM)
 SMEM = pl.BlockSpec(memory_space=pltpu.SMEM)
-
-
-def call(kernel, name, shapes, args, scratch=(), scalars=0):
+HBM = pl.BlockSpec(memory_space=pltpu.HBM)
+
+
+def call(kernel, name, shapes, args, scratch=(), scalars=0, flops=0, kind=VMEM, limit=32 * 2**10):
+    size = sum(math.prod(a.shape) * a.dtype.itemsize for a in [*args, *shapes])
     return pl.pallas_call(
         kernel,
         name=name,
         out_shape=shapes,
-        in_specs=[SMEM] * scalars + [VMEM] * (len(args) - scalars),
+        in_specs=[SMEM] * scalars + [kind] * (len(args) - scalars),
         out_specs=[VMEM] * len(shapes),
         scratch_shapes=scratch,
-        compiler_params=pltpu.CompilerParams(vmem_limit_bytes=48 * 2**20),
+        cost_estimate=pl.CostEstimate(flops=flops, bytes_accessed=size, transcendentals=0),
+        compiler_params=pltpu.CompilerParams(vmem_limit_bytes=limit * 2**10),
     )(*args)
 
 
 def rows_of(count, lanes):
     return jax.ShapeDtypeStruct((count, lanes), BF16)
+
+
+def add(extra, keep, got, bare):
+    shapes = [rows_of(*keep.shape)]
+    if bare and extra:
+        shapes.append(rows_of(keep.shape[0] - extra, keep.shape[1]))
+    outs = call(functools.partial(add_kernel, extra), "add", shapes, (keep, got))
+    return outs[0], outs[-1]
 
 
 def swap(value, axis, bit):
@@ -232,29 +307,59 @@
 
     ctx_bits = [("ctx", 2**i) for i in range(count)]
     rep_bits = [("rep", 2**i) for i in range(reps.bit_length() - 1)]
-    order_a = ctx_bits + rep_bits[:1]
-    order_b = ctx_bits[:1] + ctx_bits[2:] + rep_bits[:1] + ctx_bits[1:2]
+    size = both // devs
+    later = ctx_bits[1:] + rep_bits[:1]
+    if size % 64 == 0:
+        cut = size * 3 // 4
+        shares = [[("e", 0, cut)], [("r", 0, cut)], [("e", cut, size - cut), ("r", cut, size - cut)]]
+    else:
+        shares = [[("e", 0, size)], [("r", 0, size)]]
+    chains = [
+        (ctx_bits[:1] + later[i:] + later[:i], share, EXTRA * (i + 1 == len(shares))) for i, share in enumerate(shares)
+    ]
     where = jnp.stack([lax.axis_index("ctx"), lax.axis_index("rep")]).astype(jnp.int32)
 
-    packed = jnp.stack([inputs.reshape(devs, slice_rows, width), cotangent.reshape(devs, slice_rows, width)], axis=1)
-    moved = lax.all_to_all(packed, "ctx", split_axis=0, concat_axis=0, tiled=True)
-    moved = moved.reshape(groups, inner, 2, slice_rows, width).swapaxes(1, 2)
-    moved = moved.reshape(groups, 2, inner * slice_rows, width)
+    like = jax.ShapeDtypeStruct
+    state = like((groups, 2, inner * slice_rows, width), BF16)
+    if devs == 8:
+        part = like((devs // 2, 2, slice_rows, width), BF16)
+        send, keep = call(
+            pack_kernel, "pack", [part] * 2,
+            (where, inputs.reshape(rows, width), cotangent.reshape(rows, width)),
+            [pltpu.VMEM((rows, width), BF16)] * 2 + [pltpu.SemaphoreType.DMA((2,))], scalars=1, kind=HBM, limit=54912,
+        )
+        got = swap(send, "ctx", 1)
+        relay = call(relay_kernel, "relay", [like((2,) + part.shape[1:], BF16)] * (devs // 2 - 1), (keep, got))
+        arrived = [None] * len(relay)
+        for k in reversed(range(len(relay))):
+            arrived[k] = swap(relay[k], "ctx", 2 * (k + 1))
+        arrived = [keep, got] + arrived
+        moved_scratch = [pltpu.VMEM(state.shape, BF16)]
+    else:
+        packed = jnp.stack([a.reshape(devs, slice_rows, width) for a in (inputs, cotangent)], axis=1)
+        moved = lax.all_to_all(packed, "ctx", split_axis=0, concat_axis=0, tiled=True)
+        moved = moved.reshape(groups, inner, 2, slice_rows, width).swapaxes(1, 2)
+        arrived = [moved.reshape(state.shape)]
+        moved_scratch = []
+    params = call(
+        prep_kernel, "prep",
+        [like((both, hid), BF16), like((hid, both), BF16), like((hid, both), BF16), like((both, hid), BF16)]
+        + [like((1, hid), F32), like((1, both), F32), like((1, both), F32)],
+        (w_expand, b_expand[None], w_reduce, b_reduce[None], gate_logit[None]),
+        [pltpu.SemaphoreType.DMA((5,))], kind=HBM, limit=50432,
+    )
 
     pairs = rows // 2
     total = SECTIONS * pairs
-    half = both * hid // both // 2
-    back, send_a, keep_a, send_b, keep_b = call(
-        functools.partial(main_kernel, blocks, order_a, order_b),
+    slabs = 2 ** len(chains[0][0])
+    messages = [
+        rows_of(slabs // 2 * sum(n for _, _, n in parts) + extra, both) for _, parts, extra in chains for _ in range(2)
+    ]
+    back, *sums = call(
+        functools.partial(main_kernel, blocks, chains, len(arrived)),
         "sections",
-        [
-            jax.ShapeDtypeStruct(moved.shape, BF16),
-            rows_of(half + EXTRA, both),
-            rows_of(half + EXTRA, both),
-            rows_of(half, both),
-            rows_of(half, both),
-        ],
-        (where, moved, w_expand, b_expand[None], w_reduce, b_reduce[None], gate_logit[None]),
+        [state] + messages,
+        (where, *arrived, *params),
         [
             pltpu.VMEM((total, both), F32),
             pltpu.VMEM((total, both), BF16),
@@ -266,8 +371,10 @@
             pltpu.VMEM((total, both), F32),
             pltpu.VMEM((both, hid), F32),
             pltpu.VMEM((hid, both), F32),
-        ],
+        ]
+        + moved_scratch,
         scalars=1,
+        flops=12 * total * both * hid,
     )
 
     back = back.reshape(groups, 2, inner, slice_rows, width).swapaxes(1, 2).reshape(devs, 2, slice_rows, width)
@@ -275,27 +382,25 @@
     outputs = home[:, 0].reshape(inputs.shape)
     grad_inputs = home[:, 1].reshape(inputs.shape)
 
-    def halve(send, keep, order, extra):
-        for step, (axis, bit) in enumerate(order):
-            received = swap(send, axis, bit)
-            if step + 1 == len(order):
-                return call(functools.partial(add_kernel, extra), "add", [rows_of(*keep.shape)], (keep, received))[0]
-            size = (keep.shape[0] - extra) // 2 + extra
-            send, keep = call(
-                functools.partial(halve_kernel, extra), "halve", [rows_of(size, both)] * 2, (keep, received)
-            )
-
-    own_a = halve(send_a, keep_a, order_a, EXTRA)
-    own_b = halve(send_b, keep_b, order_b, 0)
-    for axis, bit in rep_bits[1:]:
-        got_a, got_b = swap(own_a, axis, bit), swap(own_b, axis, bit)
-        own_a = call(functools.partial(add_kernel, EXTRA), "add", [rows_of(*own_a.shape)], (own_a, got_a))[0]
-        own_b = call(functools.partial(add_kernel, 0), "add", [rows_of(*own_b.shape)], (own_b, got_b))[0]
-    size = own_b.shape[0]
-    other_a, other_b = swap(own_a[:size], "rep", 1), swap(own_b, "rep", 1)
+    states = [(sums[2 * i], sums[2 * i + 1]) for i in range(len(chains))]
+    steps = len(chains[0][0])
+    for step in range(steps):
+        got = [swap(send, *order[step]) for (send, _), (order, _, _) in zip(states, chains)]
+        for i, (_, _, extra) in enumerate(chains):
+            keep = states[i][1]
+            if step + 1 < steps:
+                count = (keep.shape[0] - extra) // 2 + extra
+                states[i] = call(functools.partial(halve_kernel, extra), "halve", [rows_of(count, both)] * 2, (keep, got[i]))
+            else:
+                states[i] = add(extra, keep, got[i], len(rep_bits) == 1)
+    for place, (axis, bit) in enumerate(rep_bits[1:]):
+        got = [swap(own, axis, bit) for own, _ in states]
+        for i, (_, _, extra) in enumerate(chains):
+            states[i] = add(extra, states[i][0], got[i], place + 2 == len(rep_bits))
+    others = [swap(bare, "rep", 1) for _, bare in states]
     factor = 1.0 / math.sqrt(reps * devs * rows)
     grad_e, grad_be, grad_r, grad_br, grad_gate = call(
-        functools.partial(final_kernel, factor),
+        functools.partial(final_kernel, factor, chains),
         "final",
         [
             jax.ShapeDtypeStruct((both // devs, hid), F32),
@@ -304,7 +409,7 @@
             jax.ShapeDtypeStruct((1, both), F32),
             jax.ShapeDtypeStruct((1, both), F32),
         ],
-        (where, own_a, other_a, own_b, other_b),
+        (where, *[own for own, _ in states], *others),
         scalars=1,
     )
     return outputs, grad_inputs, grad_e, grad_be[0], grad_r, grad_br[0], grad_gate[0]

time: 63.3 us -> 57.9 us (0.915)
  waiting for transfers between devices: 24 us -> 14.8 us
  starting transfers between devices: 22.4 us -> 26.8 us
  Pallas kernels: 11.3 us -> 13.8 us
  other arithmetic: 1.86 us -> 0.08 us
  local copies, waits for them, and re-layouts: 2.63 us -> 1.4 us
    ppermute x12 -> x22, starting transfers between devices: 13.8 us -> 23.1 us  [swap(): lax.ppermute(value, axis, [(i, i ^ bit) for i in range(lax.axis_size(axis...]
    all_to_all x1 -> x0, waiting for transfers between devices: 6.84 us -> none  [body(): lax.all_to_all(packed, 'ctx', split_axis=0, concat_axis=0, tiled=True)]
    all_to_all x1 -> x0, starting transfers between devices: 5.17 us -> none  [body(): lax.all_to_all(packed, 'ctx', split_axis=0, concat_axis=0, tiled=True)]
    pallas_call x12 -> x20, Pallas kernels: 11.3 us -> 13.8 us  [call(): pl.pallas_call(kernel, name=name, out_shape=shapes, in_specs=[SMEM] * sca...]
    ppermute x12 -> x22, waiting for transfers between devices: 17.2 us -> 14.8 us  [swap(): lax.ppermute(value, axis, [(i, i ^ bit) for i in range(lax.axis_size(axis...]
    another operation x1 -> x0, other arithmetic: 1.79 us -> none  [body(): jnp.stack([inputs.reshape(devs, slice_rows, width), cotangent.reshape(dev...]
    unnamed x10 -> x6, local copies, waits for them, and re-layouts: 1.91 us -> 0.69 us
  transfers between devices with their start and end apart: 14 -> 23, of which waited for: 7 -> 12; matrix products, arithmetic and copies ran while one was open for 1% -> 1% of each run, Pallas kernels for 1% -> 4%
where the time goes in v2:
time: 57.9 us; the launch traced here: 57.6 us
  starting transfers between devices  26.8 us (46%)
  waiting for transfers between devices  14.8 us (26%)
  Pallas kernels  13.8 us (24%)
  local copies, waits for them, and re-layouts  1.4 us (2%)
  between operations  0.75 us (1%)
    ppermute x22, starting transfers between devices, swap(): lax.ppermute(value, axis, [(i, i ^ bit) for i in range(lax.axis_size(axis...  23.1 us
    ppermute x22, waiting for transfers between devices, swap(): lax.ppermute(value, axis, [(i, i ^ bit) for i in range(lax.axis_size(axis...  14.8 us
    pallas_call x20, Pallas kernels, call(): pl.pallas_call(kernel, name=name, out_shape=shapes, in_specs=[SMEM] * sca...  13.8 us
    all_to_all x1, starting transfers between devices, body(): home = lax.all_to_all(back, 'ctx', split_axis=0, concat_axis=0, tiled=True)  3.72 us
  transfers between devices with their start and end apart: 23, of which 12 were waited for; matrix products, arithmetic and copies ran while one was open for 1% of the time, Pallas kernels for 4%

profile of v2, /device:TPU:0, one launch (start us, length us, event | category | flops | bytes accessed | tf_op | source)
XLA Modules:
  0.0 57.6 jit_solution(9858803930978084373)
XLA Ops:
  0.7 1.5 %pack.1 = (bf16[4,2,32,256]{3,2,1,0:T(8,128)(2,1)S(1)}, bf16[4,2,32,256]{3,2,1,0:T(8,128)(2,1)S(1)}) custom-call(s32[2]{0:T(128)S(1)} %pad_add_fusion.where_ref, bf16[256,256]{1,0:T(8,128)(2,1)} %bitcast.15, bf16[256,256]{1,0:T(8,128)(2,1)} %bitcast.16), custom_call_target="tpu_custom_call" | custom-call | bytes 524296 | tf_op jit(solution)/shard_map/pack/pallas_call | solution.py:270
  2.8 1.0 %collective-permute-done.got_ref.refs_1_ = bf16[4,2,32,256]{3,2,1,0:T(8,128)(2,1)S(1)} collective-permute-done((bf16[4,2,32,256]{3,2,1,0:T(8,128)(2,1)S(1)}, bf16[4,2,32,256]{3,2,1,0:T(8,128)(2,1)S(1)}, u32[]{:S(2)}, u32[]{:S(2)}) %collective-permute-start) | collective-permute-done | bytes 131104 | tf_op jit(solution)/shard_map/ppermute | solution.py:295
  3.8 2.9 %collective-permute-start.1 = (bf16[2,2,32,256]{3,2,1,0:T(8,128)(2,1)S(1)}, bf16[2,2,32,256]{3,2,1,0:T(8,128)(2,1)S(1)}, u32[]{:S(2)}, u32[]{:S(2)}) collective-permute-start(bf16[2,2,32,256]{3,2,1,0:T(8,128)(2,1)S(1)} %get-tuple-element.53), channel_id=1, source_target_pairs={{0,8},{4,12},{8,0},{12,4},{16,24},{20,28},{24,16},{28,20},{1,9},{5... | collective-permute-start | bytes 196616 | tf_op jit(solution)/shard_map/ppermute | solution.py:295
  6.7 1.5 %collective-permute-start.2 = (bf16[2,2,32,256]{3,2,1,0:T(8,128)(2,1)S(1)}, bf16[2,2,32,256]{3,2,1,0:T(8,128)(2,1)S(1)}, u32[]{:S(2)}, u32[]{:S(2)}) collective-permute-start(bf16[2,2,32,256]{3,2,1,0:T(8,128)(2,1)S(1)} %get-tuple-element.54), channel_id=1, source_target_pairs={{0,16},{4,20},{8,24},{12,28},{16,0},{20,4},{24,8},{28,12},{1,17},{... | collective-permute-start | bytes 196616 | tf_op jit(solution)/shard_map/ppermute | solution.py:295
  8.3 0.7 %copy-done.1 = f32[512]{0:T(512)S(1)} copy-done((f32[512]{0:T(512)S(1)}, f32[512]{0:T(512)}, u32[]{:S(2)}) %copy-start.1) | copy-done | bytes 2072
  8.9 1.9 %prep.1 = (bf16[512,1024]{1,0:T(8,128)(2,1)S(1)}, bf16[1024,512]{1,0:T(8,128)(2,1)S(1)}, bf16[1024,512]{1,0:T(8,128)(2,1)S(1)}, bf16[512,1024]{1,0:T(8,128)(2,1)...) custom-call(bf16[512,1024]{1,0:T(8,128)(2,1)} %we_ref.1, f32[1,1024]{1,0:T(1,128)S(1)} %bitcast.12, ...), custom_call_target="tpu_custom_call" | custom-call | bytes 6307840 | tf_op jit(solution)/shard_map/prep/pallas_call | solution.py:270
  11.0 2.4 %collective-permute-done.3.refs_4_ = bf16[2,2,32,256]{3,2,1,0:T(8,128)(2,1)S(1)} collective-permute-done((bf16[2,2,32,256]{3,2,1,0:T(8,128)(2,1)S(1)}, bf16[2,2,32,256]{3,2,1,0:T(8,128)(2,1)S(1)}, u32[]{:S(2)}, u32[]{:S(2)}) %collective-permute-start.3) | collective-permute-done | bytes 65568 | tf_op jit(solution)/shard_map/ppermute | solution.py:295
  13.4 8.4 %sections.1 = (bf16[8,2,32,256]{3,2,1,0:T(8,128)(2,1)}, bf16[384,512]{1,0:T(8,128)(2,1)S(1)}, bf16[384,512]{1,0:T(8,128)(2,1)S(1)}, bf16[384,512]{1,0:T(8,128)(2...) custom-call(s32[2]{0:T(128)S(1)} %pad_add_fusion.where_ref, ...), custom_call_target="tpu_custom_call" | custom-call | flops 3221225472 | bytes 7053320 | tf_op jit(solution)/shard_map/sections/pallas_call | solution.py:270
  22.3 1.2 %collective-permute-done.4.recv_ref = bf16[384,512]{1,0:T(8,128)(2,1)S(1)} collective-permute-done((bf16[384,512]{1,0:T(8,128)(2,1)S(1)}, bf16[384,512]{1,0:T(8,128)(2,1)S(1)}, u32[]{:S(2)}, u32[]{:S(2)}) %collective-permute-start.4) | collective-permute-done | bytes 393248 | tf_op jit(solution)/shard_map/ppermute | solution.py:295
  23.6 0.6 %collective-permute-start.5 = (bf16[192,512]{1,0:T(8,128)(2,1)S(1)}, bf16[192,512]{1,0:T(8,128)(2,1)S(1)}, u32[]{:S(2)}, u32[]{:S(2)}) collective-permute-start(bf16[192,512]{1,0:T(8,128)(2,1)S(1)} %get-tuple-element.67), channel_id=1, source_target_pairs={{0,8},{4,12},{8,0},{12,4},{16,24},{20,28},{24,16},{28,20},{1,9},{5... | collective-permute-start | bytes 589832 | tf_op jit(solution)/shard_map/ppermute | solution.py:295
  24.3 0.5 collective-permute-start.10
  24.9 1.7 %collective-permute-start.15 = (bf16[144,512]{1,0:T(8,128)(2,1)S(1)}, bf16[144,512]{1,0:T(8,128)(2,1)S(1)}, u32[]{:S(2)}, u32[]{:S(2)}) collective-permute-start(bf16[144,512]{1,0:T(8,128)(2,1)S(1)} %get-tuple-element.83), channel_id=1, source_target_pairs={{0,1},{1,0},{2,3},{3,2},{4,5},{5,4},{6,7},{7,6},{8,9},{9,8},{10,11... | collective-permute-start | bytes 442376 | tf_op jit(solution)/shard_map/ppermute | solution.py:295
  26.6 3.7 %all-to-all-start = ((bf16[8,2,32,256]{3,2,1,0:T(8,128)(2,1)}), bf16[8,2,32,256]{3,2,1,0:T(8,128)(2,1)S(1)}, u32[]{:S(2)}, u32[]{:S(2)}) async-start(bf16[8,2,32,256]{3,2,1,0:T(8,128)(2,1)} %get-tuple-element.63), calls=%async_computation | async-start | bytes 524288 | tf_op jit(solution)/shard_map/all_to_all | solution.py:381
  30.7 1.8 %collective-permute-start.6 = (bf16[96,512]{1,0:T(8,128)(2,1)S(1)}, bf16[96,512]{1,0:T(8,128)(2,1)S(1)}, u32[]{:S(2)}, u32[]{:S(2)}) collective-permute-start(bf16[96,512]{1,0:T(8,128)(2,1)S(1)} %get-tuple-element.69), channel_id=1, source_target_pairs={{0,16},{4,20},{8,24},{12,28},{16,0},{20,4},{24,8},{28,12},{1,17},{... | collective-permute-start | bytes 294920 | tf_op jit(solution)/shard_map/ppermute | solution.py:295
  32.5 0.5 collective-permute-start.11
  33.1 1.5 %collective-permute-start.16 = (bf16[80,512]{1,0:T(8,128)(2,1)S(1)}, bf16[80,512]{1,0:T(8,128)(2,1)S(1)}, u32[]{:S(2)}, u32[]{:S(2)}) collective-permute-start(bf16[80,512]{1,0:T(8,128)(2,1)S(1)} %get-tuple-element.85), channel_id=1, source_target_pairs={{0,8},{4,12},{8,0},{12,4},{16,24},{20,28},{24,16},{28,20},{1,9},{5... | collective-permute-start | bytes 245768 | tf_op jit(solution)/shard_map/ppermute | solution.py:295
  34.6 3.5 %collective-permute-done.16.recv_ref = bf16[80,512]{1,0:T(8,128)(2,1)S(1)} collective-permute-done((bf16[80,512]{1,0:T(8,128)(2,1)S(1)}, bf16[80,512]{1,0:T(8,128)(2,1)S(1)}, u32[]{:S(2)}, u32[]{:S(2)}) %collective-permute-start.16) | collective-permute-done | bytes 81952 | tf_op jit(solution)/shard_map/ppermute | solution.py:295
  38.1 1.5 %collective-permute-start.17 = (bf16[48,512]{1,0:T(8,128)(2,1)S(1)}, bf16[48,512]{1,0:T(8,128)(2,1)S(1)}, u32[]{:S(2)}, u32[]{:S(2)}) collective-permute-start(bf16[48,512]{1,0:T(8,128)(2,1)S(1)} %get-tuple-element.87), channel_id=1, source_target_pairs={{0,16},{4,20},{8,24},{12,28},{16,0},{20,4},{24,8},{28,12},{1,17},{... | collective-permute-start | bytes 147464 | tf_op jit(solution)/shard_map/ppermute | solution.py:295
  39.7 0.5 collective-permute-start.7
  40.2 1.2 %collective-permute-start.12 = (bf16[48,512]{1,0:T(8,128)(2,1)S(1)}, bf16[48,512]{1,0:T(8,128)(2,1)S(1)}, u32[]{:S(2)}, u32[]{:S(2)}) collective-permute-start(bf16[48,512]{1,0:T(8,128)(2,1)S(1)} %get-tuple-element.79), channel_id=1, source_target_pairs={{0,8},{4,12},{8,0},{12,4},{16,24},{20,28},{24,16},{28,20},{1,9},{5... | collective-permute-start | bytes 147464 | tf_op jit(solution)/shard_map/ppermute | solution.py:295
  41.5 0.8 %collective-permute-done.17.recv_ref = bf16[48,512]{1,0:T(8,128)(2,1)S(1)} collective-permute-done((bf16[48,512]{1,0:T(8,128)(2,1)S(1)}, bf16[48,512]{1,0:T(8,128)(2,1)S(1)}, u32[]{:S(2)}, u32[]{:S(2)}) %collective-permute-start.17) | collective-permute-done | bytes 49184 | tf_op jit(solution)/shard_map/ppermute | solution.py:295
  42.3 2.7 %collective-permute-start.18 = (bf16[48,512]{1,0:T(8,128)(2,1)S(1)}, bf16[48,512]{1,0:T(8,128)(2,1)S(1)}, u32[]{:S(2)}, u32[]{:S(2)}) collective-permute-start(bf16[48,512]{1,0:T(8,128)(2,1)S(1)} %add.12.keep_ref), channel_id=1, source_target_pairs={{0,2},{1,3},{2,0},{3,1},{4,6},{5,7},{6,4},{7,5},{8,10},{9,11},{10,... | collective-permute-start | bytes 147464 | tf_op jit(solution)/shard_map/ppermute | solution.py:295
  45.0 1.5 %collective-permute-start.8 = (bf16[48,512]{1,0:T(8,128)(2,1)S(1)}, bf16[48,512]{1,0:T(8,128)(2,1)S(1)}, u32[]{:S(2)}, u32[]{:S(2)}) collective-permute-start(bf16[48,512]{1,0:T(8,128)(2,1)S(1)} %add.8.keep_ref), channel_id=1, source_target_pairs={{0,2},{1,3},{2,0},{3,1},{4,6},{5,7},{6,4},{7,5},{8,10},{9,11},{10,... | collective-permute-start | bytes 147464 | tf_op jit(solution)/shard_map/ppermute | solution.py:295
  46.5 1.5 %collective-permute-start.13 = (bf16[48,512]{1,0:T(8,128)(2,1)S(1)}, bf16[48,512]{1,0:T(8,128)(2,1)S(1)}, u32[]{:S(2)}, u32[]{:S(2)}) collective-permute-start(bf16[48,512]{1,0:T(8,128)(2,1)S(1)} %add.10.keep_ref), channel_id=1, source_target_pairs={{0,2},{1,3},{2,0},{3,1},{4,6},{5,7},{6,4},{7,5},{8,10},{9,11},{10,... | collective-permute-start | bytes 147464 | tf_op jit(solution)/shard_map/ppermute | solution.py:295
  48.1 1.5 %collective-permute-done.18.recv_ref = bf16[48,512]{1,0:T(8,128)(2,1)S(1)} collective-permute-done((bf16[48,512]{1,0:T(8,128)(2,1)S(1)}, bf16[48,512]{1,0:T(8,128)(2,1)S(1)}, u32[]{:S(2)}, u32[]{:S(2)}) %collective-permute-start.18) | collective-permute-done | bytes 49184 | tf_op jit(solution)/shard_map/ppermute | solution.py:295
  49.7 1.5 %collective-permute-done.8.recv_ref = bf16[48,512]{1,0:T(8,128)(2,1)S(1)} collective-permute-done((bf16[48,512]{1,0:T(8,128)(2,1)S(1)}, bf16[48,512]{1,0:T(8,128)(2,1)S(1)}, u32[]{:S(2)}, u32[]{:S(2)}) %collective-permute-start.8) | collective-permute-done | bytes 49184 | tf_op jit(solution)/shard_map/ppermute | solution.py:295
  51.1 0.6 %collective-permute-start.19 = (bf16[48,512]{1,0:T(8,128)(2,1)S(1)}, bf16[48,512]{1,0:T(8,128)(2,1)S(1)}, u32[]{:S(2)}, u32[]{:S(2)}) collective-permute-start(bf16[48,512]{1,0:T(8,128)(2,1)S(1)} %add.9.refs_0_), channel_id=1, source_target_pairs={{0,1},{1,0},{2,3},{3,2},{4,5},{5,4},{6,7},{7,6},{8,9},{9,8},{10,11... | collective-permute-start | bytes 147464 | tf_op jit(solution)/shard_map/ppermute | solution.py:295
  52.1 1.2 %collective-permute-start.20 = (bf16[48,512]{1,0:T(8,128)(2,1)S(1)}, bf16[48,512]{1,0:T(8,128)(2,1)S(1)}, u32[]{:S(2)}, u32[]{:S(2)}) collective-permute-start(bf16[48,512]{1,0:T(8,128)(2,1)S(1)} %add.11.refs_1_), channel_id=1, source_target_pairs={{0,1},{1,0},{2,3},{3,2},{4,5},{5,4},{6,7},{7,6},{8,9},{9,8},{10,11... | collective-permute-start | bytes 147464 | tf_op jit(solution)/shard_map/ppermute | solution.py:295
  53.3 0.7 %fusion = (bf16[8,1,32,256]{3,2,1,0:T(8,128)(2,1)}, bf16[8,1,32,256]{3,2,1,0:T(8,128)(2,1)}) fusion(bf16[8,2,32,256]{3,2,1,0:T(8,128)(2,1)S(1)} %all-to-all-done), kind=kLoop, calls=%fused_computation.1 | loop fusion | bytes 524288 | tf_op jit(solution)/shard_map/slice | solution.py:383
  54.0 1.3 %collective-permute-done.19.refs_3_ = bf16[48,512]{1,0:T(8,128)(2,1)S(1)} collective-permute-done((bf16[48,512]{1,0:T(8,128)(2,1)S(1)}, bf16[48,512]{1,0:T(8,128)(2,1)S(1)}, u32[]{:S(2)}, u32[]{:S(2)}) %collective-permute-start.19) | collective-permute-done | bytes 49184 | tf_op jit(solution)/shard_map/ppermute | solution.py:295
  55.3 0.9 %collective-permute-done.20.refs_4_ = bf16[48,512]{1,0:T(8,128)(2,1)S(1)} collective-permute-done((bf16[48,512]{1,0:T(8,128)(2,1)S(1)}, bf16[48,512]{1,0:T(8,128)(2,1)S(1)}, u32[]{:S(2)}, u32[]{:S(2)}) %collective-permute-start.20) | collective-permute-done | bytes 49184 | tf_op jit(solution)/shard_map/ppermute | solution.py:295
  56.2 1.4 %final.1 = (f32[64,1024]{1,0:T(8,128)}, f32[1,1024]{1,0:T(1,128)}, f32[128,512]{1,0:T(8,128)}, f32[1,512]{1,0:T(1,128)}, f32[1,512]{1,0:T(1,128)}) custom-call(s32[2]{0:T(128)S(1)} %pad_add_fusion.where_ref, bf16[48,512]{1,0:T(8,128)(2,1)S(1)} %add.9.refs_0_, bf16[48,512]{1,0:T(8,128)(2,1)S(1)} %add.11.refs_1_, ...), custom_call_target="tpu_custom_call" | custom-call | bytes 811016 | tf_op jit(solution)/shard_map/final/pallas_call | solution.py:270
  (42 shorter events, 2.5 us)
Async XLA Ops:
  2.3 1.5 %collective-permute-start = (bf16[4,2,32,256]{3,2,1,0:T(8,128)(2,1)S(1)}, bf16[4,2,32,256]{3,2,1,0:T(8,128)(2,1)S(1)}, u32[]{:S(2)}, u32[]{:S(2)}) collective-permute-start(bf16[4,2,32,256]{3,2,1,0:T(8,128)(2,1)S(1)} %get-tuple-element.52), channel_id=1, source_target_pairs={{0,4},{4,0},{8,12},{12,8},{16,20},{20,16},{24,28},{28,24},{1,5},{5... | collective-permute-start | bytes 393224 | tf_op jit(solution)/shard_map/ppermute | solution.py:295
  3.8 4.5 %copy-start.2 = (f32[512]{0:T(512)S(1)}, f32[512]{0:T(512)}, u32[]{:S(2)}) copy-start(f32[512]{0:T(512)} %param.12) | copy-start | bytes 6148
  3.8 7.1 %collective-permute-start.1 = (bf16[2,2,32,256]{3,2,1,0:T(8,128)(2,1)S(1)}, bf16[2,2,32,256]{3,2,1,0:T(8,128)(2,1)S(1)}, u32[]{:S(2)}, u32[]{:S(2)}) collective-permute-start(bf16[2,2,32,256]{3,2,1,0:T(8,128)(2,1)S(1)} %get-tuple-element.53), channel_id=1, source_target_pairs={{0,8},{4,12},{8,0},{12,4},{16,24},{20,28},{24,16},{28,20},{1,9},{5... | collective-permute-start | bytes 196616 | tf_op jit(solution)/shard_map/ppermute | solution.py:295
  6.7 1.6 %copy-start = (f32[1024]{0:T(1024)S(1)}, f32[1024]{0:T(1024)}, u32[]{:S(2)}) copy-start(f32[1024]{0:T(1024)} %param.9) | copy-start | bytes 12292
  6.7 4.3 %collective-permute-start.2 = (bf16[2,2,32,256]{3,2,1,0:T(8,128)(2,1)S(1)}, bf16[2,2,32,256]{3,2,1,0:T(8,128)(2,1)S(1)}, u32[]{:S(2)}, u32[]{:S(2)}) collective-permute-start(bf16[2,2,32,256]{3,2,1,0:T(8,128)(2,1)S(1)} %get-tuple-element.54), channel_id=1, source_target_pairs={{0,16},{4,20},{8,24},{12,28},{16,0},{20,4},{24,8},{28,12},{1,17},{... | collective-permute-start | bytes 196616 | tf_op jit(solution)/shard_map/ppermute | solution.py:295
  8.2 5.2 %collective-permute-start.3 = (bf16[2,2,32,256]{3,2,1,0:T(8,128)(2,1)S(1)}, bf16[2,2,32,256]{3,2,1,0:T(8,128)(2,1)S(1)}, u32[]{:S(2)}, u32[]{:S(2)}) collective-permute-start(bf16[2,2,32,256]{3,2,1,0:T(8,128)(2,1)S(1)} %get-tuple-element.55), channel_id=1, source_target_pairs={{0,24},{4,28},{8,16},{12,20},{16,8},{20,12},{24,0},{28,4},{1,25},{... | collective-permute-start | bytes 196616 | tf_op jit(solution)/shard_map/ppermute | solution.py:295
  8.3 0.7 %copy-start.1 = (f32[512]{0:T(512)S(1)}, f32[512]{0:T(512)}, u32[]{:S(2)}) copy-start(f32[512]{0:T(512)} %param.11) | copy-start | bytes 6148
  21.8 1.7 %collective-permute-start.4 = (bf16[384,512]{1,0:T(8,128)(2,1)S(1)}, bf16[384,512]{1,0:T(8,128)(2,1)S(1)}, u32[]{:S(2)}, u32[]{:S(2)}) collective-permute-start(bf16[384,512]{1,0:T(8,128)(2,1)S(1)} %get-tuple-element.65), channel_id=1, source_target_pairs={{0,4},{4,0},{8,12},{12,8},{16,20},{20,16},{24,28},{28,24},{1,5},{5... | collective-permute-start | bytes 1179656 | tf_op jit(solution)/shard_map/ppermute | solution.py:295
  21.8 2.4 %collective-permute-start.9 = (bf16[384,512]{1,0:T(8,128)(2,1)S(1)}, bf16[384,512]{1,0:T(8,128)(2,1)S(1)}, u32[]{:S(2)}, u32[]{:S(2)}) collective-permute-start(bf16[384,512]{1,0:T(8,128)(2,1)S(1)} %get-tuple-element.73), channel_id=1, source_target_pairs={{0,4},{4,0},{8,12},{12,8},{16,20},{20,16},{24,28},{28,24},{1,5},{5... | collective-permute-start | bytes 1179656 | tf_op jit(solution)/shard_map/ppermute | solution.py:295
  22.3 2.5 %collective-permute-start.14 = (bf16[272,512]{1,0:T(8,128)(2,1)S(1)}, bf16[272,512]{1,0:T(8,128)(2,1)S(1)}, u32[]{:S(2)}, u32[]{:S(2)}) collective-permute-start(bf16[272,512]{1,0:T(8,128)(2,1)S(1)} %get-tuple-element.81), channel_id=1, source_target_pairs={{0,4},{4,0},{8,12},{12,8},{16,20},{20,16},{24,28},{28,24},{1,5},{5... | collective-permute-start | bytes 835592 | tf_op jit(solution)/shard_map/ppermute | solution.py:295
  23.6 7.0 %collective-permute-start.5 = (bf16[192,512]{1,0:T(8,128)(2,1)S(1)}, bf16[192,512]{1,0:T(8,128)(2,1)S(1)}, u32[]{:S(2)}, u32[]{:S(2)}) collective-permute-start(bf16[192,512]{1,0:T(8,128)(2,1)S(1)} %get-tuple-element.67), channel_id=1, source_target_pairs={{0,8},{4,12},{8,0},{12,4},{16,24},{20,28},{24,16},{28,20},{1,9},{5... | collective-permute-start | bytes 589832 | tf_op jit(solution)/shard_map/ppermute | solution.py:295
  24.3 8.2 %collective-permute-start.10 = (bf16[192,512]{1,0:T(8,128)(2,1)S(1)}, bf16[192,512]{1,0:T(8,128)(2,1)S(1)}, u32[]{:S(2)}, u32[]{:S(2)}) collective-permute-start(bf16[192,512]{1,0:T(8,128)(2,1)S(1)} %get-tuple-element.75), channel_id=1, source_target_pairs={{0,16},{4,20},{8,24},{12,28},{16,0},{20,4},{24,8},{28,12},{1,17},{... | collective-permute-start | bytes 589832 | tf_op jit(solution)/shard_map/ppermute | solution.py:295
  24.9 8.1 %collective-permute-start.15 = (bf16[144,512]{1,0:T(8,128)(2,1)S(1)}, bf16[144,512]{1,0:T(8,128)(2,1)S(1)}, u32[]{:S(2)}, u32[]{:S(2)}) collective-permute-start(bf16[144,512]{1,0:T(8,128)(2,1)S(1)} %get-tuple-element.83), channel_id=1, source_target_pairs={{0,1},{1,0},{2,3},{3,2},{4,5},{5,4},{6,7},{7,6},{8,9},{9,8},{10,11... | collective-permute-start | bytes 442376 | tf_op jit(solution)/shard_map/ppermute | solution.py:295
  26.6 26.7 %all-to-all-start = ((bf16[8,2,32,256]{3,2,1,0:T(8,128)(2,1)}), bf16[8,2,32,256]{3,2,1,0:T(8,128)(2,1)S(1)}, u32[]{:S(2)}, u32[]{:S(2)}) async-start(bf16[8,2,32,256]{3,2,1,0:T(8,128)(2,1)} %get-tuple-element.63), calls=%async_computation | async-start | bytes 524288 | tf_op jit(solution)/shard_map/all_to_all | solution.py:381
  30.7 9.0 %collective-permute-start.6 = (bf16[96,512]{1,0:T(8,128)(2,1)S(1)}, bf16[96,512]{1,0:T(8,128)(2,1)S(1)}, u32[]{:S(2)}, u32[]{:S(2)}) collective-permute-start(bf16[96,512]{1,0:T(8,128)(2,1)S(1)} %get-tuple-element.69), channel_id=1, source_target_pairs={{0,16},{4,20},{8,24},{12,28},{16,0},{20,4},{24,8},{28,12},{1,17},{... | collective-permute-start | bytes 294920 | tf_op jit(solution)/shard_map/ppermute | solution.py:295
  32.5 7.7 %collective-permute-start.11 = (bf16[96,512]{1,0:T(8,128)(2,1)S(1)}, bf16[96,512]{1,0:T(8,128)(2,1)S(1)}, u32[]{:S(2)}, u32[]{:S(2)}) collective-permute-start(bf16[96,512]{1,0:T(8,128)(2,1)S(1)} %get-tuple-element.77), channel_id=1, source_target_pairs={{0,1},{1,0},{2,3},{3,2},{4,5},{5,4},{6,7},{7,6},{8,9},{9,8},{10,11... | collective-permute-start | bytes 294920 | tf_op jit(solution)/shard_map/ppermute | solution.py:295
  33.1 5.0 %collective-permute-start.16 = (bf16[80,512]{1,0:T(8,128)(2,1)S(1)}, bf16[80,512]{1,0:T(8,128)(2,1)S(1)}, u32[]{:S(2)}, u32[]{:S(2)}) collective-permute-start(bf16[80,512]{1,0:T(8,128)(2,1)S(1)} %get-tuple-element.85), channel_id=1, source_target_pairs={{0,8},{4,12},{8,0},{12,4},{16,24},{20,28},{24,16},{28,20},{1,9},{5... | collective-permute-start | bytes 245768 | tf_op jit(solution)/shard_map/ppermute | solution.py:295
  38.1 4.2 %collective-permute-start.17 = (bf16[48,512]{1,0:T(8,128)(2,1)S(1)}, bf16[48,512]{1,0:T(8,128)(2,1)S(1)}, u32[]{:S(2)}, u32[]{:S(2)}) collective-permute-start(bf16[48,512]{1,0:T(8,128)(2,1)S(1)} %get-tuple-element.87), channel_id=1, source_target_pairs={{0,16},{4,20},{8,24},{12,28},{16,0},{20,4},{24,8},{28,12},{1,17},{... | collective-permute-start | bytes 147464 | tf_op jit(solution)/shard_map/ppermute | solution.py:295
  39.7 5.3 %collective-permute-start.7 = (bf16[48,512]{1,0:T(8,128)(2,1)S(1)}, bf16[48,512]{1,0:T(8,128)(2,1)S(1)}, u32[]{:S(2)}, u32[]{:S(2)}) collective-permute-start(bf16[48,512]{1,0:T(8,128)(2,1)S(1)} %get-tuple-element.71), channel_id=1, source_target_pairs={{0,1},{1,0},{2,3},{3,2},{4,5},{5,4},{6,7},{7,6},{8,9},{9,8},{10,11... | collective-permute-start | bytes 147464 | tf_op jit(solution)/shard_map/ppermute | solution.py:295
  40.2 6.3 %collective-permute-start.12 = (bf16[48,512]{1,0:T(8,128)(2,1)S(1)}, bf16[48,512]{1,0:T(8,128)(2,1)S(1)}, u32[]{:S(2)}, u32[]{:S(2)}) collective-permute-start(bf16[48,512]{1,0:T(8,128)(2,1)S(1)} %get-tuple-element.79), channel_id=1, source_target_pairs={{0,8},{4,12},{8,0},{12,4},{16,24},{20,28},{24,16},{28,20},{1,9},{5... | collective-permute-start | bytes 147464 | tf_op jit(solution)/shard_map/ppermute | solution.py:295
  42.3 7.3 %collective-permute-start.18 = (bf16[48,512]{1,0:T(8,128)(2,1)S(1)}, bf16[48,512]{1,0:T(8,128)(2,1)S(1)}, u32[]{:S(2)}, u32[]{:S(2)}) collective-permute-start(bf16[48,512]{1,0:T(8,128)(2,1)S(1)} %add.12.keep_ref), channel_id=1, source_target_pairs={{0,2},{1,3},{2,0},{3,1},{4,6},{5,7},{6,4},{7,5},{8,10},{9,11},{10,... | collective-permute-start | bytes 147464 | tf_op jit(solution)/shard_map/ppermute | solution.py:295
  45.0 6.1 %collective-permute-start.8 = (bf16[48,512]{1,0:T(8,128)(2,1)S(1)}, bf16[48,512]{1,0:T(8,128)(2,1)S(1)}, u32[]{:S(2)}, u32[]{:S(2)}) collective-permute-start(bf16[48,512]{1,0:T(8,128)(2,1)S(1)} %add.8.keep_ref), channel_id=1, source_target_pairs={{0,2},{1,3},{2,0},{3,1},{4,6},{5,7},{6,4},{7,5},{8,10},{9,11},{10,... | collective-permute-start | bytes 147464 | tf_op jit(solution)/shard_map/ppermute | solution.py:295
  46.5 5.5 %collective-permute-start.13 = (bf16[48,512]{1,0:T(8,128)(2,1)S(1)}, bf16[48,512]{1,0:T(8,128)(2,1)S(1)}, u32[]{:S(2)}, u32[]{:S(2)}) collective-permute-start(bf16[48,512]{1,0:T(8,128)(2,1)S(1)} %add.10.keep_ref), channel_id=1, source_target_pairs={{0,2},{1,3},{2,0},{3,1},{4,6},{5,7},{6,4},{7,5},{8,10},{9,11},{10,... | collective-permute-start | bytes 147464 | tf_op jit(solution)/shard_map/ppermute | solution.py:295
  49.6 4.5 %collective-permute-start.21 = (bf16[32,512]{1,0:T(8,128)(2,1)S(1)}, bf16[32,512]{1,0:T(8,128)(2,1)S(1)}, u32[]{:S(2)}, u32[]{:S(2)}) collective-permute-start(bf16[32,512]{1,0:T(8,128)(2,1)S(1)} %get-tuple-element.89), channel_id=1, source_target_pairs={{0,1},{1,0},{2,3},{3,2},{4,5},{5,4},{6,7},{7,6},{8,9},{9,8},{10,11... | collective-permute-start | bytes 98312 | tf_op jit(solution)/shard_map/ppermute | solution.py:295
  51.1 4.2 %collective-permute-start.19 = (bf16[48,512]{1,0:T(8,128)(2,1)S(1)}, bf16[48,512]{1,0:T(8,128)(2,1)S(1)}, u32[]{:S(2)}, u32[]{:S(2)}) collective-permute-start(bf16[48,512]{1,0:T(8,128)(2,1)S(1)} %add.9.refs_0_), channel_id=1, source_target_pairs={{0,1},{1,0},{2,3},{3,2},{4,5},{5,4},{6,7},{7,6},{8,9},{9,8},{10,11... | collective-permute-start | bytes 147464 | tf_op jit(solution)/shard_map/ppermute | solution.py:295
  52.1 4.2 %collective-permute-start.20 = (bf16[48,512]{1,0:T(8,128)(2,1)S(1)}, bf16[48,512]{1,0:T(8,128)(2,1)S(1)}, u32[]{:S(2)}, u32[]{:S(2)}) collective-permute-start(bf16[48,512]{1,0:T(8,128)(2,1)S(1)} %add.11.refs_1_), channel_id=1, source_target_pairs={{0,1},{1,0},{2,3},{3,2},{4,5},{5,4},{6,7},{7,6},{8,9},{9,8},{10,11... | collective-permute-start | bytes 147464 | tf_op jit(solution)/shard_map/ppermute | solution.py:295

commit v3 on v2

--- a/solution.py
+++ b/solution.py
@@ -47,18 +47,20 @@
     return rows[:count] + rows[EXTRA // 2 : EXTRA // 2 + count]
 
 
-def slabs_of(order, me_ctx, me_rep):
-    count = 2 ** len(order)
+def slabs_of(orders, me_ctx, me_rep):
+    steps = len(orders[0])
     slabs = []
-    for q in range(count):
-        flip_ctx, flip_rep = 0, 0
-        for place, (axis, bit) in enumerate(order):
-            if q >> (len(order) - 1 - place) & 1:
-                if axis == "ctx":
-                    flip_ctx |= bit
-                else:
-                    flip_rep |= bit
-        slabs.append((me_ctx ^ flip_ctx, (me_rep & 1) ^ flip_rep))
+    for q in range(2**steps):
+        flips = []
+        for order in orders:
+            flip = {"ctx": 0, "rep": 0}
+            for place, (axis, bit) in enumerate(order):
+                if q >> (steps - 1 - place) & 1:
+                    flip[axis] |= bit
+            flips.append(flip)
+        odd = (me_ctx & 1) ^ (q >> (steps - 1))
+        ctx, rep = (flips[0][axis] + odd * (flips[1][axis] - flips[0][axis]) for axis in ("ctx", "rep"))
+        slabs.append((me_ctx ^ ctx, (me_rep & 1) ^ rep))
     return slabs
 
 
@@ -104,12 +106,13 @@
     ) = refs[:7]
     back_ref, messages, refs = refs[7], refs[8 : 8 + 2 * len(chains)], refs[8 + 2 * len(chains) :]
     (
-        normed_s, low_s, hid_s, slope_s, gpre_s, gout_s, rstd_s, joined_s, acc_e, acc_r, *moved_s,
+        normed_s, low_s, hid_s, slope_s, gpre_s, gout_s, rstd_s, joined_s, acc_e, acc_r, sems, *moved_s,
     ) = refs
+    state_s = moved_s[0]
     if pieces == 1:
         moved_ref = arrived[0]
     else:
-        moved_ref = moved_s[0]
+        moved_ref = state_s
         keep_ref, got_ref, *relayed = arrived
         for core, ref in enumerate((keep_ref, got_ref)):
             moved_ref[where_ref[0] ^ core] = ref[0]
@@ -135,7 +138,7 @@
             put(g | block, piece[:, width:])
 
     for s, block in enumerate(blocks):
-        source = moved_ref if s == 0 else back_ref
+        source = moved_ref if s == 0 else state_s
         joined = gather(lambda g: source[g, 0], block).astype(F32)
         centred = joined - jnp.mean(joined, axis=-1, keepdims=True)
         rstd = lax.rsqrt(jnp.mean(centred * centred, axis=-1, keepdims=True) + EPSILON)
@@ -155,17 +158,19 @@
         result = (sigma * joined + mixed + br_ref[...]).astype(BF16)
 
         def put(g, piece):
-            back_ref[g, 0] = piece
+            state_s[g, 0] = piece
 
         scatter(put, result, block)
 
+    copies = [pltpu.make_async_copy(state_s.at[:, i], back_ref.at[:, i], sems.at[i]) for i in range(2)]
+    copies[0].start()
     sum_be = jnp.zeros((1, we_ref.shape[1]), F32)
     sum_br = jnp.zeros((1, both), F32)
     sum_gate = jnp.zeros((1, both), F32)
     for s in reversed(range(len(blocks))):
         block = blocks[s]
         here = pl.ds(s * pairs, pairs)
-        source = moved_ref if s == len(blocks) - 1 else back_ref
+        source = moved_ref if s == len(blocks) - 1 else state_s
         gout = gather(lambda g: source[g, 1], block)
         gout_s[here, :] = gout
         gfloat = gout.astype(F32)
@@ -183,10 +188,11 @@
         gjoined = (sigma * gfloat + rstd_s[here, :] * inner).astype(BF16)
 
         def put(g, piece):
-            back_ref[g, 1] = piece
+            state_s[g, 1] = piece
 
         scatter(put, gjoined, block)
 
+    copies[1].start()
     rows_t = (((0,), (0,)), ((), ()))
     acc_e[...] = lax.dot_general(low_s[...], gpre_s[...], rows_t, preferred_element_type=F32)
     acc_r[...] = lax.dot_general(hid_s[...], gout_s[...], rows_t, preferred_element_type=F32)
@@ -195,9 +201,9 @@
     small = jnp.concatenate(
         [sum_be[:, :both], sum_be[:, both:], sum_br, sum_gate * sigma * (1.0 - sigma)], axis=0
     )
-    for i, (order, parts, extra) in enumerate(chains):
+    for i, (orders, parts, extra) in enumerate(chains):
         send, keep = messages[2 * i], messages[2 * i + 1]
-        slabs = slabs_of(order, me_ctx, me_rep)
+        slabs = slabs_of(orders, me_ctx, me_rep)
         half = len(slabs) // 2
         size = acc_r.shape[0] // len(slabs)
         for q, (shard, side) in enumerate(slabs):
@@ -215,9 +221,12 @@
                 at += count
         if extra:
             write_extra((send, keep), small)
-
-
-def halve_kernel(extra, keep_ref, recv_ref, send_out, keep_out):
+    for copy in copies:
+        copy.wait()
+
+
+def halve_kernel(extra, keep_ref, recv_ref, *refs):
+    send_out, keep_out = refs[-2:]
     half = (keep_ref.shape[0] - extra) // 2
     for out, start in ((keep_out, 0), (send_out, half)):
         span = slice(start, start + half)
@@ -265,14 +274,14 @@
 HBM = pl.BlockSpec(memory_space=pltpu.HBM)
 
 
-def call(kernel, name, shapes, args, scratch=(), scalars=0, flops=0, kind=VMEM, limit=32 * 2**10):
+def call(kernel, name, shapes, args, scratch=(), scalars=0, flops=0, kind=VMEM, limit=32 * 2**10, far=0):
     size = sum(math.prod(a.shape) * a.dtype.itemsize for a in [*args, *shapes])
     return pl.pallas_call(
         kernel,
         name=name,
         out_shape=shapes,
         in_specs=[SMEM] * scalars + [kind] * (len(args) - scalars),
-        out_specs=[VMEM] * len(shapes),
+        out_specs=[HBM] * far + [VMEM] * (len(shapes) - far),
         scratch_shapes=scratch,
         cost_estimate=pl.CostEstimate(flops=flops, bytes_accessed=size, transcendentals=0),
         compiler_params=pltpu.CompilerParams(vmem_limit_bytes=limit * 2**10),
@@ -293,6 +302,17 @@
 
 def swap(value, axis, bit):
     return lax.ppermute(value, axis, [(i, i ^ bit) for i in range(lax.axis_size(axis))])
+
+
+def swap_by_place(value, bits):
+    devs, reps = lax.axis_size("ctx"), lax.axis_size("rep")
+    pairs = []
+    for c in range(devs):
+        axis, bit = bits[c & 1]
+        for r in range(reps):
+            to = (c ^ bit, r) if axis == "ctx" else (c, r ^ bit)
+            pairs.append((c * reps + r, to[0] * reps + to[1]))
+    return lax.ppermute(value, ("ctx", "rep"), pairs)
 
 
 def body(inputs, w_expand, b_expand, w_reduce, b_reduce, gate_logit, cotangent):
@@ -310,12 +330,14 @@
     size = both // devs
     later = ctx_bits[1:] + rep_bits[:1]
     if size % 64 == 0:
-        cut = size * 3 // 4
-        shares = [[("e", 0, cut)], [("r", 0, cut)], [("e", cut, size - cut), ("r", cut, size - cut)]]
+        cut, most = size // 2, size * 3 // 4
+        shares = [[("e", 0, cut)], [("r", 0, most)], [("e", cut, size - cut), ("r", most, size - most)]]
     else:
         shares = [[("e", 0, size)], [("r", 0, size)]]
+    turns = [(0, 0), (1, 1), (2, 2)]
     chains = [
-        (ctx_bits[:1] + later[i:] + later[:i], share, EXTRA * (i + 1 == len(shares))) for i, share in enumerate(shares)
+        (tuple(ctx_bits[:1] + later[turn:] + later[:turn] for turn in pair), share, extra)
+        for pair, share, extra in zip(turns, shares, (EXTRA, 0, 0))
     ]
     where = jnp.stack([lax.axis_index("ctx"), lax.axis_index("rep")]).astype(jnp.int32)
 
@@ -340,7 +362,7 @@
         moved = lax.all_to_all(packed, "ctx", split_axis=0, concat_axis=0, tiled=True)
         moved = moved.reshape(groups, inner, 2, slice_rows, width).swapaxes(1, 2)
         arrived = [moved.reshape(state.shape)]
-        moved_scratch = []
+        moved_scratch = [pltpu.VMEM(state.shape, BF16)]
     params = call(
         prep_kernel, "prep",
         [like((both, hid), BF16), like((hid, both), BF16), like((hid, both), BF16), like((both, hid), BF16)]
@@ -351,7 +373,7 @@
 
     pairs = rows // 2
     total = SECTIONS * pairs
-    slabs = 2 ** len(chains[0][0])
+    slabs = 2 ** len(chains[0][0][0])
     messages = [
         rows_of(slabs // 2 * sum(n for _, _, n in parts) + extra, both) for _, parts, extra in chains for _ in range(2)
     ]
@@ -371,26 +393,38 @@
             pltpu.VMEM((total, both), F32),
             pltpu.VMEM((both, hid), F32),
             pltpu.VMEM((hid, both), F32),
+            pltpu.SemaphoreType.DMA((2,)),
         ]
         + moved_scratch,
         scalars=1,
+        far=1,
         flops=12 * total * both * hid,
     )
 
-    back = back.reshape(groups, 2, inner, slice_rows, width).swapaxes(1, 2).reshape(devs, 2, slice_rows, width)
-    home = lax.all_to_all(back, "ctx", split_axis=0, concat_axis=0, tiled=True)
-    outputs = home[:, 0].reshape(inputs.shape)
-    grad_inputs = home[:, 1].reshape(inputs.shape)
+    home = None
+
+    def place(point, sends):
+        nonlocal back, home
+        if point == 1:
+            if False: sends, back = lax.optimization_barrier((sends, back))
+            back = back.reshape(groups, 2, inner, slice_rows, width).swapaxes(1, 2)
+            back = back.reshape(devs, 2, slice_rows, width)
+            home = lax.all_to_all(back, "ctx", split_axis=0, concat_axis=0, tiled=True)
+        if point == 0:
+            last, home = lax.optimization_barrier((sends[-1], home))
+            sends = sends[:-1] + [last]
+        return sends
 
     states = [(sums[2 * i], sums[2 * i + 1]) for i in range(len(chains))]
-    steps = len(chains[0][0])
+    steps = len(chains[0][0][0])
     for step in range(steps):
-        got = [swap(send, *order[step]) for (send, _), (order, _, _) in zip(states, chains)]
+        got = [swap_by_place(send, [order[step] for order in orders]) for send, (orders, _, _) in zip(place(step, [s for s, _ in states]), chains)]
         for i, (_, _, extra) in enumerate(chains):
             keep = states[i][1]
+            after = [states[i - 1][0]] if i and step in (1, 2) else []
             if step + 1 < steps:
                 count = (keep.shape[0] - extra) // 2 + extra
-                states[i] = call(functools.partial(halve_kernel, extra), "halve", [rows_of(count, both)] * 2, (keep, got[i]))
+                states[i] = call(functools.partial(halve_kernel, extra), "halve", [rows_of(count, both)] * 2, (keep, got[i], *after))
             else:
                 states[i] = add(extra, keep, got[i], len(rep_bits) == 1)
     for place, (axis, bit) in enumerate(rep_bits[1:]):
@@ -398,6 +432,7 @@
         for i, (_, _, extra) in enumerate(chains):
             states[i] = add(extra, states[i][0], got[i], place + 2 == len(rep_bits))
     others = [swap(bare, "rep", 1) for _, bare in states]
+    outputs, grad_inputs = (home[:, i].reshape(inputs.shape) for i in range(2))
     factor = 1.0 / math.sqrt(reps * devs * rows)
     grad_e, grad_be, grad_r, grad_br, grad_gate = call(
         functools.partial(final_kernel, factor, chains),

time: 57.9 us -> 57.6 us (level)
    ppermute x22 -> x10, starting transfers between devices: 23.1 us -> 12.8 us  [swap(): lax.ppermute(value, axis, [(i, i ^ bit) for i in range(lax.axis_size(axis...]
    ppermute x0 -> x12, starting transfers between devices: none -> 10 us  [swap_by_place(): return lax.ppermute(value, ('ctx', 'rep'), pairs)]
    ppermute x22 -> x10, waiting for transfers between devices: 14.8 us -> 8.38 us  [swap(): lax.ppermute(value, axis, [(i, i ^ bit) for i in range(lax.axis_size(axis...]
    ppermute x0 -> x12, waiting for transfers between devices: none -> 6.3 us  [swap_by_place(): return lax.ppermute(value, ('ctx', 'rep'), pairs)]
  transfers between devices with their start and end apart: 23 -> 23, of which waited for: 12 -> 13; matrix products, arithmetic and copies ran while one was open for 1% -> 1% of each run, Pallas kernels for 4% -> 4%
where the time goes in v3:
time: 57.6 us; the launch traced here: 57.3 us
  starting transfers between devices  26.6 us (46%)
  waiting for transfers between devices  14.7 us (26%)
  Pallas kernels  13.8 us (24%)
  local copies, waits for them, and re-layouts  1.4 us (2%)
  between operations  0.78 us (1%)
    pallas_call x20, Pallas kernels, call(): pl.pallas_call(kernel, name=name, out_shape=shapes, in_specs=[SMEM] * sca...  13.8 us
    ppermute x10, starting transfers between devices, swap(): lax.ppermute(value, axis, [(i, i ^ bit) for i in range(lax.axis_size(axis...  12.8 us
    ppermute x12, starting transfers between devices, swap_by_place(): return lax.ppermute(value, ('ctx', 'rep'), pairs)  10 us
    ppermute x10, waiting for transfers between devices, swap(): lax.ppermute(value, axis, [(i, i ^ bit) for i in range(lax.axis_size(axis...  8.38 us
    ppermute x12, waiting for transfers between devices, swap_by_place(): return lax.ppermute(value, ('ctx', 'rep'), pairs)  6.3 us
    all_to_all x1, starting transfers between devices, place(): home = lax.all_to_all(back, 'ctx', split_axis=0, concat_axis=0, tiled=True)  3.72 us
  transfers between devices with their start and end apart: 23, of which 13 were waited for; matrix products, arithmetic and copies ran while one was open for 1% of the time, Pallas kernels for 4%

profile of v3, /device:TPU:0, one launch (start us, length us, event | category | flops | bytes accessed | tf_op | source)
XLA Modules:
  0.0 57.3 jit_solution(8528595349491741601)
XLA Ops:
  0.7 1.5 %pack.1 = (bf16[4,2,32,256]{3,2,1,0:T(8,128)(2,1)S(1)}, bf16[4,2,32,256]{3,2,1,0:T(8,128)(2,1)S(1)}) custom-call(s32[2]{0:T(128)S(1)} %pad_add_fusion.where_ref, bf16[256,256]{1,0:T(8,128)(2,1)} %bitcast.15, bf16[256,256]{1,0:T(8,128)(2,1)} %bitcast.16), custom_call_target="tpu_custom_call" | custom-call | bytes 524296 | tf_op jit(solution)/shard_map/pack/pallas_call | solution.py:279
  2.8 1.0 %collective-permute-done.got_ref.refs_1_ = bf16[4,2,32,256]{3,2,1,0:T(8,128)(2,1)S(1)} collective-permute-done((bf16[4,2,32,256]{3,2,1,0:T(8,128)(2,1)S(1)}, bf16[4,2,32,256]{3,2,1,0:T(8,128)(2,1)S(1)}, u32[]{:S(2)}, u32[]{:S(2)}) %collective-permute-start) | collective-permute-done | bytes 131104 | tf_op jit(solution)/shard_map/ppermute | solution.py:304
  3.8 2.9 %collective-permute-start.1 = (bf16[2,2,32,256]{3,2,1,0:T(8,128)(2,1)S(1)}, bf16[2,2,32,256]{3,2,1,0:T(8,128)(2,1)S(1)}, u32[]{:S(2)}, u32[]{:S(2)}) collective-permute-start(bf16[2,2,32,256]{3,2,1,0:T(8,128)(2,1)S(1)} %get-tuple-element.53), channel_id=1, source_target_pairs={{0,8},{4,12},{8,0},{12,4},{16,24},{20,28},{24,16},{28,20},{1,9},{5... | collective-permute-start | bytes 196616 | tf_op jit(solution)/shard_map/ppermute | solution.py:304
  6.7 1.5 %collective-permute-start.2 = (bf16[2,2,32,256]{3,2,1,0:T(8,128)(2,1)S(1)}, bf16[2,2,32,256]{3,2,1,0:T(8,128)(2,1)S(1)}, u32[]{:S(2)}, u32[]{:S(2)}) collective-permute-start(bf16[2,2,32,256]{3,2,1,0:T(8,128)(2,1)S(1)} %get-tuple-element.54), channel_id=1, source_target_pairs={{0,16},{4,20},{8,24},{12,28},{16,0},{20,4},{24,8},{28,12},{1,17},{... | collective-permute-start | bytes 196616 | tf_op jit(solution)/shard_map/ppermute | solution.py:304
  8.3 0.7 %copy-done.1 = f32[512]{0:T(512)S(1)} copy-done((f32[512]{0:T(512)S(1)}, f32[512]{0:T(512)}, u32[]{:S(2)}) %copy-start.1) | copy-done | bytes 2072
  8.9 1.9 %prep.1 = (bf16[512,1024]{1,0:T(8,128)(2,1)S(1)}, bf16[1024,512]{1,0:T(8,128)(2,1)S(1)}, bf16[1024,512]{1,0:T(8,128)(2,1)S(1)}, bf16[512,1024]{1,0:T(8,128)(2,1)...) custom-call(bf16[512,1024]{1,0:T(8,128)(2,1)} %we_ref.1, f32[1,1024]{1,0:T(1,128)S(1)} %bitcast.12, ...), custom_call_target="tpu_custom_call" | custom-call | bytes 6307840 | tf_op jit(solution)/shard_map/prep/pallas_call | solution.py:279
  11.0 2.4 %collective-permute-done.3.refs_4_ = bf16[2,2,32,256]{3,2,1,0:T(8,128)(2,1)S(1)} collective-permute-done((bf16[2,2,32,256]{3,2,1,0:T(8,128)(2,1)S(1)}, bf16[2,2,32,256]{3,2,1,0:T(8,128)(2,1)S(1)}, u32[]{:S(2)}, u32[]{:S(2)}) %collective-permute-start.3) | collective-permute-done | bytes 65568 | tf_op jit(solution)/shard_map/ppermute | solution.py:304
  13.4 8.4 %sections.1 = (bf16[8,2,32,256]{3,2,1,0:T(8,128)(2,1)}, bf16[272,512]{1,0:T(8,128)(2,1)S(1)}, bf16[272,512]{1,0:T(8,128)(2,1)S(1)}, bf16[384,512]{1,0:T(8,128)(2...) custom-call(s32[2]{0:T(128)S(1)} %pad_add_fusion.where_ref, ...), custom_call_target="tpu_custom_call" | custom-call | flops 3221225472 | bytes 7053320 | tf_op jit(solution)/shard_map/sections/pallas_call | solution.py:279
  22.4 1.1 %collective-permute-done.9.recv_ref = bf16[384,512]{1,0:T(8,128)(2,1)S(1)} collective-permute-done((bf16[384,512]{1,0:T(8,128)(2,1)S(1)}, bf16[384,512]{1,0:T(8,128)(2,1)S(1)}, u32[]{:S(2)}, u32[]{:S(2)}) %collective-permute-start.9) | collective-permute-done | bytes 393248 | tf_op jit(solution)/shard_map/ppermute | solution.py:315
  23.7 0.6 collective-permute-start.10
  24.3 1.6 %collective-permute-start.15 = (bf16[192,512]{1,0:T(8,128)(2,1)S(1)}, bf16[192,512]{1,0:T(8,128)(2,1)S(1)}, u32[]{:S(2)}, u32[]{:S(2)}) collective-permute-start(bf16[192,512]{1,0:T(8,128)(2,1)S(1)} %get-tuple-element.84), channel_id=1, source_target_pairs={{0,1},{1,0},{2,3},{3,2},{4,5},{5,4},{6,7},{7,6},{8,9},{9,8},{10,11... | collective-permute-start | bytes 589832 | tf_op jit(solution)/shard_map/ppermute | solution.py:315
  26.0 0.6 %collective-permute-start.5 = (bf16[144,512]{1,0:T(8,128)(2,1)S(1)}, bf16[144,512]{1,0:T(8,128)(2,1)S(1)}, u32[]{:S(2)}, u32[]{:S(2)}) collective-permute-start(bf16[144,512]{1,0:T(8,128)(2,1)S(1)} %get-tuple-element.67), channel_id=1, source_target_pairs={{0,8},{1,9},{2,10},{3,11},{4,12},{5,13},{6,14},{7,15},{8,0},{9,1},... | collective-permute-start | bytes 442376 | tf_op jit(solution)/shard_map/ppermute | solution.py:315
  26.6 3.7 %all-to-all-start = ((bf16[8,2,32,256]{3,2,1,0:T(8,128)(2,1)}), bf16[8,2,32,256]{3,2,1,0:T(8,128)(2,1)S(1)}, u32[]{:S(2)}, u32[]{:S(2)}) async-start(bf16[8,2,32,256]{3,2,1,0:T(8,128)(2,1)} %get-tuple-element.63), calls=%async_computation | async-start | bytes 524288 | tf_op jit(solution)/shard_map/all_to_all | solution.py:412
  30.4 1.2 %collective-permute-done.5.recv_ref = bf16[144,512]{1,0:T(8,128)(2,1)S(1)} collective-permute-done((bf16[144,512]{1,0:T(8,128)(2,1)S(1)}, bf16[144,512]{1,0:T(8,128)(2,1)S(1)}, u32[]{:S(2)}, u32[]{:S(2)}) %collective-permute-start.5) | collective-permute-done | bytes 147488 | tf_op jit(solution)/shard_map/ppermute | solution.py:315
  31.7 0.6 %collective-permute-start.11 = (bf16[96,512]{1,0:T(8,128)(2,1)S(1)}, bf16[96,512]{1,0:T(8,128)(2,1)S(1)}, u32[]{:S(2)}, u32[]{:S(2)}) collective-permute-start(bf16[96,512]{1,0:T(8,128)(2,1)S(1)} %get-tuple-element.78.refs_0_), channel_id=1, source_target_pairs={{0,1},{1,0},{2,3},{3,2},{4,5},{5,4},{6,7},{7,6},{8,9},{9,8},{10,11... | collective-permute-start | bytes 294920 | tf_op jit(solution)/shard_map/ppermute | solution.py:315
  32.4 0.7 %collective-permute-start.16 = (bf16[96,512]{1,0:T(8,128)(2,1)S(1)}, bf16[96,512]{1,0:T(8,128)(2,1)S(1)}, u32[]{:S(2)}, u32[]{:S(2)}) collective-permute-start(bf16[96,512]{1,0:T(8,128)(2,1)S(1)} %get-tuple-element.86), channel_id=1, source_target_pairs={{0,8},{1,9},{2,10},{3,11},{4,12},{5,13},{6,14},{7,15},{8,0},{9,1},... | collective-permute-start | bytes 294920 | tf_op jit(solution)/shard_map/ppermute | solution.py:315
  33.1 1.5 %collective-permute-start.6 = (bf16[80,512]{1,0:T(8,128)(2,1)S(1)}, bf16[80,512]{1,0:T(8,128)(2,1)S(1)}, u32[]{:S(2)}, u32[]{:S(2)}) collective-permute-start(bf16[80,512]{1,0:T(8,128)(2,1)S(1)} %get-tuple-element.69.refs_0_), channel_id=1, source_target_pairs={{0,16},{1,17},{2,18},{3,19},{4,20},{5,21},{6,22},{7,23},{8,24},{9,... | collective-permute-start | bytes 245768 | tf_op jit(solution)/shard_map/ppermute | solution.py:315
  34.6 3.6 %collective-permute-done.6.recv_ref = bf16[80,512]{1,0:T(8,128)(2,1)S(1)} collective-permute-done((bf16[80,512]{1,0:T(8,128)(2,1)S(1)}, bf16[80,512]{1,0:T(8,128)(2,1)S(1)}, u32[]{:S(2)}, u32[]{:S(2)}) %collective-permute-start.6) | collective-permute-done | bytes 81952 | tf_op jit(solution)/shard_map/ppermute | solution.py:315
  38.2 1.1 %collective-permute-start.7 = (bf16[48,512]{1,0:T(8,128)(2,1)S(1)}, bf16[48,512]{1,0:T(8,128)(2,1)S(1)}, u32[]{:S(2)}, u32[]{:S(2)}) collective-permute-start(bf16[48,512]{1,0:T(8,128)(2,1)S(1)} %get-tuple-element.71.refs_0_), channel_id=1, source_target_pairs={{0,1},{1,0},{2,3},{3,2},{4,5},{5,4},{6,7},{7,6},{8,9},{9,8},{10,11... | collective-permute-start | bytes 147464 | tf_op jit(solution)/shard_map/ppermute | solution.py:315
  39.3 1.3 %collective-permute-start.12 = (bf16[48,512]{1,0:T(8,128)(2,1)S(1)}, bf16[48,512]{1,0:T(8,128)(2,1)S(1)}, u32[]{:S(2)}, u32[]{:S(2)}) collective-permute-start(bf16[48,512]{1,0:T(8,128)(2,1)S(1)} %get-tuple-element.80.refs_0_), channel_id=1, source_target_pairs={{0,8},{1,9},{2,10},{3,11},{4,12},{5,13},{6,14},{7,15},{8,0},{9,1},... | collective-permute-start | bytes 147464 | tf_op jit(solution)/shard_map/ppermute | solution.py:315
  40.6 1.4 %collective-permute-start.17 = (bf16[48,512]{1,0:T(8,128)(2,1)S(1)}, bf16[48,512]{1,0:T(8,128)(2,1)S(1)}, u32[]{:S(2)}, u32[]{:S(2)}) collective-permute-start(bf16[48,512]{1,0:T(8,128)(2,1)S(1)} %get-tuple-element.88), channel_id=1, source_target_pairs={{0,16},{1,17},{2,18},{3,19},{4,20},{5,21},{6,22},{7,23},{8,24},{9,... | collective-permute-start | bytes 147464 | tf_op jit(solution)/shard_map/ppermute | solution.py:315
  42.4 2.6 %collective-permute-start.8 = (bf16[48,512]{1,0:T(8,128)(2,1)S(1)}, bf16[48,512]{1,0:T(8,128)(2,1)S(1)}, u32[]{:S(2)}, u32[]{:S(2)}) collective-permute-start(bf16[48,512]{1,0:T(8,128)(2,1)S(1)} %add.8.keep_ref), channel_id=1, source_target_pairs={{0,2},{1,3},{2,0},{3,1},{4,6},{5,7},{6,4},{7,5},{8,10},{9,11},{10,... | collective-permute-start | bytes 147464 | tf_op jit(solution)/shard_map/ppermute | solution.py:304
  45.1 1.1 %collective-permute-start.13 = (bf16[48,512]{1,0:T(8,128)(2,1)S(1)}, bf16[48,512]{1,0:T(8,128)(2,1)S(1)}, u32[]{:S(2)}, u32[]{:S(2)}) collective-permute-start(bf16[48,512]{1,0:T(8,128)(2,1)S(1)} %add.10.keep_ref), channel_id=1, source_target_pairs={{0,2},{1,3},{2,0},{3,1},{4,6},{5,7},{6,4},{7,5},{8,10},{9,11},{10,... | collective-permute-start | bytes 147464 | tf_op jit(solution)/shard_map/ppermute | solution.py:304
  46.2 2.0 %collective-permute-start.18 = (bf16[48,512]{1,0:T(8,128)(2,1)S(1)}, bf16[48,512]{1,0:T(8,128)(2,1)S(1)}, u32[]{:S(2)}, u32[]{:S(2)}) collective-permute-start(bf16[48,512]{1,0:T(8,128)(2,1)S(1)} %add.12.keep_ref), channel_id=1, source_target_pairs={{0,2},{1,3},{2,0},{3,1},{4,6},{5,7},{6,4},{7,5},{8,10},{9,11},{10,... | collective-permute-start | bytes 147464 | tf_op jit(solution)/shard_map/ppermute | solution.py:304
  48.1 1.4 %collective-permute-done.8.recv_ref = bf16[48,512]{1,0:T(8,128)(2,1)S(1)} collective-permute-done((bf16[48,512]{1,0:T(8,128)(2,1)S(1)}, bf16[48,512]{1,0:T(8,128)(2,1)S(1)}, u32[]{:S(2)}, u32[]{:S(2)}) %collective-permute-start.8) | collective-permute-done | bytes 49184 | tf_op jit(solution)/shard_map/ppermute | solution.py:304
  49.6 0.6 %collective-permute-done.13.recv_ref = bf16[48,512]{1,0:T(8,128)(2,1)S(1)} collective-permute-done((bf16[48,512]{1,0:T(8,128)(2,1)S(1)}, bf16[48,512]{1,0:T(8,128)(2,1)S(1)}, u32[]{:S(2)}, u32[]{:S(2)}) %collective-permute-start.13) | collective-permute-done | bytes 49184 | tf_op jit(solution)/shard_map/ppermute | solution.py:304
  50.2 1.5 %collective-permute-start.20 = (bf16[48,512]{1,0:T(8,128)(2,1)S(1)}, bf16[48,512]{1,0:T(8,128)(2,1)S(1)}, u32[]{:S(2)}, u32[]{:S(2)}) collective-permute-start(bf16[48,512]{1,0:T(8,128)(2,1)S(1)} %add.11.refs_1_), channel_id=1, source_target_pairs={{0,1},{1,0},{2,3},{3,2},{4,5},{5,4},{6,7},{7,6},{8,9},{9,8},{10,11... | collective-permute-start | bytes 147464 | tf_op jit(solution)/shard_map/ppermute | solution.py:304
  51.8 0.6 collective-permute-start.21
  52.4 0.7 %fusion = (bf16[8,1,32,256]{3,2,1,0:T(8,128)(2,1)}, bf16[8,1,32,256]{3,2,1,0:T(8,128)(2,1)}) fusion(bf16[8,2,32,256]{3,2,1,0:T(8,128)(2,1)S(1)} %all-to-all-done), kind=kLoop, calls=%fused_computation.1 | loop fusion | bytes 524288 | tf_op jit(solution)/shard_map/slice | solution.py:435
  53.5 0.8 %collective-permute-done.20.refs_4_ = bf16[48,512]{1,0:T(8,128)(2,1)S(1)} collective-permute-done((bf16[48,512]{1,0:T(8,128)(2,1)S(1)}, bf16[48,512]{1,0:T(8,128)(2,1)S(1)}, u32[]{:S(2)}, u32[]{:S(2)}) %collective-permute-start.20) | collective-permute-done | bytes 49184 | tf_op jit(solution)/shard_map/ppermute | solution.py:304
  54.3 1.6 %collective-permute-done.21.refs_5_ = bf16[48,512]{1,0:T(8,128)(2,1)S(1)} collective-permute-done((bf16[48,512]{1,0:T(8,128)(2,1)S(1)}, bf16[48,512]{1,0:T(8,128)(2,1)S(1)}, u32[]{:S(2)}, u32[]{:S(2)}) %collective-permute-start.21) | collective-permute-done | bytes 49184 | tf_op jit(solution)/shard_map/ppermute | solution.py:304
  56.0 1.4 %final.1 = (f32[64,1024]{1,0:T(8,128)}, f32[1,1024]{1,0:T(1,128)}, f32[128,512]{1,0:T(8,128)}, f32[1,512]{1,0:T(1,128)}, f32[1,512]{1,0:T(1,128)}) custom-call(s32[2]{0:T(128)S(1)} %pad_add_fusion.where_ref, bf16[48,512]{1,0:T(8,128)(2,1)S(1)} %get-tuple-element.72.refs_0_, bf16[48,512]{1,0:T(8,128)(2,1)S(1)} %add.11.refs_1_, ...), custom_call_target="tpu_custom_call" | custom-call | bytes 811016 | tf_op jit(solution)/shard_map/final/pallas_call | solution.py:279
  (42 shorter events, 2.9 us)
Async XLA Ops:
  2.3 1.5 %collective-permute-start = (bf16[4,2,32,256]{3,2,1,0:T(8,128)(2,1)S(1)}, bf16[4,2,32,256]{3,2,1,0:T(8,128)(2,1)S(1)}, u32[]{:S(2)}, u32[]{:S(2)}) collective-permute-start(bf16[4,2,32,256]{3,2,1,0:T(8,128)(2,1)S(1)} %get-tuple-element.52), channel_id=1, source_target_pairs={{0,4},{4,0},{8,12},{12,8},{16,20},{20,16},{24,28},{28,24},{1,5},{5... | collective-permute-start | bytes 393224 | tf_op jit(solution)/shard_map/ppermute | solution.py:304
  3.8 4.5 %copy-start.2 = (f32[512]{0:T(512)S(1)}, f32[512]{0:T(512)}, u32[]{:S(2)}) copy-start(f32[512]{0:T(512)} %param.12) | copy-start | bytes 6148
  3.8 7.1 %collective-permute-start.1 = (bf16[2,2,32,256]{3,2,1,0:T(8,128)(2,1)S(1)}, bf16[2,2,32,256]{3,2,1,0:T(8,128)(2,1)S(1)}, u32[]{:S(2)}, u32[]{:S(2)}) collective-permute-start(bf16[2,2,32,256]{3,2,1,0:T(8,128)(2,1)S(1)} %get-tuple-element.53), channel_id=1, source_target_pairs={{0,8},{4,12},{8,0},{12,4},{16,24},{20,28},{24,16},{28,20},{1,9},{5... | collective-permute-start | bytes 196616 | tf_op jit(solution)/shard_map/ppermute | solution.py:304
  6.7 1.6 %copy-start = (f32[1024]{0:T(1024)S(1)}, f32[1024]{0:T(1024)}, u32[]{:S(2)}) copy-start(f32[1024]{0:T(1024)} %param.9) | copy-start | bytes 12292
  6.7 4.3 %collective-permute-start.2 = (bf16[2,2,32,256]{3,2,1,0:T(8,128)(2,1)S(1)}, bf16[2,2,32,256]{3,2,1,0:T(8,128)(2,1)S(1)}, u32[]{:S(2)}, u32[]{:S(2)}) collective-permute-start(bf16[2,2,32,256]{3,2,1,0:T(8,128)(2,1)S(1)} %get-tuple-element.54), channel_id=1, source_target_pairs={{0,16},{4,20},{8,24},{12,28},{16,0},{20,4},{24,8},{28,12},{1,17},{... | collective-permute-start | bytes 196616 | tf_op jit(solution)/shard_map/ppermute | solution.py:304
  8.2 5.2 %collective-permute-start.3 = (bf16[2,2,32,256]{3,2,1,0:T(8,128)(2,1)S(1)}, bf16[2,2,32,256]{3,2,1,0:T(8,128)(2,1)S(1)}, u32[]{:S(2)}, u32[]{:S(2)}) collective-permute-start(bf16[2,2,32,256]{3,2,1,0:T(8,128)(2,1)S(1)} %get-tuple-element.55), channel_id=1, source_target_pairs={{0,24},{4,28},{8,16},{12,20},{16,8},{20,12},{24,0},{28,4},{1,25},{... | collective-permute-start | bytes 196616 | tf_op jit(solution)/shard_map/ppermute | solution.py:304
  8.3 0.7 %copy-start.1 = (f32[512]{0:T(512)S(1)}, f32[512]{0:T(512)}, u32[]{:S(2)}) copy-start(f32[512]{0:T(512)} %param.11) | copy-start | bytes 6148
  21.8 1.8 %collective-permute-start.9 = (bf16[384,512]{1,0:T(8,128)(2,1)S(1)}, bf16[384,512]{1,0:T(8,128)(2,1)S(1)}, u32[]{:S(2)}, u32[]{:S(2)}) collective-permute-start(bf16[384,512]{1,0:T(8,128)(2,1)S(1)} %get-tuple-element.74), channel_id=1, source_target_pairs={{0,4},{1,5},{2,6},{3,7},{4,0},{5,1},{6,2},{7,3},{8,12},{9,13},{10,... | collective-permute-start | bytes 1179656 | tf_op jit(solution)/shard_map/ppermute | solution.py:315
  21.9 2.4 %collective-permute-start.14 = (bf16[384,512]{1,0:T(8,128)(2,1)S(1)}, bf16[384,512]{1,0:T(8,128)(2,1)S(1)}, u32[]{:S(2)}, u32[]{:S(2)}) collective-permute-start(bf16[384,512]{1,0:T(8,128)(2,1)S(1)} %get-tuple-element.82), channel_id=1, source_target_pairs={{0,4},{1,5},{2,6},{3,7},{4,0},{5,1},{6,2},{7,3},{8,12},{9,13},{10,... | collective-permute-start | bytes 1179656 | tf_op jit(solution)/shard_map/ppermute | solution.py:315
  22.3 3.6 %collective-permute-start.4 = (bf16[272,512]{1,0:T(8,128)(2,1)S(1)}, bf16[272,512]{1,0:T(8,128)(2,1)S(1)}, u32[]{:S(2)}, u32[]{:S(2)}) collective-permute-start(bf16[272,512]{1,0:T(8,128)(2,1)S(1)} %get-tuple-element.65), channel_id=1, source_target_pairs={{0,4},{1,5},{2,6},{3,7},{4,0},{5,1},{6,2},{7,3},{8,12},{9,13},{10,... | collective-permute-start | bytes 835592 | tf_op jit(solution)/shard_map/ppermute | solution.py:315
  23.7 8.0 %collective-permute-start.10 = (bf16[192,512]{1,0:T(8,128)(2,1)S(1)}, bf16[192,512]{1,0:T(8,128)(2,1)S(1)}, u32[]{:S(2)}, u32[]{:S(2)}) collective-permute-start(bf16[192,512]{1,0:T(8,128)(2,1)S(1)} %get-tuple-element.76), channel_id=1, source_target_pairs={{0,16},{1,17},{2,18},{3,19},{4,20},{5,21},{6,22},{7,23},{8,24},{9,... | collective-permute-start | bytes 589832 | tf_op jit(solution)/shard_map/ppermute | solution.py:315
  24.3 8.0 %collective-permute-start.15 = (bf16[192,512]{1,0:T(8,128)(2,1)S(1)}, bf16[192,512]{1,0:T(8,128)(2,1)S(1)}, u32[]{:S(2)}, u32[]{:S(2)}) collective-permute-start(bf16[192,512]{1,0:T(8,128)(2,1)S(1)} %get-tuple-element.84), channel_id=1, source_target_pairs={{0,1},{1,0},{2,3},{3,2},{4,5},{5,4},{6,7},{7,6},{8,9},{9,8},{10,11... | collective-permute-start | bytes 589832 | tf_op jit(solution)/shard_map/ppermute | solution.py:315
  26.0 5.6 %collective-permute-start.5 = (bf16[144,512]{1,0:T(8,128)(2,1)S(1)}, bf16[144,512]{1,0:T(8,128)(2,1)S(1)}, u32[]{:S(2)}, u32[]{:S(2)}) collective-permute-start(bf16[144,512]{1,0:T(8,128)(2,1)S(1)} %get-tuple-element.67), channel_id=1, source_target_pairs={{0,8},{1,9},{2,10},{3,11},{4,12},{5,13},{6,14},{7,15},{8,0},{9,1},... | collective-permute-start | bytes 442376 | tf_op jit(solution)/shard_map/ppermute | solution.py:315
  26.6 25.7 %all-to-all-start = ((bf16[8,2,32,256]{3,2,1,0:T(8,128)(2,1)}), bf16[8,2,32,256]{3,2,1,0:T(8,128)(2,1)S(1)}, u32[]{:S(2)}, u32[]{:S(2)}) async-start(bf16[8,2,32,256]{3,2,1,0:T(8,128)(2,1)} %get-tuple-element.63), calls=%async_computation | async-start | bytes 524288 | tf_op jit(solution)/shard_map/all_to_all | solution.py:412
  31.7 7.6 %collective-permute-start.11 = (bf16[96,512]{1,0:T(8,128)(2,1)S(1)}, bf16[96,512]{1,0:T(8,128)(2,1)S(1)}, u32[]{:S(2)}, u32[]{:S(2)}) collective-permute-start(bf16[96,512]{1,0:T(8,128)(2,1)S(1)} %get-tuple-element.78.refs_0_), channel_id=1, source_target_pairs={{0,1},{1,0},{2,3},{3,2},{4,5},{5,4},{6,7},{7,6},{8,9},{9,8},{10,11... | collective-permute-start | bytes 294920 | tf_op jit(solution)/shard_map/ppermute | solution.py:315
  32.4 8.2 %collective-permute-start.16 = (bf16[96,512]{1,0:T(8,128)(2,1)S(1)}, bf16[96,512]{1,0:T(8,128)(2,1)S(1)}, u32[]{:S(2)}, u32[]{:S(2)}) collective-permute-start(bf16[96,512]{1,0:T(8,128)(2,1)S(1)} %get-tuple-element.86), channel_id=1, source_target_pairs={{0,8},{1,9},{2,10},{3,11},{4,12},{5,13},{6,14},{7,15},{8,0},{9,1},... | collective-permute-start | bytes 294920 | tf_op jit(solution)/shard_map/ppermute | solution.py:315
  33.1 5.0 %collective-permute-start.6 = (bf16[80,512]{1,0:T(8,128)(2,1)S(1)}, bf16[80,512]{1,0:T(8,128)(2,1)S(1)}, u32[]{:S(2)}, u32[]{:S(2)}) collective-permute-start(bf16[80,512]{1,0:T(8,128)(2,1)S(1)} %get-tuple-element.69.refs_0_), channel_id=1, source_target_pairs={{0,16},{1,17},{2,18},{3,19},{4,20},{5,21},{6,22},{7,23},{8,24},{9,... | collective-permute-start | bytes 245768 | tf_op jit(solution)/shard_map/ppermute | solution.py:315
  38.2 4.2 %collective-permute-start.7 = (bf16[48,512]{1,0:T(8,128)(2,1)S(1)}, bf16[48,512]{1,0:T(8,128)(2,1)S(1)}, u32[]{:S(2)}, u32[]{:S(2)}) collective-permute-start(bf16[48,512]{1,0:T(8,128)(2,1)S(1)} %get-tuple-element.71.refs_0_), channel_id=1, source_target_pairs={{0,1},{1,0},{2,3},{3,2},{4,5},{5,4},{6,7},{7,6},{8,9},{9,8},{10,11... | collective-permute-start | bytes 147464 | tf_op jit(solution)/shard_map/ppermute | solution.py:315
  39.3 5.7 %collective-permute-start.12 = (bf16[48,512]{1,0:T(8,128)(2,1)S(1)}, bf16[48,512]{1,0:T(8,128)(2,1)S(1)}, u32[]{:S(2)}, u32[]{:S(2)}) collective-permute-start(bf16[48,512]{1,0:T(8,128)(2,1)S(1)} %get-tuple-element.80.refs_0_), channel_id=1, source_target_pairs={{0,8},{1,9},{2,10},{3,11},{4,12},{5,13},{6,14},{7,15},{8,0},{9,1},... | collective-permute-start | bytes 147464 | tf_op jit(solution)/shard_map/ppermute | solution.py:315
  40.6 5.5 %collective-permute-start.17 = (bf16[48,512]{1,0:T(8,128)(2,1)S(1)}, bf16[48,512]{1,0:T(8,128)(2,1)S(1)}, u32[]{:S(2)}, u32[]{:S(2)}) collective-permute-start(bf16[48,512]{1,0:T(8,128)(2,1)S(1)} %get-tuple-element.88), channel_id=1, source_target_pairs={{0,16},{1,17},{2,18},{3,19},{4,20},{5,21},{6,22},{7,23},{8,24},{9,... | collective-permute-start | bytes 147464 | tf_op jit(solution)/shard_map/ppermute | solution.py:315
  42.4 7.1 %collective-permute-start.8 = (bf16[48,512]{1,0:T(8,128)(2,1)S(1)}, bf16[48,512]{1,0:T(8,128)(2,1)S(1)}, u32[]{:S(2)}, u32[]{:S(2)}) collective-permute-start(bf16[48,512]{1,0:T(8,128)(2,1)S(1)} %add.8.keep_ref), channel_id=1, source_target_pairs={{0,2},{1,3},{2,0},{3,1},{4,6},{5,7},{6,4},{7,5},{8,10},{9,11},{10,... | collective-permute-start | bytes 147464 | tf_op jit(solution)/shard_map/ppermute | solution.py:304
  45.1 5.1 %collective-permute-start.13 = (bf16[48,512]{1,0:T(8,128)(2,1)S(1)}, bf16[48,512]{1,0:T(8,128)(2,1)S(1)}, u32[]{:S(2)}, u32[]{:S(2)}) collective-permute-start(bf16[48,512]{1,0:T(8,128)(2,1)S(1)} %add.10.keep_ref), channel_id=1, source_target_pairs={{0,2},{1,3},{2,0},{3,1},{4,6},{5,7},{6,4},{7,5},{8,10},{9,11},{10,... | collective-permute-start | bytes 147464 | tf_op jit(solution)/shard_map/ppermute | solution.py:304
  46.2 5.6 %collective-permute-start.18 = (bf16[48,512]{1,0:T(8,128)(2,1)S(1)}, bf16[48,512]{1,0:T(8,128)(2,1)S(1)}, u32[]{:S(2)}, u32[]{:S(2)}) collective-permute-start(bf16[48,512]{1,0:T(8,128)(2,1)S(1)} %add.12.keep_ref), channel_id=1, source_target_pairs={{0,2},{1,3},{2,0},{3,1},{4,6},{5,7},{6,4},{7,5},{8,10},{9,11},{10,... | collective-permute-start | bytes 147464 | tf_op jit(solution)/shard_map/ppermute | solution.py:304
  49.5 4.0 %collective-permute-start.19 = (bf16[32,512]{1,0:T(8,128)(2,1)S(1)}, bf16[32,512]{1,0:T(8,128)(2,1)S(1)}, u32[]{:S(2)}, u32[]{:S(2)}) collective-permute-start(bf16[32,512]{1,0:T(8,128)(2,1)S(1)} %get-tuple-element.89), channel_id=1, source_target_pairs={{0,1},{1,0},{2,3},{3,2},{4,5},{5,4},{6,7},{7,6},{8,9},{9,8},{10,11... | collective-permute-start | bytes 98312 | tf_op jit(solution)/shard_map/ppermute | solution.py:304
  50.2 4.2 %collective-permute-start.20 = (bf16[48,512]{1,0:T(8,128)(2,1)S(1)}, bf16[48,512]{1,0:T(8,128)(2,1)S(1)}, u32[]{:S(2)}, u32[]{:S(2)}) collective-permute-start(bf16[48,512]{1,0:T(8,128)(2,1)S(1)} %add.11.refs_1_), channel_id=1, source_target_pairs={{0,1},{1,0},{2,3},{3,2},{4,5},{5,4},{6,7},{7,6},{8,9},{9,8},{10,11... | collective-permute-start | bytes 147464 | tf_op jit(solution)/shard_map/ppermute | solution.py:304
  51.8 4.2 %collective-permute-start.21 = (bf16[48,512]{1,0:T(8,128)(2,1)S(1)}, bf16[48,512]{1,0:T(8,128)(2,1)S(1)}, u32[]{:S(2)}, u32[]{:S(2)}) collective-permute-start(bf16[48,512]{1,0:T(8,128)(2,1)S(1)} %add.13.refs_2_), channel_id=1, source_target_pairs={{0,1},{1,0},{2,3},{3,2},{4,5},{5,4},{6,7},{7,6},{8,9},{9,8},{10,11... | collective-permute-start | bytes 147464 | tf_op jit(solution)/shard_map/ppermute | solution.py:304

commit v4 on v3

--- a/solution.py
+++ b/solution.py
@@ -235,13 +235,17 @@
         write_extra((send_out, keep_out), read_extra(keep_ref, 4) + read_extra(recv_ref, 4))
 
 
-def add_kernel(extra, keep_ref, recv_ref, out_ref, *bare_ref):
-    size = keep_ref.shape[0] - extra
-    total = (keep_ref[:size, :].astype(F32) + recv_ref[:size, :].astype(F32)).astype(BF16)
-    for ref in (out_ref, *bare_ref):
-        ref[:size, :] = total
+def add_kernel(extra, count, *refs):
+    kept, got, outs = refs[:count], refs[count : 2 * count], refs[2 * count :]
+    at = 0
+    for i, (keep_ref, recv_ref) in enumerate(zip(kept, got)):
+        size = keep_ref.shape[0] - (0 if i else extra)
+        total = (keep_ref[:size, :].astype(F32) + recv_ref[:size, :].astype(F32)).astype(BF16)
+        for ref in outs:
+            ref[at : at + size, :] = total
+        at += size
     if extra:
-        write_extra((out_ref,), read_extra(keep_ref, 4) + read_extra(recv_ref, 4))
+        write_extra(outs[:1], read_extra(kept[0], 4) + read_extra(got[0], 4))
 
 
 def final_kernel(factor, chains, where_ref, *refs):
@@ -292,11 +296,12 @@
     return jax.ShapeDtypeStruct((count, lanes), BF16)
 
 
-def add(extra, keep, got, bare):
-    shapes = [rows_of(*keep.shape)]
+def add(extra, kept, got, bare):
+    size = sum(keep.shape[0] for keep in kept)
+    shapes = [rows_of(size, kept[0].shape[1])]
     if bare and extra:
-        shapes.append(rows_of(keep.shape[0] - extra, keep.shape[1]))
-    outs = call(functools.partial(add_kernel, extra), "add", shapes, (keep, got))
+        shapes.append(rows_of(size - extra, kept[0].shape[1]))
+    outs = call(functools.partial(add_kernel, extra, len(kept)), "add", shapes, (*kept, *got))
     return outs[0], outs[-1]
 
 
@@ -328,16 +333,15 @@
     ctx_bits = [("ctx", 2**i) for i in range(count)]
     rep_bits = [("rep", 2**i) for i in range(reps.bit_length() - 1)]
     size = both // devs
-    later = ctx_bits[1:] + rep_bits[:1]
+    later = (ctx_bits[1:] + rep_bits[:1])[::-1]
     if size % 64 == 0:
-        cut, most = size // 2, size * 3 // 4
-        shares = [[("e", 0, cut)], [("r", 0, most)], [("e", cut, size - cut), ("r", most, size - most)]]
+        cut = size * 3 // 4
+        shares = [[("e", 0, cut)], [("r", 0, cut)], [("e", cut, size - cut), ("r", cut, size - cut)]]
     else:
         shares = [[("e", 0, size)], [("r", 0, size)]]
-    turns = [(0, 0), (1, 1), (2, 2)]
     chains = [
-        (tuple(ctx_bits[:1] + later[turn:] + later[:turn] for turn in pair), share, extra)
-        for pair, share, extra in zip(turns, shares, (EXTRA, 0, 0))
+        ((ctx_bits[:1] + later[turn:] + later[:turn],) * 2, share, EXTRA * (turn == 0))
+        for turn, share in zip(reversed(range(len(shares))), shares)
     ]
     where = jnp.stack([lax.axis_index("ctx"), lax.axis_index("rep")]).astype(jnp.int32)
 
@@ -401,41 +405,40 @@
         flops=12 * total * both * hid,
     )
 
-    home = None
-
-    def place(point, sends):
-        nonlocal back, home
-        if point == 1:
-            if False: sends, back = lax.optimization_barrier((sends, back))
-            back = back.reshape(groups, 2, inner, slice_rows, width).swapaxes(1, 2)
-            back = back.reshape(devs, 2, slice_rows, width)
-            home = lax.all_to_all(back, "ctx", split_axis=0, concat_axis=0, tiled=True)
-        if point == 0:
-            last, home = lax.optimization_barrier((sends[-1], home))
-            sends = sends[:-1] + [last]
-        return sends
+    back = back.reshape(groups, 2, inner, slice_rows, width).swapaxes(1, 2)
+    home = lax.all_to_all(back.reshape(devs, 2, slice_rows, width), "ctx", split_axis=0, concat_axis=0, tiled=True)
 
     states = [(sums[2 * i], sums[2 * i + 1]) for i in range(len(chains))]
     steps = len(chains[0][0][0])
     for step in range(steps):
-        got = [swap_by_place(send, [order[step] for order in orders]) for send, (orders, _, _) in zip(place(step, [s for s, _ in states]), chains)]
+        got = [
+            swap_by_place(send, [order[step] for order in orders]) for (send, _), (orders, _, _) in zip(states, chains)
+        ]
+        if step + 1 == steps:
+            break
         for i, (_, _, extra) in enumerate(chains):
             keep = states[i][1]
-            after = [states[i - 1][0]] if i and step in (1, 2) else []
-            if step + 1 < steps:
-                count = (keep.shape[0] - extra) // 2 + extra
-                states[i] = call(functools.partial(halve_kernel, extra), "halve", [rows_of(count, both)] * 2, (keep, got[i], *after))
-            else:
-                states[i] = add(extra, keep, got[i], len(rep_bits) == 1)
-    for place, (axis, bit) in enumerate(rep_bits[1:]):
+            after = [states[i - 1][0]] if i and step else []
+            count = (keep.shape[0] - extra) // 2 + extra
+            states[i] = call(
+                functools.partial(halve_kernel, extra), "halve", [rows_of(count, both)] * 2, (keep, got[i], *after)
+            )
+    joined = [(i,) for i in range(len(chains))]
+    ends = [(None, sum((chains[i][1] for i in group), []), chains[group[0]][2]) for group in joined]
+    alone = len(rep_bits) == 1
+    states = [
+        add(extra, [states[i][1] for i in group], [got[i] for i in group], alone)
+        for group, (_, _, extra) in zip(joined, ends)
+    ]
+    for turn, (axis, bit) in enumerate(rep_bits[1:]):
         got = [swap(own, axis, bit) for own, _ in states]
-        for i, (_, _, extra) in enumerate(chains):
-            states[i] = add(extra, states[i][0], got[i], place + 2 == len(rep_bits))
+        for i, (_, _, extra) in enumerate(ends):
+            states[i] = add(extra, [states[i][0]], [got[i]], turn + 2 == len(rep_bits))
     others = [swap(bare, "rep", 1) for _, bare in states]
     outputs, grad_inputs = (home[:, i].reshape(inputs.shape) for i in range(2))
     factor = 1.0 / math.sqrt(reps * devs * rows)
     grad_e, grad_be, grad_r, grad_br, grad_gate = call(
-        functools.partial(final_kernel, factor, chains),
+        functools.partial(final_kernel, factor, ends),
         "final",
         [
             jax.ShapeDtypeStruct((both // devs, hid), F32),

time: 57.6 us -> 56.5 us (0.981)
  waiting for transfers between devices: 14.7 us -> 10.2 us
  starting transfers between devices: 26.6 us -> 29.9 us
    ppermute x12, waiting for transfers between devices: 6.3 us -> 3.66 us  [swap_by_place(): return lax.ppermute(value, ('ctx', 'rep'), pairs)]
    ppermute x10, starting transfers between devices: 12.8 us -> 15.4 us  [swap(): lax.ppermute(value, axis, [(i, i ^ bit) for i in range(lax.axis_size(axis...]
    ppermute x10, waiting for transfers between devices: 8.38 us -> 6.58 us  [swap(): lax.ppermute(value, axis, [(i, i ^ bit) for i in range(lax.axis_size(axis...]
    ppermute x12, starting transfers between devices: 10 us -> 10.7 us  [swap_by_place(): return lax.ppermute(value, ('ctx', 'rep'), pairs)]
  transfers between devices with their start and end apart: 23 -> 23, of which waited for: 13 -> 11; matrix products, arithmetic and copies ran while one was open for 1% -> 1% of each run, Pallas kernels for 4% -> 4%
where the time goes in v4:
time: 56.5 us; the launch traced here: 56.2 us
  starting transfers between devices  29.9 us (53%)
  Pallas kernels  13.8 us (24%)
  waiting for transfers between devices  10.2 us (18%)
  local copies, waits for them, and re-layouts  1.4 us (2%)
  between operations  0.76 us (1%)
    ppermute x10, starting transfers between devices, swap(): lax.ppermute(value, axis, [(i, i ^ bit) for i in range(lax.axis_size(axis...  15.4 us
    pallas_call x20, Pallas kernels, call(): pl.pallas_call(kernel, name=name, out_shape=shapes, in_specs=[SMEM] * sca...  13.8 us
    ppermute x12, starting transfers between devices, swap_by_place(): return lax.ppermute(value, ('ctx', 'rep'), pairs)  10.7 us
    ppermute x10, waiting for transfers between devices, swap(): lax.ppermute(value, axis, [(i, i ^ bit) for i in range(lax.axis_size(axis...  6.58 us
    all_to_all x1, starting transfers between devices, body(): lax.all_to_all(back.reshape(devs, 2, slice_rows, width), 'ctx', split_axi...  3.72 us
    ppermute x12, waiting for transfers between devices, swap_by_place(): return lax.ppermute(value, ('ctx', 'rep'), pairs)  3.66 us
  transfers between devices with their start and end apart: 23, of which 11 were waited for; matrix products, arithmetic and copies ran while one was open for 1% of the time, Pallas kernels for 4%

profile of v4, /device:TPU:0, one launch (start us, length us, event | category | flops | bytes accessed | tf_op | source)
XLA Modules:
  0.0 56.2 jit_solution(11993637564555371669)
XLA Ops:
  0.7 1.5 %pack.1 = (bf16[4,2,32,256]{3,2,1,0:T(8,128)(2,1)S(1)}, bf16[4,2,32,256]{3,2,1,0:T(8,128)(2,1)S(1)}) custom-call(s32[2]{0:T(128)S(1)} %pad_add_fusion.where_ref, bf16[256,256]{1,0:T(8,128)(2,1)} %bitcast.15, bf16[256,256]{1,0:T(8,128)(2,1)} %bitcast.16), custom_call_target="tpu_custom_call" | custom-call | bytes 524296 | tf_op jit(solution)/shard_map/pack/pallas_call | solution.py:283
  2.3 0.5 collective-permute-start
  2.8 1.0 %collective-permute-done.got_ref.refs_1_ = bf16[4,2,32,256]{3,2,1,0:T(8,128)(2,1)S(1)} collective-permute-done((bf16[4,2,32,256]{3,2,1,0:T(8,128)(2,1)S(1)}, bf16[4,2,32,256]{3,2,1,0:T(8,128)(2,1)S(1)}, u32[]{:S(2)}, u32[]{:S(2)}) %collective-permute-start) | collective-permute-done | bytes 131104 | tf_op jit(solution)/shard_map/ppermute | solution.py:309
  3.8 2.9 %collective-permute-start.1 = (bf16[2,2,32,256]{3,2,1,0:T(8,128)(2,1)S(1)}, bf16[2,2,32,256]{3,2,1,0:T(8,128)(2,1)S(1)}, u32[]{:S(2)}, u32[]{:S(2)}) collective-permute-start(bf16[2,2,32,256]{3,2,1,0:T(8,128)(2,1)S(1)} %get-tuple-element.53), channel_id=1, source_target_pairs={{0,8},{4,12},{8,0},{12,4},{16,24},{20,28},{24,16},{28,20},{1,9},{5... | collective-permute-start | bytes 196616 | tf_op jit(solution)/shard_map/ppermute | solution.py:309
  6.7 1.5 %collective-permute-start.2 = (bf16[2,2,32,256]{3,2,1,0:T(8,128)(2,1)S(1)}, bf16[2,2,32,256]{3,2,1,0:T(8,128)(2,1)S(1)}, u32[]{:S(2)}, u32[]{:S(2)}) collective-permute-start(bf16[2,2,32,256]{3,2,1,0:T(8,128)(2,1)S(1)} %get-tuple-element.54), channel_id=1, source_target_pairs={{0,16},{4,20},{8,24},{12,28},{16,0},{20,4},{24,8},{28,12},{1,17},{... | collective-permute-start | bytes 196616 | tf_op jit(solution)/shard_map/ppermute | solution.py:309
  8.3 0.7 %copy-done.1 = f32[512]{0:T(512)S(1)} copy-done((f32[512]{0:T(512)S(1)}, f32[512]{0:T(512)}, u32[]{:S(2)}) %copy-start.1) | copy-done | bytes 2072
  8.9 1.9 %prep.1 = (bf16[512,1024]{1,0:T(8,128)(2,1)S(1)}, bf16[1024,512]{1,0:T(8,128)(2,1)S(1)}, bf16[1024,512]{1,0:T(8,128)(2,1)S(1)}, bf16[512,1024]{1,0:T(8,128)(2,1)...) custom-call(bf16[512,1024]{1,0:T(8,128)(2,1)} %we_ref.1, f32[1,1024]{1,0:T(1,128)S(1)} %bitcast.12, ...), custom_call_target="tpu_custom_call" | custom-call | bytes 6307840 | tf_op jit(solution)/shard_map/prep/pallas_call | solution.py:283
  11.0 2.4 %collective-permute-done.3.refs_4_ = bf16[2,2,32,256]{3,2,1,0:T(8,128)(2,1)S(1)} collective-permute-done((bf16[2,2,32,256]{3,2,1,0:T(8,128)(2,1)S(1)}, bf16[2,2,32,256]{3,2,1,0:T(8,128)(2,1)S(1)}, u32[]{:S(2)}, u32[]{:S(2)}) %collective-permute-start.3) | collective-permute-done | bytes 65568 | tf_op jit(solution)/shard_map/ppermute | solution.py:309
  13.4 8.4 %sections.1 = (bf16[8,2,32,256]{3,2,1,0:T(8,128)(2,1)}, bf16[384,512]{1,0:T(8,128)(2,1)S(1)}, bf16[384,512]{1,0:T(8,128)(2,1)S(1)}, bf16[384,512]{1,0:T(8,128)(2...) custom-call(s32[2]{0:T(128)S(1)} %pad_add_fusion.where_ref, ...), custom_call_target="tpu_custom_call" | custom-call | flops 3221225472 | bytes 7053320 | tf_op jit(solution)/shard_map/sections/pallas_call | solution.py:283
  21.9 0.5 collective-permute-start.9
  22.4 1.1 %collective-permute-done.4.recv_ref = bf16[384,512]{1,0:T(8,128)(2,1)S(1)} collective-permute-done((bf16[384,512]{1,0:T(8,128)(2,1)S(1)}, bf16[384,512]{1,0:T(8,128)(2,1)S(1)}, u32[]{:S(2)}, u32[]{:S(2)}) %collective-permute-start.4) | collective-permute-done | bytes 393248 | tf_op jit(solution)/shard_map/ppermute | solution.py:320
  23.7 0.6 %collective-permute-start.5 = (bf16[192,512]{1,0:T(8,128)(2,1)S(1)}, bf16[192,512]{1,0:T(8,128)(2,1)S(1)}, u32[]{:S(2)}, u32[]{:S(2)}) collective-permute-start(bf16[192,512]{1,0:T(8,128)(2,1)S(1)} %get-tuple-element.67), channel_id=1, source_target_pairs={{0,8},{1,9},{2,10},{3,11},{4,12},{5,13},{6,14},{7,15},{8,0},{9,1},... | collective-permute-start | bytes 589832 | tf_op jit(solution)/shard_map/ppermute | solution.py:320
  24.3 0.5 collective-permute-start.10
  25.0 1.7 %collective-permute-start.15 = (bf16[144,512]{1,0:T(8,128)(2,1)S(1)}, bf16[144,512]{1,0:T(8,128)(2,1)S(1)}, u32[]{:S(2)}, u32[]{:S(2)}) collective-permute-start(bf16[144,512]{1,0:T(8,128)(2,1)S(1)} %get-tuple-element.83), channel_id=1, source_target_pairs={{0,1},{1,0},{2,3},{3,2},{4,5},{5,4},{6,7},{7,6},{8,9},{9,8},{10,11... | collective-permute-start | bytes 442376 | tf_op jit(solution)/shard_map/ppermute | solution.py:320
  26.6 3.7 %all-to-all-start = ((bf16[8,2,32,256]{3,2,1,0:T(8,128)(2,1)}), bf16[8,2,32,256]{3,2,1,0:T(8,128)(2,1)S(1)}, u32[]{:S(2)}, u32[]{:S(2)}) async-start(bf16[8,2,32,256]{3,2,1,0:T(8,128)(2,1)} %get-tuple-element.63), calls=%async_computation | async-start | bytes 524288 | tf_op jit(solution)/shard_map/all_to_all | solution.py:409
  30.7 1.6 %collective-permute-start.6 = (bf16[96,512]{1,0:T(8,128)(2,1)S(1)}, bf16[96,512]{1,0:T(8,128)(2,1)S(1)}, u32[]{:S(2)}, u32[]{:S(2)}) collective-permute-start(bf16[96,512]{1,0:T(8,128)(2,1)S(1)} %get-tuple-element.69.refs_0_), channel_id=1, source_target_pairs={{0,1},{1,0},{2,3},{3,2},{4,5},{5,4},{6,7},{7,6},{8,9},{9,8},{10,11... | collective-permute-start | bytes 294920 | tf_op jit(solution)/shard_map/ppermute | solution.py:320
  32.4 0.7 %collective-permute-start.11 = (bf16[96,512]{1,0:T(8,128)(2,1)S(1)}, bf16[96,512]{1,0:T(8,128)(2,1)S(1)}, u32[]{:S(2)}, u32[]{:S(2)}) collective-permute-start(bf16[96,512]{1,0:T(8,128)(2,1)S(1)} %get-tuple-element.77.refs_0_), channel_id=1, source_target_pairs={{0,8},{1,9},{2,10},{3,11},{4,12},{5,13},{6,14},{7,15},{8,0},{9,1},... | collective-permute-start | bytes 294920 | tf_op jit(solution)/shard_map/ppermute | solution.py:320
  33.1 1.5 %collective-permute-start.16 = (bf16[80,512]{1,0:T(8,128)(2,1)S(1)}, bf16[80,512]{1,0:T(8,128)(2,1)S(1)}, u32[]{:S(2)}, u32[]{:S(2)}) collective-permute-start(bf16[80,512]{1,0:T(8,128)(2,1)S(1)} %get-tuple-element.85), channel_id=1, source_target_pairs={{0,16},{1,17},{2,18},{3,19},{4,20},{5,21},{6,22},{7,23},{8,24},{9,... | collective-permute-start | bytes 245768 | tf_op jit(solution)/shard_map/ppermute | solution.py:320
  34.7 1.0 %collective-permute-done.6.recv_ref = bf16[96,512]{1,0:T(8,128)(2,1)S(1)} collective-permute-done((bf16[96,512]{1,0:T(8,128)(2,1)S(1)}, bf16[96,512]{1,0:T(8,128)(2,1)S(1)}, u32[]{:S(2)}, u32[]{:S(2)}) %collective-permute-start.6) | collective-permute-done | bytes 98336 | tf_op jit(solution)/shard_map/ppermute | solution.py:320
  35.7 1.7 %collective-permute-start.7 = (bf16[48,512]{1,0:T(8,128)(2,1)S(1)}, bf16[48,512]{1,0:T(8,128)(2,1)S(1)}, u32[]{:S(2)}, u32[]{:S(2)}) collective-permute-start(bf16[48,512]{1,0:T(8,128)(2,1)S(1)} %get-tuple-element.71.refs_0_), channel_id=1, source_target_pairs={{0,16},{1,17},{2,18},{3,19},{4,20},{5,21},{6,22},{7,23},{8,24},{9,... | collective-permute-start | bytes 147464 | tf_op jit(solution)/shard_map/ppermute | solution.py:320
  37.4 1.1 %collective-permute-done.11.recv_ref = bf16[96,512]{1,0:T(8,128)(2,1)S(1)} collective-permute-done((bf16[96,512]{1,0:T(8,128)(2,1)S(1)}, bf16[96,512]{1,0:T(8,128)(2,1)S(1)}, u32[]{:S(2)}, u32[]{:S(2)}) %collective-permute-start.11) | collective-permute-done | bytes 98336 | tf_op jit(solution)/shard_map/ppermute | solution.py:320
  38.7 1.3 %collective-permute-start.17 = (bf16[48,512]{1,0:T(8,128)(2,1)S(1)}, bf16[48,512]{1,0:T(8,128)(2,1)S(1)}, u32[]{:S(2)}, u32[]{:S(2)}) collective-permute-start(bf16[48,512]{1,0:T(8,128)(2,1)S(1)} %get-tuple-element.87), channel_id=1, source_target_pairs={{0,8},{1,9},{2,10},{3,11},{4,12},{5,13},{6,14},{7,15},{8,0},{9,1},... | collective-permute-start | bytes 147464 | tf_op jit(solution)/shard_map/ppermute | solution.py:320
  40.4 2.6 %collective-permute-start.8 = (bf16[48,512]{1,0:T(8,128)(2,1)S(1)}, bf16[48,512]{1,0:T(8,128)(2,1)S(1)}, u32[]{:S(2)}, u32[]{:S(2)}) collective-permute-start(bf16[48,512]{1,0:T(8,128)(2,1)S(1)} %add.8.refs_0_), channel_id=1, source_target_pairs={{0,2},{1,3},{2,0},{3,1},{4,6},{5,7},{6,4},{7,5},{8,10},{9,11},{10,... | collective-permute-start | bytes 147464 | tf_op jit(solution)/shard_map/ppermute | solution.py:309
  43.1 2.4 %collective-permute-start.18 = (bf16[48,512]{1,0:T(8,128)(2,1)S(1)}, bf16[48,512]{1,0:T(8,128)(2,1)S(1)}, u32[]{:S(2)}, u32[]{:S(2)}) collective-permute-start(bf16[48,512]{1,0:T(8,128)(2,1)S(1)} %add.12.refs_0_), channel_id=1, source_target_pairs={{0,2},{1,3},{2,0},{3,1},{4,6},{5,7},{6,4},{7,5},{8,10},{9,11},{10,... | collective-permute-start | bytes 147464 | tf_op jit(solution)/shard_map/ppermute | solution.py:309
  45.5 1.2 %collective-permute-start.13 = (bf16[48,512]{1,0:T(8,128)(2,1)S(1)}, bf16[48,512]{1,0:T(8,128)(2,1)S(1)}, u32[]{:S(2)}, u32[]{:S(2)}) collective-permute-start(bf16[48,512]{1,0:T(8,128)(2,1)S(1)} %add.10.refs_0_), channel_id=1, source_target_pairs={{0,2},{1,3},{2,0},{3,1},{4,6},{5,7},{6,4},{7,5},{8,10},{9,11},{10,... | collective-permute-start | bytes 147464 | tf_op jit(solution)/shard_map/ppermute | solution.py:309
  46.7 1.4 %collective-permute-start.19 = (bf16[48,512]{1,0:T(8,128)(2,1)S(1)}, bf16[48,512]{1,0:T(8,128)(2,1)S(1)}, u32[]{:S(2)}, u32[]{:S(2)}) collective-permute-start(bf16[48,512]{1,0:T(8,128)(2,1)S(1)} %add.9.refs_0_), channel_id=1, source_target_pairs={{0,1},{1,0},{2,3},{3,2},{4,5},{5,4},{6,7},{7,6},{8,9},{9,8},{10,11... | collective-permute-start | bytes 147464 | tf_op jit(solution)/shard_map/ppermute | solution.py:309
  48.1 0.6 %collective-permute-done.18.refs_1_ = bf16[48,512]{1,0:T(8,128)(2,1)S(1)} collective-permute-done((bf16[48,512]{1,0:T(8,128)(2,1)S(1)}, bf16[48,512]{1,0:T(8,128)(2,1)S(1)}, u32[]{:S(2)}, u32[]{:S(2)}) %collective-permute-start.18) | collective-permute-done | bytes 49184 | tf_op jit(solution)/shard_map/ppermute | solution.py:309
  48.8 1.4 %collective-permute-start.21 = (bf16[32,512]{1,0:T(8,128)(2,1)S(1)}, bf16[32,512]{1,0:T(8,128)(2,1)S(1)}, u32[]{:S(2)}, u32[]{:S(2)}) collective-permute-start(bf16[32,512]{1,0:T(8,128)(2,1)S(1)} %get-tuple-element.89), channel_id=1, source_target_pairs={{0,1},{1,0},{2,3},{3,2},{4,5},{5,4},{6,7},{7,6},{8,9},{9,8},{10,11... | collective-permute-start | bytes 98312 | tf_op jit(solution)/shard_map/ppermute | solution.py:309
  50.6 1.4 %collective-permute-start.20 = (bf16[48,512]{1,0:T(8,128)(2,1)S(1)}, bf16[48,512]{1,0:T(8,128)(2,1)S(1)}, u32[]{:S(2)}, u32[]{:S(2)}) collective-permute-start(bf16[48,512]{1,0:T(8,128)(2,1)S(1)} %add.11.refs_1_), channel_id=1, source_target_pairs={{0,1},{1,0},{2,3},{3,2},{4,5},{5,4},{6,7},{7,6},{8,9},{9,8},{10,11... | collective-permute-start | bytes 147464 | tf_op jit(solution)/shard_map/ppermute | solution.py:309
  52.0 0.7 %fusion = (bf16[8,1,32,256]{3,2,1,0:T(8,128)(2,1)}, bf16[8,1,32,256]{3,2,1,0:T(8,128)(2,1)}) fusion(bf16[8,2,32,256]{3,2,1,0:T(8,128)(2,1)S(1)} %all-to-all-done), kind=kLoop, calls=%fused_computation.1 | loop fusion | bytes 524288 | tf_op jit(solution)/shard_map/slice | solution.py:438
  52.8 2.0 %collective-permute-done.20.refs_4_ = bf16[48,512]{1,0:T(8,128)(2,1)S(1)} collective-permute-done((bf16[48,512]{1,0:T(8,128)(2,1)S(1)}, bf16[48,512]{1,0:T(8,128)(2,1)S(1)}, u32[]{:S(2)}, u32[]{:S(2)}) %collective-permute-start.20) | collective-permute-done | bytes 49184 | tf_op jit(solution)/shard_map/ppermute | solution.py:309
  54.8 1.4 %final.1 = (f32[64,1024]{1,0:T(8,128)}, f32[1,1024]{1,0:T(1,128)}, f32[128,512]{1,0:T(8,128)}, f32[1,512]{1,0:T(1,128)}, f32[1,512]{1,0:T(1,128)}) custom-call(s32[2]{0:T(128)S(1)} %pad_add_fusion.where_ref, bf16[48,512]{1,0:T(8,128)(2,1)S(1)} %add.9.refs_0_, bf16[48,512]{1,0:T(8,128)(2,1)S(1)} %add.11.refs_1_, ...), custom_call_target="tpu_custom_call" | custom-call | bytes 811016 | tf_op jit(solution)/shard_map/final/pallas_call | solution.py:283
  (42 shorter events, 2.3 us)
Async XLA Ops:
  2.3 1.5 %collective-permute-start = (bf16[4,2,32,256]{3,2,1,0:T(8,128)(2,1)S(1)}, bf16[4,2,32,256]{3,2,1,0:T(8,128)(2,1)S(1)}, u32[]{:S(2)}, u32[]{:S(2)}) collective-permute-start(bf16[4,2,32,256]{3,2,1,0:T(8,128)(2,1)S(1)} %get-tuple-element.52), channel_id=1, source_target_pairs={{0,4},{4,0},{8,12},{12,8},{16,20},{20,16},{24,28},{28,24},{1,5},{5... | collective-permute-start | bytes 393224 | tf_op jit(solution)/shard_map/ppermute | solution.py:309
  3.8 4.5 %copy-start.2 = (f32[512]{0:T(512)S(1)}, f32[512]{0:T(512)}, u32[]{:S(2)}) copy-start(f32[512]{0:T(512)} %param.12) | copy-start | bytes 6148
  3.8 7.1 %collective-permute-start.1 = (bf16[2,2,32,256]{3,2,1,0:T(8,128)(2,1)S(1)}, bf16[2,2,32,256]{3,2,1,0:T(8,128)(2,1)S(1)}, u32[]{:S(2)}, u32[]{:S(2)}) collective-permute-start(bf16[2,2,32,256]{3,2,1,0:T(8,128)(2,1)S(1)} %get-tuple-element.53), channel_id=1, source_target_pairs={{0,8},{4,12},{8,0},{12,4},{16,24},{20,28},{24,16},{28,20},{1,9},{5... | collective-permute-start | bytes 196616 | tf_op jit(solution)/shard_map/ppermute | solution.py:309
  6.7 1.6 %copy-start = (f32[1024]{0:T(1024)S(1)}, f32[1024]{0:T(1024)}, u32[]{:S(2)}) copy-start(f32[1024]{0:T(1024)} %param.9) | copy-start | bytes 12292
  6.7 4.3 %collective-permute-start.2 = (bf16[2,2,32,256]{3,2,1,0:T(8,128)(2,1)S(1)}, bf16[2,2,32,256]{3,2,1,0:T(8,128)(2,1)S(1)}, u32[]{:S(2)}, u32[]{:S(2)}) collective-permute-start(bf16[2,2,32,256]{3,2,1,0:T(8,128)(2,1)S(1)} %get-tuple-element.54), channel_id=1, source_target_pairs={{0,16},{4,20},{8,24},{12,28},{16,0},{20,4},{24,8},{28,12},{1,17},{... | collective-permute-start | bytes 196616 | tf_op jit(solution)/shard_map/ppermute | solution.py:309
  8.2 5.2 %collective-permute-start.3 = (bf16[2,2,32,256]{3,2,1,0:T(8,128)(2,1)S(1)}, bf16[2,2,32,256]{3,2,1,0:T(8,128)(2,1)S(1)}, u32[]{:S(2)}, u32[]{:S(2)}) collective-permute-start(bf16[2,2,32,256]{3,2,1,0:T(8,128)(2,1)S(1)} %get-tuple-element.55), channel_id=1, source_target_pairs={{0,24},{4,28},{8,16},{12,20},{16,8},{20,12},{24,0},{28,4},{1,25},{... | collective-permute-start | bytes 196616 | tf_op jit(solution)/shard_map/ppermute | solution.py:309
  8.3 0.7 %copy-start.1 = (f32[512]{0:T(512)S(1)}, f32[512]{0:T(512)}, u32[]{:S(2)}) copy-start(f32[512]{0:T(512)} %param.11) | copy-start | bytes 6148
  21.8 1.8 %collective-permute-start.4 = (bf16[384,512]{1,0:T(8,128)(2,1)S(1)}, bf16[384,512]{1,0:T(8,128)(2,1)S(1)}, u32[]{:S(2)}, u32[]{:S(2)}) collective-permute-start(bf16[384,512]{1,0:T(8,128)(2,1)S(1)} %get-tuple-element.65), channel_id=1, source_target_pairs={{0,4},{1,5},{2,6},{3,7},{4,0},{5,1},{6,2},{7,3},{8,12},{9,13},{10,... | collective-permute-start | bytes 1179656 | tf_op jit(solution)/shard_map/ppermute | solution.py:320
  21.9 2.4 %collective-permute-start.9 = (bf16[384,512]{1,0:T(8,128)(2,1)S(1)}, bf16[384,512]{1,0:T(8,128)(2,1)S(1)}, u32[]{:S(2)}, u32[]{:S(2)}) collective-permute-start(bf16[384,512]{1,0:T(8,128)(2,1)S(1)} %get-tuple-element.73), channel_id=1, source_target_pairs={{0,4},{1,5},{2,6},{3,7},{4,0},{5,1},{6,2},{7,3},{8,12},{9,13},{10,... | collective-permute-start | bytes 1179656 | tf_op jit(solution)/shard_map/ppermute | solution.py:320
  22.3 2.5 %collective-permute-start.14 = (bf16[272,512]{1,0:T(8,128)(2,1)S(1)}, bf16[272,512]{1,0:T(8,128)(2,1)S(1)}, u32[]{:S(2)}, u32[]{:S(2)}) collective-permute-start(bf16[272,512]{1,0:T(8,128)(2,1)S(1)} %get-tuple-element.81), channel_id=1, source_target_pairs={{0,4},{1,5},{2,6},{3,7},{4,0},{5,1},{6,2},{7,3},{8,12},{9,13},{10,... | collective-permute-start | bytes 835592 | tf_op jit(solution)/shard_map/ppermute | solution.py:320
  23.7 7.0 %collective-permute-start.5 = (bf16[192,512]{1,0:T(8,128)(2,1)S(1)}, bf16[192,512]{1,0:T(8,128)(2,1)S(1)}, u32[]{:S(2)}, u32[]{:S(2)}) collective-permute-start(bf16[192,512]{1,0:T(8,128)(2,1)S(1)} %get-tuple-element.67), channel_id=1, source_target_pairs={{0,8},{1,9},{2,10},{3,11},{4,12},{5,13},{6,14},{7,15},{8,0},{9,1},... | collective-permute-start | bytes 589832 | tf_op jit(solution)/shard_map/ppermute | solution.py:320
  24.3 8.0 %collective-permute-start.10 = (bf16[192,512]{1,0:T(8,128)(2,1)S(1)}, bf16[192,512]{1,0:T(8,128)(2,1)S(1)}, u32[]{:S(2)}, u32[]{:S(2)}) collective-permute-start(bf16[192,512]{1,0:T(8,128)(2,1)S(1)} %get-tuple-element.75), channel_id=1, source_target_pairs={{0,16},{1,17},{2,18},{3,19},{4,20},{5,21},{6,22},{7,23},{8,24},{9,... | collective-permute-start | bytes 589832 | tf_op jit(solution)/shard_map/ppermute | solution.py:320
  25.0 8.1 %collective-permute-start.15 = (bf16[144,512]{1,0:T(8,128)(2,1)S(1)}, bf16[144,512]{1,0:T(8,128)(2,1)S(1)}, u32[]{:S(2)}, u32[]{:S(2)}) collective-permute-start(bf16[144,512]{1,0:T(8,128)(2,1)S(1)} %get-tuple-element.83), channel_id=1, source_target_pairs={{0,1},{1,0},{2,3},{3,2},{4,5},{5,4},{6,7},{7,6},{8,9},{9,8},{10,11... | collective-permute-start | bytes 442376 | tf_op jit(solution)/shard_map/ppermute | solution.py:320
  26.6 25.4 %all-to-all-start = ((bf16[8,2,32,256]{3,2,1,0:T(8,128)(2,1)}), bf16[8,2,32,256]{3,2,1,0:T(8,128)(2,1)S(1)}, u32[]{:S(2)}, u32[]{:S(2)}) async-start(bf16[8,2,32,256]{3,2,1,0:T(8,128)(2,1)} %get-tuple-element.63), calls=%async_computation | async-start | bytes 524288 | tf_op jit(solution)/shard_map/all_to_all | solution.py:409
  30.7 5.0 %collective-permute-start.6 = (bf16[96,512]{1,0:T(8,128)(2,1)S(1)}, bf16[96,512]{1,0:T(8,128)(2,1)S(1)}, u32[]{:S(2)}, u32[]{:S(2)}) collective-permute-start(bf16[96,512]{1,0:T(8,128)(2,1)S(1)} %get-tuple-element.69.refs_0_), channel_id=1, source_target_pairs={{0,1},{1,0},{2,3},{3,2},{4,5},{5,4},{6,7},{7,6},{8,9},{9,8},{10,11... | collective-permute-start | bytes 294920 | tf_op jit(solution)/shard_map/ppermute | solution.py:320
  32.4 6.1 %collective-permute-start.11 = (bf16[96,512]{1,0:T(8,128)(2,1)S(1)}, bf16[96,512]{1,0:T(8,128)(2,1)S(1)}, u32[]{:S(2)}, u32[]{:S(2)}) collective-permute-start(bf16[96,512]{1,0:T(8,128)(2,1)S(1)} %get-tuple-element.77.refs_0_), channel_id=1, source_target_pairs={{0,8},{1,9},{2,10},{3,11},{4,12},{5,13},{6,14},{7,15},{8,0},{9,1},... | collective-permute-start | bytes 294920 | tf_op jit(solution)/shard_map/ppermute | solution.py:320
  33.1 5.5 %collective-permute-start.16 = (bf16[80,512]{1,0:T(8,128)(2,1)S(1)}, bf16[80,512]{1,0:T(8,128)(2,1)S(1)}, u32[]{:S(2)}, u32[]{:S(2)}) collective-permute-start(bf16[80,512]{1,0:T(8,128)(2,1)S(1)} %get-tuple-element.85), channel_id=1, source_target_pairs={{0,16},{1,17},{2,18},{3,19},{4,20},{5,21},{6,22},{7,23},{8,24},{9,... | collective-permute-start | bytes 245768 | tf_op jit(solution)/shard_map/ppermute | solution.py:320
  35.7 4.7 %collective-permute-start.7 = (bf16[48,512]{1,0:T(8,128)(2,1)S(1)}, bf16[48,512]{1,0:T(8,128)(2,1)S(1)}, u32[]{:S(2)}, u32[]{:S(2)}) collective-permute-start(bf16[48,512]{1,0:T(8,128)(2,1)S(1)} %get-tuple-element.71.refs_0_), channel_id=1, source_target_pairs={{0,16},{1,17},{2,18},{3,19},{4,20},{5,21},{6,22},{7,23},{8,24},{9,... | collective-permute-start | bytes 147464 | tf_op jit(solution)/shard_map/ppermute | solution.py:320
  38.7 4.4 %collective-permute-start.17 = (bf16[48,512]{1,0:T(8,128)(2,1)S(1)}, bf16[48,512]{1,0:T(8,128)(2,1)S(1)}, u32[]{:S(2)}, u32[]{:S(2)}) collective-permute-start(bf16[48,512]{1,0:T(8,128)(2,1)S(1)} %get-tuple-element.87), channel_id=1, source_target_pairs={{0,8},{1,9},{2,10},{3,11},{4,12},{5,13},{6,14},{7,15},{8,0},{9,1},... | collective-permute-start | bytes 147464 | tf_op jit(solution)/shard_map/ppermute | solution.py:320
  39.9 5.6 %collective-permute-start.12 = (bf16[48,512]{1,0:T(8,128)(2,1)S(1)}, bf16[48,512]{1,0:T(8,128)(2,1)S(1)}, u32[]{:S(2)}, u32[]{:S(2)}) collective-permute-start(bf16[48,512]{1,0:T(8,128)(2,1)S(1)} %get-tuple-element.79.refs_0_), channel_id=1, source_target_pairs={{0,1},{1,0},{2,3},{3,2},{4,5},{5,4},{6,7},{7,6},{8,9},{9,8},{10,11... | collective-permute-start | bytes 147464 | tf_op jit(solution)/shard_map/ppermute | solution.py:320
  40.4 6.3 %collective-permute-start.8 = (bf16[48,512]{1,0:T(8,128)(2,1)S(1)}, bf16[48,512]{1,0:T(8,128)(2,1)S(1)}, u32[]{:S(2)}, u32[]{:S(2)}) collective-permute-start(bf16[48,512]{1,0:T(8,128)(2,1)S(1)} %add.8.refs_0_), channel_id=1, source_target_pairs={{0,2},{1,3},{2,0},{3,1},{4,6},{5,7},{6,4},{7,5},{8,10},{9,11},{10,... | collective-permute-start | bytes 147464 | tf_op jit(solution)/shard_map/ppermute | solution.py:309
  43.1 5.7 %collective-permute-start.18 = (bf16[48,512]{1,0:T(8,128)(2,1)S(1)}, bf16[48,512]{1,0:T(8,128)(2,1)S(1)}, u32[]{:S(2)}, u32[]{:S(2)}) collective-permute-start(bf16[48,512]{1,0:T(8,128)(2,1)S(1)} %add.12.refs_0_), channel_id=1, source_target_pairs={{0,2},{1,3},{2,0},{3,1},{4,6},{5,7},{6,4},{7,5},{8,10},{9,11},{10,... | collective-permute-start | bytes 147464 | tf_op jit(solution)/shard_map/ppermute | solution.py:309
  45.5 5.1 %collective-permute-start.13 = (bf16[48,512]{1,0:T(8,128)(2,1)S(1)}, bf16[48,512]{1,0:T(8,128)(2,1)S(1)}, u32[]{:S(2)}, u32[]{:S(2)}) collective-permute-start(bf16[48,512]{1,0:T(8,128)(2,1)S(1)} %add.10.refs_0_), channel_id=1, source_target_pairs={{0,2},{1,3},{2,0},{3,1},{4,6},{5,7},{6,4},{7,5},{8,10},{9,11},{10,... | collective-permute-start | bytes 147464 | tf_op jit(solution)/shard_map/ppermute | solution.py:309
  46.7 6.1 %collective-permute-start.19 = (bf16[48,512]{1,0:T(8,128)(2,1)S(1)}, bf16[48,512]{1,0:T(8,128)(2,1)S(1)}, u32[]{:S(2)}, u32[]{:S(2)}) collective-permute-start(bf16[48,512]{1,0:T(8,128)(2,1)S(1)} %add.9.refs_0_), channel_id=1, source_target_pairs={{0,1},{1,0},{2,3},{3,2},{4,5},{5,4},{6,7},{7,6},{8,9},{9,8},{10,11... | collective-permute-start | bytes 147464 | tf_op jit(solution)/shard_map/ppermute | solution.py:309
  48.8 4.0 %collective-permute-start.21 = (bf16[32,512]{1,0:T(8,128)(2,1)S(1)}, bf16[32,512]{1,0:T(8,128)(2,1)S(1)}, u32[]{:S(2)}, u32[]{:S(2)}) collective-permute-start(bf16[32,512]{1,0:T(8,128)(2,1)S(1)} %get-tuple-element.89), channel_id=1, source_target_pairs={{0,1},{1,0},{2,3},{3,2},{4,5},{5,4},{6,7},{7,6},{8,9},{9,8},{10,11... | collective-permute-start | bytes 98312 | tf_op jit(solution)/shard_map/ppermute | solution.py:309
  50.6 4.2 %collective-permute-start.20 = (bf16[48,512]{1,0:T(8,128)(2,1)S(1)}, bf16[48,512]{1,0:T(8,128)(2,1)S(1)}, u32[]{:S(2)}, u32[]{:S(2)}) collective-permute-start(bf16[48,512]{1,0:T(8,128)(2,1)S(1)} %add.11.refs_1_), channel_id=1, source_target_pairs={{0,1},{1,0},{2,3},{3,2},{4,5},{5,4},{6,7},{7,6},{8,9},{9,8},{10,11... | collective-permute-start | bytes 147464 | tf_op jit(solution)/shard_map/ppermute | solution.py:309
